TPU v7x, 256 devices: a whole 4x4x8 slice. The times are simulated.
256 devices in a mesh: gx: 16 (over x_hi, y, core), gz: 16 (over z, x_lo).
Axes of the slice: x: 4 (x_hi: 2, x_lo: 2; x = x_hi * 2 + x_lo), y: 4, z: 8, core: 2. Of those that a mesh axis runs over, the one named last changes fastest.
Arguments:
- vertical_now: float32 [640, 16, 2048], P('gz', None, 'gx'), may hold values from -6 to 6
- vertical_section: float32 [640, 16, 2048], P('gz', None, 'gx'), may hold values from -6 to 6
- theta_now: float32 [640, 16, 2048], P('gz', None, 'gx'), may hold values from -6 to 6
- theta_section: float32 [640, 16, 2048], P('gz', None, 'gx'), may hold values from -6 to 6
- east_wind: bfloat16 [640, 16, 2048], P('gz', None, 'gx'), may hold values from -5 to 5
- north_wind: bfloat16 [640, 16, 2048], P('gz', None, 'gx'), may hold values from -5 to 5
- eddy_viscosity: bfloat16 [640, 16, 2048], P('gz', None, 'gx'), may hold values from 0.019897461 to 0.19921875
- density: float32 [640], P('gz'), may hold values from 0.7 to 1.4
- coupling: float32 [640], P('gz'), may hold values from 10 to 200
- cloud_top: int32 [16, 16], P(None, 'gx'), may hold values from 160 to 479
Outputs:
- vertical_next: float32 [640, 16, 2048], P('gz', None, 'gx')
- theta_next: float32 [640, 16, 2048], P('gz', None, 'gx')
All inputs are finite; a program needn't handle non-finite values.
Results may differ from a plain program's by a relative error of at most 0.0003.
Values may be sent and summed in bfloat16 or wider, within the bound.
No kernel may reach another device: no remote copies, remote signals or barrier semaphores. Data moves between devices by JAX's collectives and lax.ppermute only.
A program may use at most 64 MiB of HBM per device.

v0:
```python
import jax
import jax.numpy as jnp
from jax import lax
from jax.sharding import PartitionSpec as P

COURANT = 0.25
MIXED_BOOST = 4.0
HEAT_RATIO = 3.0


def with_halo(cells, sides, width):
    for axis, dim in sides:
        count = lax.axis_size(axis)
        head = lax.slice_in_dim(cells, 0, width, axis=dim)
        tail = lax.slice_in_dim(cells, cells.shape[dim] - width, cells.shape[dim], axis=dim)
        cells = jnp.concatenate(
            [
                lax.ppermute(tail, axis, [(i, (i + 1) % count) for i in range(count)]),
                cells,
                lax.ppermute(head, axis, [((i + 1) % count, i) for i in range(count)]),
            ],
            axis=dim,
        )
    return cells


def face_flux(shifted, face_speed, mixing):
    ahead_face = (
        2.0 * shifted(-2)
        - 13.0 * shifted(-1)
        + 47.0 * shifted(0)
        + 27.0 * shifted(1)
        - 3.0 * shifted(2)
    ) / 60.0
    behind = (
        2.0 * shifted(3)
        - 13.0 * shifted(2)
        + 47.0 * shifted(1)
        + 27.0 * shifted(0)
        - 3.0 * shifted(-1)
    ) / 60.0
    upwind = jnp.where(face_speed >= 0.0, ahead_face, behind)
    return COURANT * face_speed * upwind - mixing * (shifted(1) - shifted(0))


def periodic_change(values, velocity, viscous, axis_pos):

    def shifted(offset):
        return jnp.roll(values, -offset, axis=axis_pos)

    face_speed = 0.5 * (velocity + jnp.roll(velocity, -1, axis=axis_pos))
    mixing = 0.5 * (viscous + jnp.roll(viscous, -1, axis=axis_pos))
    face_fluxes = face_flux(shifted, face_speed, mixing)
    return face_fluxes - jnp.roll(face_fluxes, 1, axis=axis_pos)


def face_coef(height, coupled, ceiling, factor):
    return factor * coupled * jnp.where(height <= ceiling, MIXED_BOOST + 1.0, 1.0)


def block_inverse(weight, low_coef, high_coef):
    diagonal = jnp.moveaxis(weight[..., None] + low_coef + high_coef, 1, 0)
    lowers = jnp.moveaxis(low_coef, 1, 0)
    highers = jnp.moveaxis(high_coef, 1, 0)
    block_size = diagonal.shape[0]
    identity = jnp.eye(block_size, dtype=jnp.float32)

    def block_forward(state_pair, member):
        ratio_prev, solved_prev = state_pair
        diag_here, low_here, high_here, unit_row = member
        pivot_value = diag_here - low_here * ratio_prev
        ratio_next = high_here / pivot_value
        solved = (unit_row + low_here[..., None] * solved_prev) / pivot_value[..., None]
        return ((ratio_next, solved), (ratio_next, solved))

    start_state = (
        jnp.zeros(diagonal.shape[1:], jnp.float32),
        jnp.zeros(diagonal.shape[1:] + (block_size,), jnp.float32),
    )
    final_state, (ratios, eliminated) = lax.scan(
        block_forward, start_state, (diagonal, lowers, highers, identity)
    )

    def block_backward(following, member):
        ratio_here, solved = member
        current = solved + ratio_here[..., None] * following
        return (current, current)

    final_top, inverse = lax.scan(
        block_backward,
        jnp.zeros(eliminated.shape[1:], jnp.float32),
        (ratios, eliminated),
        reverse=True,
    )
    return inverse


def block_factors(weight, lower_faces, upper_faces, heights, ceiling, factor):
    low_coef = face_coef(heights[..., None], lower_faces[..., None], ceiling, factor)
    high_coef = face_coef(heights[..., None] + 1, upper_faces[..., None], ceiling, factor)
    inverse = block_inverse(weight, low_coef, high_coef)
    left_spike = -inverse[..., 0] * low_coef[:, 0][None]
    right_spike = -inverse[..., -1] * high_coef[:, -1][None]
    return (inverse, left_spike, right_spike)


def apply_inverse(inverse, blocks):
    return jnp.einsum("knjm,nmjc->nkjc", inverse, blocks, precision=lax.Precision.HIGHEST)


def edge_rows(solved, left_spike, right_spike):
    width = solved.shape[-1]

    def spread(values):
        return jnp.broadcast_to(values[..., None], values.shape + (width,))

    return jnp.stack(
        [
            solved[:, 0],
            solved[:, -1],
            spread(left_spike[0]),
            spread(left_spike[-1]),
            spread(right_spike[0]),
            spread(right_spike[-1]),
        ],
        axis=1,
    )


def interface_all(edges):
    zeros = jnp.zeros(edges.shape[2:], jnp.float32)

    def interface_forward(state_pair, pieces):
        tail_value, tail_slope = state_pair
        rhs_top = pieces[0]
        rhs_bottom = pieces[1]
        left_top = pieces[2]
        left_bottom = pieces[3]
        right_top = pieces[4]
        right_bottom = pieces[5]
        divisor = 1.0 - left_top * tail_slope
        lead_value = (rhs_top - left_top * tail_value) / divisor
        lead_slope = right_top / divisor
        value_next = rhs_bottom - left_bottom * tail_value + left_bottom * tail_slope * lead_value
        slope_next = right_bottom + left_bottom * tail_slope * lead_slope
        return ((value_next, slope_next), (lead_value, lead_slope, value_next, slope_next))

    final_state, terms = lax.scan(interface_forward, (zeros, zeros), edges)

    def interface_backward(following, member_terms):
        lead_value, lead_slope, tail_value, tail_slope = member_terms
        return (
            lead_value - lead_slope * following,
            (following, tail_value - tail_slope * following),
        )

    final_top, (after_tops, bottoms) = lax.scan(interface_backward, zeros, terms, reverse=True)
    lower_all = jnp.concatenate([zeros[None], bottoms[:-1]], axis=0)
    return (after_tops, lower_all)


def combine_blocks(solved, left_spike, right_spike, upper_all, lower_all):
    left_levels = jnp.moveaxis(left_spike, 0, 1)[..., None]
    right_levels = jnp.moveaxis(right_spike, 0, 1)[..., None]
    return solved - right_levels * upper_all[:, None] - left_levels * lower_all[:, None]


def shards(
    vertical_now,
    vertical_section,
    theta_now,
    theta_section,
    east_wind,
    north_wind,
    eddy_viscosity,
    density,
    coupling,
    cloud_top,
):
    layers_here = vertical_section.shape[0]
    slab_width = vertical_section.shape[2]
    section_pair = jnp.stack([vertical_section, theta_section])
    former = jnp.stack([vertical_now, theta_now])
    padded = with_halo(section_pair, (("gx", 3),), 3)
    wind_rims = with_halo(jnp.stack([east_wind, eddy_viscosity]), (("gx", 3),), 1).astype(
        jnp.float32
    )

    def shifted(offset):
        return padded[..., 2 + offset : 3 + offset + slab_width]

    face_speed = 0.5 * (wind_rims[0, ..., : slab_width + 1] + wind_rims[0, ..., 1:])
    mixing = 0.5 * (wind_rims[1, ..., : slab_width + 1] + wind_rims[1, ..., 1:])
    face_fluxes = face_flux(shifted, face_speed, mixing)
    along_x = face_fluxes[..., 1:] - face_fluxes[..., :slab_width]
    viscous = eddy_viscosity.astype(jnp.float32)
    along_y = periodic_change(section_pair, north_wind.astype(jnp.float32), viscous, -2)
    change = -(along_x + along_y)
    explicit = former / 3.0 + 2.0 * (section_pair + change) / 3.0
    group_size = lax.axis_size("gz")
    member = lax.axis_index("gz")
    top_rows = cloud_top[:, 0]
    row_count = top_rows.shape[0] // group_size
    ceiling = lax.dynamic_slice_in_dim(top_rows, member * row_count, row_count)
    dens_all, coup_all = (
        lax.all_gather(density, "gz", axis=0, tiled=True),
        lax.all_gather(coupling, "gz", axis=0, tiled=True),
    )
    total_levels = layers_here * group_size
    heights = jnp.arange(total_levels, dtype=jnp.int32)
    lower_faces = jnp.where(heights >= 1, coup_all, 0.0)
    upper_faces = jnp.concatenate([coup_all[1:], jnp.zeros((1,), jnp.float32)])
    block_shape = (group_size, layers_here)
    factors = [
        block_factors(
            dens_all.reshape(block_shape),
            lower_faces.reshape(block_shape),
            upper_faces.reshape(block_shape),
            heights.reshape(block_shape),
            ceiling,
            factor,
        )
        for factor in (1.0, HEAT_RATIO)
    ]
    column_pair = (
        lax.all_to_all(explicit[0], "gz", split_axis=1, concat_axis=0, tiled=True),
        lax.all_to_all(explicit[1], "gz", split_axis=1, concat_axis=0, tiled=True),
    )
    finished = []
    for (inverse, left_spike, right_spike), column in zip(factors, column_pair):
        width = column.shape[-1]
        blocks = (dens_all[:, None, None] * column).reshape(
            group_size, layers_here, row_count, width
        )
        solved = apply_inverse(inverse, blocks)
        upper_all, lower_all = interface_all(edge_rows(solved, left_spike, right_spike))
        done = combine_blocks(solved, left_spike, right_spike, upper_all, lower_all)
        finished.append(done.reshape(total_levels, row_count, width))
    vertical_next = lax.all_to_all(finished[0], "gz", split_axis=0, concat_axis=1, tiled=True)
    theta_next = lax.all_to_all(finished[1], "gz", split_axis=0, concat_axis=1, tiled=True)
    return (vertical_next, theta_next)


def solution(mesh):
    return jax.shard_map(
        shards,
        mesh=mesh,
        in_specs=(
            P("gz", None, "gx"),
            P("gz", None, "gx"),
            P("gz", None, "gx"),
            P("gz", None, "gx"),
            P("gz", None, "gx"),
            P("gz", None, "gx"),
            P("gz", None, "gx"),
            P("gz"),
            P("gz"),
            P(None, "gx"),
        ),
        out_specs=(P("gz", None, "gx"), P("gz", None, "gx")),
        check_vma=False,
    )
```

profile of v0, /device:TPU:2, one launch (start us, length us, event | category | flops | bytes accessed | tf_op | source)
XLA Modules:
  0.0 184.3 jit_solution(15111820159471291503)
XLA Ops:
  0.7 1.6 fusion.89
  2.3 1.0 copy.181
  3.2 0.9 copy.182
  4.2 5.4 %collective-permute-start.3 = (f32[2,40,16,3]{1,2,3,0:T(8,128)}, f32[2,40,16,3]{1,2,3,0:T(8,128)}, u32[]{:S(2)}, u32[]{:S(2)}) collective-permute-start(f32[2,40,16,3]{1,2,3,0:T(8,128)} %copy.182), channel_id=1, source_target_pairs={{16,0},{32,16},{48,32},{64,48},{80,64},{96,80},{112,96},{128,112},... | collective-permute-start | bytes 46088 | tf_op jit(solution)/shard_map/ppermute | solution.py:20
  9.5 1.0 slice_maximum_fusion
  10.5 5.4 %collective-permute-start.1 = (bf16[2,40,16,1]{3,2,1,0:T(8,128)(2,1)}, bf16[2,40,16,1]{3,2,1,0:T(8,128)(2,1)}, u32[]{:S(2)}, u32[]{:S(2)}) collective-permute-start(bf16[2,40,16,1]{3,2,1,0:T(8,128)(2,1)} %get-tuple-element.1325), channel_id=1, source_target_pairs={{16,0},{32,16},{48,32},{64,48},{80,64},{96,80},{112,96},{128,112},... | collective-permute-start | bytes 7688 | tf_op jit(solution)/shard_map/ppermute | solution.py:20
  15.9 1.1 fusion.93
  17.0 0.7 fusion.127
  17.7 0.9 fusion.91
  18.6 0.7 fusion.128
  19.4 0.7 fusion.123
  20.4 0.3 copy-done.25
  20.7 0.6 dynamic-slice.1
  22.0 0.2 dynamic-update-slice
  22.2 0.2 dynamic-update-slice.1
  22.5 35.0 %all-reduce.4 = (f32[640]{0:T(1024)S(1)}, f32[640]{0:T(1024)S(1)}) all-reduce(f32[640]{0:T(1024)S(1)} %dynamic-update-slice.1, f32[640]{0:T(1024)S(1)} %dynamic-update-slice), channel_id=1, replica_groups=mesh['gx'=16,'gz'=16] {'gz'}, use_global_device_ids=true, to_apply=%add.3 | all-reduce | flops 1280 | bytes 10240
  57.6 0.8 copy.147
  58.4 0.7 copy.148
  59.2 0.8 copy.159
  60.3 0.7 constant_dynamic-slice_fusion.32
  61.0 0.7 add_bitcast_fusion
  61.8 0.7 slice_reduce_fusion.4
  62.7 7.3 %while.152 = (s32[]{:T(128)}, f32[16,1]{0,1:T(1,128)S(1)}, f32[16,1,40]{2,1,0:T(1,128)S(1)}, f32[40,16,1]{1,2,0:T(1,128)S(1)}, f32[40,16,1,40]{3,1,2,0:T(8,128)S...) while((s32[]{:T(128)}, f32[16,1]{0,1:T(1,128)S(1)}, ...), condition=%wide.region_9.10_spmd.clone, body=%wide.region_8.9_spmd.clone.sunk | while | flops 2627 | bytes 26340 | solution.py:80
  70.0 6.4 %while.153 = (s32[]{:T(128)}, f32[16,1,40]{2,1,0:T(1,128)S(1)}, f32[40,16,1,40]{3,1,2,0:T(8,128)S(1)}, f32[40,16,1,40]{3,1,2,0:T(8,128)S(1)}, f32[40,16,1]{1,2,0...) while((s32[]{:T(128)}, f32[16,1,40]{2,1,0:T(1,128)S(1)}, f32[40,16,1,40]{3,1,2,0:T(8,128)S(1)}, ...), condition=%wide.region_11.12_spmd.clone, body=%wide.region_10.11_spmd.clone.sunk | while | flops 1924 | bytes 29495 | solution.py:89
  76.4 0.9 copy.175
  77.7 7.3 %while.148 = (s32[]{:T(128)}, f32[16,1]{0,1:T(1,128)S(1)}, f32[16,1,40]{2,1,0:T(1,128)S(1)}, f32[40,16,1]{1,2,0:T(1,128)S(1)}, f32[40,16,1,40]{3,1,2,0:T(8,128)S...) while((s32[]{:T(128)}, f32[16,1]{0,1:T(1,128)S(1)}, ...), condition=%wide.region_1.2_spmd.clone, body=%wide.region_0.1_spmd.clone.sunk | while | flops 2627 | bytes 26340 | solution.py:80
  85.0 6.4 %while.149 = (s32[]{:T(128)}, f32[16,1,40]{2,1,0:T(1,128)S(1)}, f32[40,16,1,40]{3,1,2,0:T(8,128)S(1)}, f32[40,16,1,40]{3,1,2,0:T(8,128)S(1)}, f32[40,16,1]{1,2,0...) while((s32[]{:T(128)}, f32[16,1,40]{2,1,0:T(1,128)S(1)}, f32[40,16,1,40]{3,1,2,0:T(8,128)S(1)}, ...), condition=%wide.region_3.4_spmd.clone, body=%wide.region_2.3_spmd.clone.sunk | while | flops 1924 | bytes 29495 | solution.py:89
  91.5 1.1 pad_maximum_fusion
  92.7 0.6 copy-done.21
  93.3 0.8 fusion.134
  94.2 0.9 copy-done.5
  95.3 0.8 copy-done.9
  96.2 1.6 fusion.109
  98.0 0.9 slice.365
  98.9 1.4 maximum_convert_fusion
  100.3 0.4 multiply_bitcast_fusion
  100.7 0.2 fusion.115
  101.0 1.2 copy.138
  102.2 1.2 copy.146
  103.6 1.9 %copy.141 = f32[2,40,16,3]{3,1,2,0:T(8,128)} copy(f32[2,40,16,3]{1,2,3,0:T(8,128)} %collective-permute-done.2) | data formatting | bytes 30720 | tf_op jit(solution)/shard_map/ppermute | solution.py:18
  105.5 1.9 %copy.145 = f32[2,40,16,3]{3,1,2,0:T(8,128)} copy(f32[2,40,16,3]{1,2,3,0:T(8,128)} %collective-permute-done.3) | data formatting | bytes 30720 | tf_op jit(solution)/shard_map/ppermute | solution.py:20
  107.5 4.5 %fusion.80 = f32[2,40,16,129]{3,1,2,0:T(8,128)S(1)} fusion(f32[2,40,16,3]{3,1,2,0:T(8,128)} %copy.141, f32[2,40,16,128]{3,1,2,0:T(8,128)S(1)} %get-tuple-element.1305, f32[2,40,16,3]{3,1,2,0:T(8,128)} %copy.145, f32[40,16,129]{2,0,1:T(8,128)} %copy.146, f32[40,16,129]{2,0,1:T(8,128)} %copy.138, pred[40,16,129]{2,0,1:T(8,128)(4,1)S(1)} %copy.139), kind=kLoop, calls=%fused_computation.177 | loop fusion | flops 5118720 | bytes 2089600 | tf_op jit(solution)/shard_map/sub | solution.py:43
  112.0 0.7 fusion.99
  112.6 0.9 slice_bitcast_fusion
  113.5 6.9 %all-to-all-start.2 = ((f32[40,16,128]{2,0,1:T(8,128)}), f32[40,16,128]{2,0,1:T(8,128)S(1)}, u32[]{:S(2)}, u32[]{:S(2)}) async-start(f32[40,16,128]{2,0,1:T(8,128)} %get-tuple-element.1302), calls=%async_computation.2 | async-start | bytes 655360 | tf_op jit(solution)/shard_map/all_to_all | solution.py:227
  120.8 0.2 copy.167
  121.0 0.2 slice_reduce_fusion.10
  121.6 11.1 %all-to-all-done.2 = f32[40,16,128]{2,0,1:T(8,128)S(1)} async-done(((f32[40,16,128]{2,0,1:T(8,128)}), f32[40,16,128]{2,0,1:T(8,128)S(1)}, u32[]{:S(2)}, u32[]{:S(2)}) %all-to-all-start.2) | async-done | bytes 327712 | tf_op jit(solution)/shard_map/all_to_all | solution.py:227
  132.8 5.0 %all-to-all-start = ((f32[40,16,128]{2,0,1:T(8,128)}), f32[40,16,128]{2,0,1:T(8,128)S(1)}, u32[]{:S(2)}, u32[]{:S(2)}) async-start(f32[40,16,128]{2,0,1:T(8,128)} %get-tuple-element.1303), calls=%async_computation | async-start | bytes 655360 | tf_op jit(solution)/shard_map/all_to_all | solution.py:226
  137.8 0.8 convolution_bitcast_fusion
  139.1 0.8 while.154
  140.0 0.9 while.155
  141.0 1.0 multiply_subtract_fusion.2
  142.0 8.3 %all-to-all-done = f32[40,16,128]{2,0,1:T(8,128)S(1)} async-done(((f32[40,16,128]{2,0,1:T(8,128)}), f32[40,16,128]{2,0,1:T(8,128)S(1)}, u32[]{:S(2)}, u32[]{:S(2)}) %all-to-all-start) | async-done | bytes 327712 | tf_op jit(solution)/shard_map/all_to_all | solution.py:226
  150.3 5.2 %all-to-all-start.3 = ((f32[640,1,128]{2,1,0:T(1,128)}), f32[640,1,128]{2,1,0:T(1,128)S(1)}, u32[]{:S(2)}, u32[]{:S(2)}) async-start(f32[640,1,128]{2,1,0:T(1,128)} %bitcast.55), calls=%async_computation.3 | async-start | bytes 655360 | tf_op jit(solution)/shard_map/all_to_all | solution.py:240
  155.4 0.8 convolution_bitcast_fusion.1
  156.7 0.8 while.150
  157.6 0.9 while.151
  158.6 1.0 multiply_subtract_fusion.3
  159.6 9.6 %all-to-all-done.3 = f32[640,1,128]{2,1,0:T(1,128)S(1)} async-done(((f32[640,1,128]{2,1,0:T(1,128)}), f32[640,1,128]{2,1,0:T(1,128)S(1)}, u32[]{:S(2)}, u32[]{:S(2)}) %all-to-all-start.3) | async-done | bytes 327712 | tf_op jit(solution)/shard_map/all_to_all | solution.py:240
  169.1 4.0 %all-to-all-start.1 = ((f32[640,1,128]{2,1,0:T(1,128)}), f32[640,1,128]{2,1,0:T(1,128)S(1)}, u32[]{:S(2)}, u32[]{:S(2)}) async-start(f32[640,1,128]{2,1,0:T(1,128)} %bitcast.31), calls=%async_computation.1 | async-start | bytes 655360 | tf_op jit(solution)/shard_map/all_to_all | solution.py:239
  173.1 0.8 copy.180
  173.9 9.7 %all-to-all-done.1 = f32[640,1,128]{2,1,0:T(1,128)S(1)} async-done(((f32[640,1,128]{2,1,0:T(1,128)}), f32[640,1,128]{2,1,0:T(1,128)S(1)}, u32[]{:S(2)}, u32[]{:S(2)}) %all-to-all-start.1) | async-done | bytes 327712 | tf_op jit(solution)/shard_map/all_to_all | solution.py:239
  183.6 0.8 copy.179
  (872 shorter events, 27.3 us)
Async XLA Ops:
  0.6 59.7 %copy-start = (s32[16,1]{0,1:T(1,128)S(1)}, s32[16,1]{0,1:T(1,128)}, u32[]{:S(2)}) copy-start(s32[16,1]{0,1:T(1,128)} %param.35) | copy-start | bytes 196
  0.6 8.9 %copy-start.3 = (bf16[40,16,128]{2,1,0:T(8,128)(2,1)S(1)}, bf16[40,16,128]{2,1,0:T(8,128)(2,1)}, u32[]{:S(2)}) copy-start(bf16[40,16,128]{2,1,0:T(8,128)(2,1)} %param.32) | copy-start | bytes 491524
  0.7 8.9 %copy-start.11 = (bf16[40,16,128]{2,1,0:T(8,128)(2,1)S(1)}, bf16[40,16,128]{2,1,0:T(8,128)(2,1)}, u32[]{:S(2)}) copy-start(bf16[40,16,128]{2,1,0:T(8,128)(2,1)} %param.30) | copy-start | bytes 491524
  2.2 13.6 %copy-start.1 = (f32[40,16,128]{2,1,0:T(8,128)S(1)}, f32[40,16,128]{2,1,0:T(8,128)}, u32[]{:S(2)}) copy-start(f32[40,16,128]{2,1,0:T(8,128)} %param.27) | copy-start | bytes 983044
  2.2 13.6 %copy-start.2 = (f32[40,16,128]{2,1,0:T(8,128)S(1)}, f32[40,16,128]{2,1,0:T(8,128)}, u32[]{:S(2)}) copy-start(f32[40,16,128]{2,1,0:T(8,128)} %param.29) | copy-start | bytes 983044
  3.2 100.3 %collective-permute-start.2 = (f32[2,40,16,3]{1,2,3,0:T(8,128)}, f32[2,40,16,3]{1,2,3,0:T(8,128)}, u32[]{:S(2)}, u32[]{:S(2)}) collective-permute-start(f32[2,40,16,3]{1,2,3,0:T(8,128)} %copy.181), channel_id=1, source_target_pairs={{0,16},{16,32},{32,48},{48,64},{64,80},{80,96},{96,112},{112,128},... | collective-permute-start | bytes 46088 | tf_op jit(solution)/shard_map/ppermute | solution.py:18
  4.2 101.3 %collective-permute-start.3 = (f32[2,40,16,3]{1,2,3,0:T(8,128)}, f32[2,40,16,3]{1,2,3,0:T(8,128)}, u32[]{:S(2)}, u32[]{:S(2)}) collective-permute-start(f32[2,40,16,3]{1,2,3,0:T(8,128)} %copy.182), channel_id=1, source_target_pairs={{16,0},{32,16},{48,32},{64,48},{80,64},{96,80},{112,96},{128,112},... | collective-permute-start | bytes 46088 | tf_op jit(solution)/shard_map/ppermute | solution.py:20
  10.5 88.4 %collective-permute-start = (bf16[2,40,16,1]{3,2,1,0:T(8,128)(2,1)}, bf16[2,40,16,1]{3,2,1,0:T(8,128)(2,1)}, u32[]{:S(2)}, u32[]{:S(2)}) collective-permute-start(bf16[2,40,16,1]{3,2,1,0:T(8,128)(2,1)} %get-tuple-element.1324), channel_id=1, source_target_pairs={{0,16},{16,32},{32,48},{48,64},{64,80},{80,96},{96,112},{112,128},... | collective-permute-start | bytes 7688 | tf_op jit(solution)/shard_map/ppermute | solution.py:18
  10.5 88.4 %collective-permute-start.1 = (bf16[2,40,16,1]{3,2,1,0:T(8,128)(2,1)}, bf16[2,40,16,1]{3,2,1,0:T(8,128)(2,1)}, u32[]{:S(2)}, u32[]{:S(2)}) collective-permute-start(bf16[2,40,16,1]{3,2,1,0:T(8,128)(2,1)} %get-tuple-element.1325), channel_id=1, source_target_pairs={{16,0},{32,16},{48,32},{64,48},{80,64},{96,80},{112,96},{128,112},... | collective-permute-start | bytes 7688 | tf_op jit(solution)/shard_map/ppermute | solution.py:20
  18.6 1.4 copy-start.4
  20.1 0.7 copy-start.25
  20.1 1.9 %copy-start.23 = (f32[40]{0:T(128)S(1)}, f32[40]{0:T(128)}, u32[]{:S(2)}) copy-start(f32[40]{0:T(128)} %param.33) | copy-start | bytes 484
  20.1 2.2 %copy-start.24 = (f32[40]{0:T(128)S(1)}, f32[40]{0:T(128)}, u32[]{:S(2)}) copy-start(f32[40]{0:T(128)} %param.34) | copy-start | bytes 484
  61.7 16.0 %copy-start.19 = (f32[16,40,1]{1,0,2:T(8,128)}, f32[16,40,1]{1,0,2:T(8,128)S(1)}, u32[]{:S(2)}) copy-start(f32[16,40,1]{1,0,2:T(8,128)S(1)} %get-tuple-element.1328) | copy-start | bytes 7684
  91.4 1.2 copy-start.14
  91.4 1.2 copy-start.15
  91.5 2.6 %copy-start.13 = (f32[2,40,2,128]{3,2,1,0:T(2,128)S(1)}, f32[2,40,2,128]{3,2,1,0:T(2,128)}, u32[]{:S(2)}) copy-start(f32[2,40,2,128]{3,2,1,0:T(2,128)} %get-tuple-element.1313) | copy-start | bytes 245764
  92.6 0.7 copy-start.21
  92.6 0.7 copy-start.22
  92.6 1.4 copy-start.6
  92.6 1.4 copy-start.7
  94.0 1.1 copy-start.5
  94.1 1.1 copy-start.17
  94.1 1.1 copy-start.18
  95.1 1.0 copy-start.9
  95.1 1.1 copy-start.10
  95.2 1.1 copy-start.16
  97.8 1.1 copy-start.12
  107.5 4.5 %copy-start.8 = (f32[2,40,15,128]{3,1,2,0:T(8,128)S(1)}, f32[2,40,15,128]{3,1,2,0:T(8,128)}, u32[]{:S(2)}) copy-start(f32[2,40,15,128]{3,1,2,0:T(8,128)} %slice.365) | copy-start | bytes 1843204
  112.6 8.4 %copy-start.20 = (f32[16,40,1]{1,0,2:T(8,128)S(1)}, f32[16,40,1]{1,0,2:T(8,128)}, u32[]{:S(2)}) copy-start(f32[16,40,1]{1,0,2:T(8,128)} %copy-done.19) | copy-start | bytes 7684
  113.5 19.3 %all-to-all-start.2 = ((f32[40,16,128]{2,0,1:T(8,128)}), f32[40,16,128]{2,0,1:T(8,128)S(1)}, u32[]{:S(2)}, u32[]{:S(2)}) async-start(f32[40,16,128]{2,0,1:T(8,128)} %get-tuple-element.1302), calls=%async_computation.2 | async-start | bytes 655360 | tf_op jit(solution)/shard_map/all_to_all | solution.py:227
  132.8 17.5 %all-to-all-start = ((f32[40,16,128]{2,0,1:T(8,128)}), f32[40,16,128]{2,0,1:T(8,128)S(1)}, u32[]{:S(2)}, u32[]{:S(2)}) async-start(f32[40,16,128]{2,0,1:T(8,128)} %get-tuple-element.1303), calls=%async_computation | async-start | bytes 655360 | tf_op jit(solution)/shard_map/all_to_all | solution.py:226
  150.3 18.9 %all-to-all-start.3 = ((f32[640,1,128]{2,1,0:T(1,128)}), f32[640,1,128]{2,1,0:T(1,128)S(1)}, u32[]{:S(2)}, u32[]{:S(2)}) async-start(f32[640,1,128]{2,1,0:T(1,128)} %bitcast.55), calls=%async_computation.3 | async-start | bytes 655360 | tf_op jit(solution)/shard_map/all_to_all | solution.py:240
  169.1 14.4 %all-to-all-start.1 = ((f32[640,1,128]{2,1,0:T(1,128)}), f32[640,1,128]{2,1,0:T(1,128)S(1)}, u32[]{:S(2)}, u32[]{:S(2)}) async-start(f32[640,1,128]{2,1,0:T(1,128)} %bitcast.31), calls=%async_computation.1 | async-start | bytes 655360 | tf_op jit(solution)/shard_map/all_to_all | solution.py:239
where the time goes:
time: 186 us; the launch traced here: 184 us
  other arithmetic  40.6 us (22%)
  waiting for transfers between devices  38.7 us (21%)
  blocking collectives  35 us (19%)
  starting transfers between devices  31.8 us (17%)
  local copies, waits for them, and re-layouts  26.9 us (14%)
  loops' own time  7.7 us (4%)
  between operations  2.14 us (1%)
    unnamed x1, blocking collectives  35 us
    all_to_all x1, waiting for transfers between devices, shards(): lax.all_to_all(explicit[1], 'gz', split_axis=1, concat_axis=0, tiled=True)  11.1 us
    ppermute x2, starting transfers between devices, with_halo(): lax.ppermute(head, axis, [((i + 1) % count, i) for i in range(count)])  10.7 us
    all_to_all x1, waiting for transfers between devices, shards(): lax.all_to_all(finished[0], 'gz', split_axis=0, concat_axis=1, tiled=True)  9.67 us
    all_to_all x1, waiting for transfers between devices, shards(): lax.all_to_all(finished[1], 'gz', split_axis=0, concat_axis=1, tiled=True)  9.57 us
    div x80, other arithmetic, block_forward(): (unit_row + low_here[..., None] * solved_prev) / pivot_value[..., None]  8.8 us
    all_to_all x1, waiting for transfers between devices, shards(): lax.all_to_all(explicit[0], 'gz', split_axis=1, concat_axis=0, tiled=True)  8.31 us
    unnamed x69, local copies, waits for them, and re-layouts  7.87 us
  transfers between devices with their start and end apart: 8, of which 4 were waited for; matrix products, arithmetic and copies ran while one was open for 30% of the time, Pallas kernels for 0%

commit v1 on v0

v1 whole, which is shorter than its diff:
```python
import functools

import jax
import jax.numpy as jnp
from jax import lax
from jax.experimental import pallas as pl
from jax.experimental.pallas import tpu as pltpu
from jax.sharding import PartitionSpec as P

COURANT = 0.25
MIXED_BOOST = 4.0
HEAT_RATIO = 3.0
RATIOS = (1.0, HEAT_RATIO)
LEVELS = 40
ROWS = 16
LANES = 128
CELLS = LEVELS * ROWS
STATE = 5 * ROWS
VMEM = pl.BlockSpec(memory_space=pltpu.VMEM)
SMEM = pl.BlockSpec(memory_space=pltpu.SMEM)
PARAMS = pltpu.CompilerParams(vmem_limit_bytes=32 * 1024 * 1024)
F32 = jnp.float32


def iota(shape, dim):
    return lax.broadcasted_iota(jnp.int32, shape, dim)


def split3(x, axis):
    high = x.astype(jnp.bfloat16)
    rest = x - high.astype(F32)
    mid = rest.astype(jnp.bfloat16)
    low = (rest - mid.astype(F32)).astype(jnp.bfloat16)
    return jnp.concatenate([high, mid, low], axis=axis)


def flux(qs, speed_sum, mixing_sum):
    qm2, qm1, q0, q1, q2, q3 = qs
    speed = speed_sum * (0.5 * COURANT / 60.0)
    step = q0 - q1
    mean = (qm2 + q3) - 8.0 * (qm1 + q2) + 37.0 * (q0 + q1)
    skew = (qm2 - q3) - 5.0 * (qm1 - q2) + 10.0 * step
    return speed * mean + jnp.abs(speed) * skew + (0.5 * mixing_sum) * step


def strip_selectors():
    rows = [[-1] * 64 for _ in range(4)]
    for field in range(2):
        for cell in range(3):
            rows[field][3 * field + cell] = cell
            rows[field][8 + 3 * field + cell] = LANES - 3 + cell
        for cell in range(5):
            rows[field][16 + 16 * field + 3 + cell] = cell
            rows[field][24 + 16 * field + cell] = LANES - 5 + cell
    for kind in range(2):
        rows[2 + kind][6 + kind] = 0
        rows[2 + kind][14 + kind] = LANES - 1
        for cell in range(3):
            rows[2 + kind][48 + 8 * kind + 1 + cell] = cell
            rows[2 + kind][48 + 8 * kind + 4 + cell] = LANES - 3 + cell
    return rows


def lane_selector(lanes):
    row = iota((len(lanes), LANES), 0)
    lane = iota((len(lanes), LANES), 1)
    hit = jnp.zeros((len(lanes), LANES), jnp.bool_)
    start = 0
    while start < len(lanes):
        if lanes[start] < 0:
            start += 1
            continue
        stop = start + 1
        while stop < len(lanes) and lanes[stop] == lanes[stop - 1] + 1:
            stop += 1
        hit = hit | ((row >= start) & (row < stop) & (lane - row == lanes[start] - start))
        start = stop
    return jnp.where(hit, 1.0, 0.0).astype(jnp.bfloat16)


def pick_lanes(select, x):
    dims = (((1,), (1,)), ((), ()))
    if x.dtype == jnp.bfloat16:
        return lax.dot_general(select, x, dims, preferred_element_type=F32)
    high = x.astype(jnp.bfloat16)
    rest = x - high.astype(F32)
    mid = rest.astype(jnp.bfloat16)
    low = (rest - mid.astype(F32)).astype(jnp.bfloat16)
    parts = [lax.dot_general(select, p, dims, preferred_element_type=F32) for p in (high, mid, low)]
    return parts[0] + (parts[1] + parts[2])


def pack_kernel(w_ref, t_ref, east_ref, visc_ref, near_ref, far_ref, own_ref):
    odd = lax.rem(lax.axis_index("gx"), 2)
    rows = strip_selectors()
    total = None
    for ref, lanes in zip((w_ref, t_ref, east_ref, visc_ref), rows):
        part = pick_lanes(lane_selector(lanes), ref[...].reshape(CELLS, LANES))
        total = part if total is None else total + part
    left, right = total[0:8], total[8:16]
    is_odd = odd == 1
    near_ref[...] = jnp.where(is_odd, left, right)
    far_ref[...] = jnp.where(is_odd, right, left)
    own_ref[...] = total[16:]


def main_kernel(
    wn_ref, ws_ref, tn_ref, ts_ref, east_ref, north_ref, visc_ref, dens_ref, coup_ref, top_ref,
    rhs_ref, up_ref, down_ref, sums_ref, dense_ref, packed_ref,
):
    first = lax.axis_index("gz") * LEVELS
    tile = (ROWS, LANES)
    top = jnp.broadcast_to(top_ref[...], tile)
    lane = iota(tile, 1)
    one = jnp.ones(tile, F32)

    def resist(k):
        boost = jnp.where(first + k <= top, 1.0 / (1.0 + MIXED_BOOST), 1.0)
        return boost / (one * coup_ref[k])

    u = [one, one]
    v = [one, one]
    n = [one * dens_ref[0]] * 2
    m = [one * dens_ref[LEVELS - 1]] * 2
    for f in range(2):
        up_ref[f, 0] = u[f]
        down_ref[f, LEVELS - 1] = v[f]
    for k in range(1, LEVELS):
        j = LEVELS - 1 - k
        res_u = resist(k)
        res_v = resist(j + 1)
        for f in range(2):
            u[f] = u[f] + n[f] * (res_u * (1.0 / RATIOS[f]))
            n[f] = n[f] + dens_ref[k] * u[f]
            up_ref[f, k] = u[f]
            v[f] = v[f] + m[f] * (res_v * (1.0 / RATIOS[f]))
            m[f] = m[f] + dens_ref[j] * v[f]
            down_ref[f, j] = v[f]
    inv = [1.0 / n[f] for f in range(2)]

    for k in range(LEVELS):
        packed = jnp.where(lane < 16, up_ref[0, k] * inv[0], down_ref[0, k] * inv[0])
        packed = jnp.where(lane < 32, packed, up_ref[1, k] * inv[1])
        packed = jnp.where(lane < 48, packed, down_ref[1, k] * inv[1])
        packed = jnp.where(lane < 64, packed, one * dens_ref[k])
        packed_ref[k] = packed
    dense_ref[...] = pick_lanes(
        lane_selector([0, 16, 32, 48, 64, -1, -1, -1]), packed_ref[...].reshape(CELLS, LANES)
    )

    inside = (lane >= 2) & (lane <= LANES - 4)

    def level(k, carry):
        east = east_ref[k].astype(F32)
        north = north_ref[k].astype(F32)
        visc = visc_ref[k].astype(F32)
        east_sum = jnp.where(inside, east + pltpu.roll(east, LANES - 1, 1), 0.0)
        visc_x = jnp.where(inside, visc + pltpu.roll(visc, LANES - 1, 1), 0.0)
        north_sum = north + pltpu.roll(north, ROWS - 1, 0)
        visc_y = visc + pltpu.roll(visc, ROWS - 1, 0)
        weight = dens_ref[k]
        out = []
        for f, (now_ref, sec_ref) in enumerate(((wn_ref, ws_ref), (tn_ref, ts_ref))):
            q = sec_ref[k]
            qx = [q if s == 0 else pltpu.roll(q, (-s) % LANES, 1) for s in range(-2, 4)]
            fx = flux(qx, east_sum, visc_x)
            qy = [q if s == 0 else pltpu.roll(q, (-s) % ROWS, 0) for s in range(-2, 4)]
            fy = flux(qy, north_sum, visc_y)
            change = (pltpu.roll(fx, 1, 1) - fx) + (pltpu.roll(fy, 1, 0) - fy)
            explicit = now_ref[k] * (1.0 / 3.0) + (q + change) * (2.0 / 3.0)
            b = explicit * weight
            rhs_ref[f, k] = b
            out.append(carry[2 * f] + down_ref[f, k] * b)
            out.append(carry[2 * f + 1] + up_ref[f, k] * b)
        return tuple(out)

    zero = jnp.zeros(tile, F32)
    sums = lax.fori_loop(0, LEVELS, level, (zero,) * 4)
    for f in range(2):
        sums_ref[f * ROWS:(f + 1) * ROWS] = sums[2 * f] * inv[f]
        sums_ref[(2 + f) * ROWS:(3 + f) * ROWS] = sums[2 * f + 1] * inv[f]
    coef = jnp.zeros(tile, F32)
    boost = jnp.where(first <= top, 1.0 + MIXED_BOOST, 1.0)
    below = jnp.where(first >= 1, 1.0, 0.0)
    for f in range(2):
        values = (
            down_ref[f, 0] * inv[f],
            inv[f],
            up_ref[f, LEVELS - 1] * inv[f],
            boost * (coup_ref[0] * RATIOS[f] * below),
        )
        for i, value in enumerate(values):
            coef = jnp.where(lane == 4 * f + i, value, coef)
    sums_ref[4 * ROWS:] = coef


def face_spread():
    row = lax.rem(iota((24, LANES), 0), 8)
    lane = iota((24, LANES), 1)
    face = jnp.where(row < 3, row - 1, LANES - 6 + row)
    spread = jnp.where(lane == face, -1.0, 0.0) + jnp.where(lane == face + 1, 1.0, 0.0)
    return jnp.where(row < 6, spread, 0.0).astype(jnp.bfloat16)


def spread_faces(faces):
    return lax.dot_general(
        split3(faces, 0), face_spread(), (((0,), (0,)), ((), ())), preferred_element_type=F32
    )


def edge_kernel(near_ref, far_ref, own_ref, sums_ref, dense_ref, state_ref, faces_ref, strip_ref):
    odd = lax.rem(lax.axis_index("gx"), 2) == 1
    near, far = near_ref[...], far_ref[...]
    left = jnp.where(odd, near, far)
    right = jnp.where(odd, far, near)
    strip_ref[...] = own_ref[...]
    for f in range(2):
        strip_ref[16 * f:16 * f + 3] = left[3 * f:3 * f + 3]
        strip_ref[16 * f + 13:16 * f + 16] = right[3 * f:3 * f + 3]
    for kind in range(2):
        strip_ref[32 + 8 * kind:33 + 8 * kind] = left[6 + kind:7 + kind]
        strip_ref[39 + 8 * kind:40 + 8 * kind] = right[6 + kind:7 + kind]
    faces_ref[...] = jnp.zeros(faces_ref.shape, F32)
    weight = dense_ref[4:5] * (2.0 / 3.0)
    for side in range(2):
        at = 32 + 4 * side
        speed = strip_ref[at:at + 3] + strip_ref[at + 1:at + 4]
        mixing = strip_ref[at + 8:at + 11] + strip_ref[at + 9:at + 12]
        for f in range(2):
            at = 16 * f + 8 * side
            qs = [strip_ref[at + s:at + s + 3] for s in range(6)]
            faces_ref[8 * f + 3 * side:8 * f + 3 * side + 3] = flux(qs, speed, mixing) * weight
    for f in range(2):
        faces = faces_ref[8 * f:8 * f + 8]
        for part in range(2):
            product = faces * dense_ref[2 * f + part:2 * f + part + 1]
            folded = product[:, :LANES]
            for i in range(1, CELLS // LANES):
                folded = folded + product[:, i * LANES:(i + 1) * LANES]
            total = jnp.sum(spread_faces(folded).reshape(LANES // ROWS, ROWS, LANES), axis=0)
            at = (2 * (1 - part) + f) * ROWS
            state_ref[at:at + ROWS] = sums_ref[at:at + ROWS] + total
    state_ref[4 * ROWS:] = sums_ref[4 * ROWS:]


def unpack(state, f):
    yf = state[f * ROWS:(f + 1) * ROWS]
    yl = state[(2 + f) * ROWS:(3 + f) * ROWS]
    coef = state[4 * ROWS:]
    z = [jnp.broadcast_to(coef[:, 4 * f + i:4 * f + i + 1], (ROWS, LANES)) for i in range(4)]
    return (yf, yl, *z)


def join(lower, upper):
    lane = iota((ROWS, LANES), 1)
    firsts, lasts = [], []
    coef = jnp.zeros((ROWS, LANES), F32)
    for f in range(2):
        yf_a, yl_a, z11_a, z12_a, z22_a, a_a = unpack(lower, f)
        yf_b, yl_b, z11_b, z12_b, z22_b, a_b = unpack(upper, f)
        g = a_b / (1.0 + a_b * (z22_a + z11_b))
        flow = g * (yl_a - yf_b)
        firsts.append(yf_a - z12_a * flow)
        lasts.append(yl_b + z12_b * flow)
        values = (z11_a - z12_a * z12_a * g, z12_a * g * z12_b, z22_b - z12_b * z12_b * g, a_a)
        for i, value in enumerate(values):
            coef = jnp.where(lane == 4 * f + i, value, coef)
    return jnp.concatenate(firsts + lasts + [coef], axis=0)


def bit(place):
    return lax.rem(lax.div(lax.axis_index("gz"), 1 << place), 2) == 1


def join_pair(own, other, place):
    high = bit(place)
    return join(jnp.where(high, other, own), jnp.where(high, own, other))


def four_kernel(own_ref, one_ref, two_ref, three_ref, pair_ref, total_ref):
    mine = join_pair(own_ref[...], one_ref[...], 0)
    other = join_pair(two_ref[...], three_ref[...], 0)
    pair_ref[...] = other
    total_ref[...] = join_pair(mine, other, 1)


def two_kernel(place, own_ref, other_ref, total_ref):
    total_ref[...] = join_pair(own_ref[...], other_ref[...], place)


def final_kernel(rhs_ref, up_ref, down_ref, faces_ref, own_ref, p0_ref, p1_ref, p2_ref, p3_ref, w_ref, t_ref, b_ref):
    zero = jnp.zeros((ROWS, LANES), F32)
    partners = [p0_ref[...], p1_ref[...], p2_ref[...], p3_ref[...]]
    own = own_ref[...]
    flows = []
    for f in range(2):
        yf_above, z_above, a_above = zero, zero, zero
        yl_below, z_below = zero, zero
        for place in (3, 2, 1, 0):
            yf, yl, z11, z12, z22, a = unpack(partners[place], f)
            below = bit(place)
            g = a_above / (1.0 + a_above * (z_above + z22))
            flow = g * (yf_above - yl)
            yf_above = jnp.where(below, yf_above, yf + z12 * flow)
            z_above = jnp.where(below, z_above, z11 - z12 * z12 * g)
            a_above = jnp.where(below, a_above, a)
            g = a / (1.0 + a * (z_below + z11))
            flow = g * (yl_below - yf)
            yl_below = jnp.where(below, yl + z12 * flow, yl_below)
            z_below = jnp.where(below, z22 - z12 * z12 * g, z_below)
        yf, yl, z11, z12, z22, a = unpack(own, f)
        p = 1.0 + a * (z_below + z11)
        q = 1.0 + a_above * (z_above + z22)
        s_below = a * (yl_below - yf)
        s_above = a_above * (yf_above - yl)
        scale = z12 / (p * q - a * a_above * z12 * z12)
        flows.append((
            (s_below * q - a * z12 * s_above) * scale,
            (s_above * p - a_above * z12 * s_below) * scale,
            z12,
        ))
    for f in range(2):
        spread = spread_faces(faces_ref[8 * f:8 * f + 8]).reshape(LEVELS, ROWS, LANES)
        b_ref[f] = (rhs_ref[f] + spread) * flows[f][2][None]
    outs = (w_ref, t_ref)

    def upward(k, carry):
        new = []
        for f in range(2):
            s = carry[f] + up_ref[f, k] * b_ref[f, k]
            outs[f][k] = s * down_ref[f, k]
            new.append(s)
        return tuple(new)

    lax.fori_loop(0, LEVELS, upward, (flows[0][0], flows[1][0]))

    def downward(i, carry):
        k = LEVELS - 1 - i
        new = []
        for f in range(2):
            outs[f][k] = outs[f][k] + up_ref[f, k] * carry[f]
            new.append(carry[f] + down_ref[f, k] * b_ref[f, k])
        return tuple(new)

    lax.fori_loop(0, LEVELS, downward, (flows[0][1], flows[1][1]))


def call(kernel, shapes, in_specs, scratch=(), flops=0):
    return pl.pallas_call(
        kernel,
        out_shape=[jax.ShapeDtypeStruct(s, F32) for s in shapes],
        in_specs=in_specs,
        out_specs=[VMEM] * len(shapes),
        scratch_shapes=list(scratch),
        compiler_params=PARAMS,
        cost_estimate=pl.CostEstimate(flops=flops, bytes_accessed=flops // 8, transcendentals=0),
    )


def shards(
    vertical_now, vertical_section, theta_now, theta_section,
    east_wind, north_wind, eddy_viscosity, density, coupling, cloud_top,
):
    strip = (8, CELLS)
    count = 16
    near, far, own = call(pack_kernel, [strip, strip, (48, CELLS)], [VMEM] * 4)(
        vertical_section, theta_section, east_wind, eddy_viscosity
    )
    far = lax.ppermute(
        far, "gx", [(i, (i + 1) % count if i % 2 else (i - 1) % count) for i in range(count)]
    )
    near = lax.ppermute(near, "gx", [(i, i ^ 1) for i in range(count)])
    block = (2, LEVELS, ROWS, LANES)
    rhs, up, down, sums, dense = call(
        main_kernel,
        [block, block, block, (STATE, LANES), strip],
        [VMEM] * 7 + [SMEM, SMEM, VMEM],
        [pltpu.VMEM((LEVELS, ROWS, LANES), F32)],
        flops=16_000_000,
    )(
        vertical_now, vertical_section, theta_now, theta_section,
        east_wind, north_wind, eddy_viscosity, density, coupling, cloud_top,
    )
    state_shape = (STATE, LANES)
    state, faces = call(
        edge_kernel, [state_shape, (16, CELLS)], [VMEM] * 5, [pltpu.VMEM((48, CELLS), F32)]
    )(near, far, own, sums, dense)

    def swap(x, partner):
        return lax.ppermute(x, "gz", [(i, partner(i)) for i in range(count)])

    three, two, one = (swap(state, lambda i, k=k: i ^ k) for k in (3, 2, 1))
    pair, four = call(four_kernel, [state_shape] * 2, [VMEM] * 4)(state, one, two, three)
    four_other = swap(four, lambda i: i ^ 4)
    (eight,) = call(functools.partial(two_kernel, 2), [state_shape], [VMEM] * 2)(four, four_other)
    eight_other = swap(eight, lambda i: (7 - i // 2) * 2 + i % 2)
    part = (LEVELS, ROWS, LANES)
    w_next, t_next = call(
        final_kernel, [part, part], [VMEM] * 9, [pltpu.VMEM(block, F32)]
    )(rhs, up, down, faces, state, one, pair, four_other, eight_other)
    return (w_next, t_next)


def solution(mesh):
    wide = P("gz", None, "gx")
    return jax.shard_map(
        shards,
        mesh=mesh,
        in_specs=(wide,) * 7 + (P("gz"), P("gz"), P(None, "gx")),
        out_specs=(wide, wide),
        check_vma=False,
    )
```

time: 186 us -> 44.3 us (0.24)
  other arithmetic: 40.6 us -> 0 us
  blocking collectives: 35 us -> 0 us
  waiting for transfers between devices: 38.7 us -> 7.63 us
  local copies, waits for them, and re-layouts: 26.9 us -> 6.74 us
  starting transfers between devices: 31.8 us -> 17 us
  Pallas kernels: 0 us -> 11.4 us
  loops' own time: 7.7 us -> 0 us
    all_to_all x4 -> x0, waiting for transfers between devices: 38.7 us -> none  [the longest x1 11.1 us: shards(): lax.all_to_all(explicit[1], 'gz', split_axis=1, concat_axis=0, tiled=True)]
    unnamed x1 -> x0, blocking collectives: 35 us -> none
    all_to_all x4 -> x0, starting transfers between devices: 21.1 us -> none  [the longest x1 6.93 us: shards(): lax.all_to_all(explicit[1], 'gz', split_axis=1, concat_axis=0, tiled=True)]
    pallas_call x0 -> x6, Pallas kernels: none -> 11.4 us  [the longest x1 8.2 us: shards(): call(main_kernel, [block, block, block, (STATE, LANES), strip], [VMEM] *...]
    div x80 -> x0, other arithmetic: 8.8 us -> none  [block_forward(): (unit_row + low_here[..., None] * solved_prev) / pivot_value[..., None]]
    sub x36 -> x0, other arithmetic: 8.59 us -> none  [the longest x2 6.03 us: face_flux(): return COURANT * face_speed * upwind - mixing * (shifted(1) - shifted(0))]
    another operation x10 -> x0, other arithmetic: 7.86 us -> none  [the longest x8 6.85 us: shards(): section_pair = jnp.stack([vertical_section, theta_section])]
    add x81 -> x0, other arithmetic: 7.81 us -> none  [the longest x80 7.16 us: block_backward(): current = solved + ratio_here[..., None] * following]
  transfers between devices with their start and end apart: 8 -> 7, of which waited for: 4 -> 4; matrix products, arithmetic and copies ran while one was open for 30% -> 0% of each run, Pallas kernels for 0% -> 19%
where the time goes in v1:
time: 44.3 us; the launch traced here: 43.6 us
  starting transfers between devices  17 us (38%)
  Pallas kernels  11.4 us (26%)
  waiting for transfers between devices  7.63 us (17%)
  local copies, waits for them, and re-layouts  6.74 us (15%)
  between operations  0.77 us (2%)
    ppermute x5, starting transfers between devices, swap(): return lax.ppermute(x, 'gz', [(i, partner(i)) for i in range(count)])  12.3 us
    pallas_call x1, Pallas kernels, shards(): call(main_kernel, [block, block, block, (STATE, LANES), strip], [VMEM] *...  8.2 us
    ppermute x5, waiting for transfers between devices, swap(): return lax.ppermute(x, 'gz', [(i, partner(i)) for i in range(count)])  7.62 us
    unnamed x29, local copies, waits for them, and re-layouts  6.74 us
    ppermute x1, starting transfers between devices, shards(): lax.ppermute(far, 'gx', [(i, (i + 1) % count if i % 2 else (i - 1) % coun...  4.65 us
    pallas_call x1, Pallas kernels, shards(): call(final_kernel, [part, part], [VMEM] * 9, [pltpu.VMEM(block, F32)])  1.87 us
  transfers between devices with their start and end apart: 7, of which 4 were waited for; matrix products, arithmetic and copies ran while one was open for 0% of the time, Pallas kernels for 19%

profile of v1, /device:TPU:2, one launch (start us, length us, event | category | flops | bytes accessed | tf_op | source)
XLA Modules:
  0.0 43.6 jit_solution(14095410430939883534)
XLA Ops:
  0.6 0.0 copy-start
  0.6 1.0 %copy-done = f32[40,16,128]{2,1,0:T(8,128)S(1)} copy-done((f32[40,16,128]{2,1,0:T(8,128)S(1)}, f32[40,16,128]{2,1,0:T(8,128)}, u32[]{:S(2)}) %copy-start) | copy-done | bytes 327704
  1.6 0.0 copy-start.2
  1.6 1.0 %copy-done.2 = f32[40,16,128]{2,1,0:T(8,128)S(1)} copy-done((f32[40,16,128]{2,1,0:T(8,128)S(1)}, f32[40,16,128]{2,1,0:T(8,128)}, u32[]{:S(2)}) %copy-start.2) | copy-done | bytes 327704
  2.6 0.0 copy-start.4
  2.6 0.9 %copy-done.4 = bf16[40,16,128]{2,1,0:T(8,128)(2,1)S(1)} copy-done((bf16[40,16,128]{2,1,0:T(8,128)(2,1)S(1)}, bf16[40,16,128]{2,1,0:T(8,128)(2,1)}, u32[]{:S(2)}) %copy-start.4) | copy-done | bytes 163864
  3.5 0.0 copy-start.6
  3.5 0.9 %copy-done.6 = bf16[40,16,128]{2,1,0:T(8,128)(2,1)S(1)} copy-done((bf16[40,16,128]{2,1,0:T(8,128)(2,1)S(1)}, bf16[40,16,128]{2,1,0:T(8,128)(2,1)}, u32[]{:S(2)}) %copy-start.6) | copy-done | bytes 163864
  4.4 0.0 copy-start.1
  4.4 0.0 copy-start.3
  4.4 0.0 copy-start.5
  4.4 0.0 copy-start.7
  4.4 0.6 %shard_map.114 = (f32[8,640]{1,0:T(8,128)S(1)}, f32[8,640]{1,0:T(8,128)S(1)}, f32[48,640]{1,0:T(8,128)S(1)}) custom-call(f32[40,16,128]{2,1,0:T(8,128)S(1)} %copy-done, f32[40,16,128]{2,1,0:T(8,128)S(1)} %copy-done.2, bf16[40,16,128]{2,1,0:T(8,128)(2,1)S(1)} %copy-done.4, bf16[40,16,128]{2,1,0:T(8,128)(2,1)S(1)} %copy-done.6), custom_call_target="tpu_custom_call" | custom-call | tf_op jit(solution)/shard_map/pallas_call | solution.py:366
  5.0 0.0 copy-start.13
  5.0 0.1 collective-permute-start
  5.2 0.0 copy-start.11
  5.2 0.0 copy-start.12
  5.2 4.7 %collective-permute-start.1 = (f32[8,640]{1,0:T(8,128)S(1)}, f32[8,640]{1,0:T(8,128)S(1)}, u32[]{:S(2)}, u32[]{:S(2)}) collective-permute-start(f32[8,640]{1,0:T(8,128)S(1)} %get-tuple-element.18), channel_id=1, source_target_pairs={{0,240},{16,32},{32,16},{48,64},{64,48},{80,96},{96,80},{112,128},... | collective-permute-start | bytes 61448 | tf_op jit(solution)/shard_map/ppermute | solution.py:369
  9.8 0.0 copy-done.13
  9.8 0.1 copy.12.top_ref
  9.9 0.0 copy-done.1
  9.9 0.0 copy-done.3
  9.9 0.0 copy-done.5
  9.9 0.0 copy-done.7
  9.9 0.0 copy-done.11
  9.9 0.0 copy-done.12
  10.0 0.0 copy-start.8
  10.0 1.0 %copy-done.8 = f32[40,16,128]{2,1,0:T(8,128)S(1)} copy-done((f32[40,16,128]{2,1,0:T(8,128)S(1)}, f32[40,16,128]{2,1,0:T(8,128)}, u32[]{:S(2)}) %copy-start.8) | copy-done | bytes 327704
  10.9 0.0 copy-start.9
  10.9 1.0 %copy-done.9 = f32[40,16,128]{2,1,0:T(8,128)S(1)} copy-done((f32[40,16,128]{2,1,0:T(8,128)S(1)}, f32[40,16,128]{2,1,0:T(8,128)}, u32[]{:S(2)}) %copy-start.9) | copy-done | bytes 327704
  11.9 0.0 copy-start.10
  11.9 0.9 %copy-done.10 = bf16[40,16,128]{2,1,0:T(8,128)(2,1)S(1)} copy-done((bf16[40,16,128]{2,1,0:T(8,128)(2,1)S(1)}, bf16[40,16,128]{2,1,0:T(8,128)(2,1)}, u32[]{:S(2)}) %copy-start.10) | copy-done | bytes 163864
  12.8 8.2 %shard_map.113 = (f32[2,40,16,128]{3,2,1,0:T(8,128)S(1)}, f32[2,40,16,128]{3,2,1,0:T(8,128)S(1)}, f32[2,40,16,128]{3,2,1,0:T(8,128)S(1)}, f32[80,128]{1,0:T(8,128)S(1)}, f32[8,640]{1,0:T(8,128)S(1)}) custom-call(f32[40,16,128]{2,1,0:T(8,128)S(1)} %copy-done.8, f32[40,16,128]{2,1,0:T(8,128)S(1)} %copy-done.1, f32[40,16,128]{2,1,0:T(8,128)S(1)} %copy-done.9, ...), custom_call_target="tpu_custom_call" | custom-call | flops 16000000 | bytes 2000000 | tf_op jit(solution)/shard_map/pallas_call | solution.py:374
  21.0 0.0 collective-permute-done.near_ref
  21.0 0.0 collective-permute-done.1.far_ref
  21.1 0.3 shard_map.115
  21.4 2.9 %collective-permute-start.4 = (f32[80,128]{1,0:T(8,128)S(1)}, f32[80,128]{1,0:T(8,128)S(1)}, u32[]{:S(2)}, u32[]{:S(2)}) collective-permute-start(f32[80,128]{1,0:T(8,128)S(1)} %get-tuple-element.23.own_ref), channel_id=1, source_target_pairs={{0,3},{1,2},{2,1},{3,0},{4,7},{5,6},{6,5},{7,4},{8,11},{9,10},{10,... | collective-permute-start | bytes 122888 | tf_op jit(solution)/shard_map/ppermute | solution.py:390
  24.3 0.1 collective-permute-start.3
  24.4 0.6 %collective-permute-start.2 = (f32[80,128]{1,0:T(8,128)S(1)}, f32[80,128]{1,0:T(8,128)S(1)}, u32[]{:S(2)}, u32[]{:S(2)}) collective-permute-start(f32[80,128]{1,0:T(8,128)S(1)} %get-tuple-element.23.own_ref), channel_id=1, source_target_pairs={{0,1},{1,0},{2,3},{3,2},{4,5},{5,4},{6,7},{7,6},{8,9},{9,8},{10,11... | collective-permute-start | bytes 122888 | tf_op jit(solution)/shard_map/ppermute | solution.py:390
  25.0 1.4 %collective-permute-done.4.three_ref = f32[80,128]{1,0:T(8,128)S(1)} collective-permute-done((f32[80,128]{1,0:T(8,128)S(1)}, f32[80,128]{1,0:T(8,128)S(1)}, u32[]{:S(2)}, u32[]{:S(2)}) %collective-permute-start.4) | collective-permute-done | bytes 40992 | tf_op jit(solution)/shard_map/ppermute | solution.py:390
  26.4 2.2 %collective-permute-done.3.two_ref = f32[80,128]{1,0:T(8,128)S(1)} collective-permute-done((f32[80,128]{1,0:T(8,128)S(1)}, f32[80,128]{1,0:T(8,128)S(1)}, u32[]{:S(2)}, u32[]{:S(2)}) %collective-permute-start.3) | collective-permute-done | bytes 40992 | tf_op jit(solution)/shard_map/ppermute | solution.py:390
  28.6 0.0 collective-permute-done.2.one_ref.p0_ref
  28.6 0.3 shard_map.116
  28.9 3.1 %collective-permute-start.5 = (f32[80,128]{1,0:T(8,128)S(1)}, f32[80,128]{1,0:T(8,128)S(1)}, u32[]{:S(2)}, u32[]{:S(2)}) collective-permute-start(f32[80,128]{1,0:T(8,128)S(1)} %get-tuple-element.25.own_ref), channel_id=1, source_target_pairs={{0,4},{1,5},{2,6},{3,7},{4,0},{5,1},{6,2},{7,3},{8,12},{9,13},{10,... | collective-permute-start | bytes 122888 | tf_op jit(solution)/shard_map/ppermute | solution.py:390
  32.1 2.0 %collective-permute-done.5.other_ref.p2_ref = f32[80,128]{1,0:T(8,128)S(1)} collective-permute-done((f32[80,128]{1,0:T(8,128)S(1)}, f32[80,128]{1,0:T(8,128)S(1)}, u32[]{:S(2)}, u32[]{:S(2)}) %collective-permute-start.5) | collective-permute-done | bytes 40992 | tf_op jit(solution)/shard_map/ppermute | solution.py:390
  34.0 0.1 shard_map.117
  34.2 5.6 %collective-permute-start.6 = (f32[80,128]{1,0:T(8,128)S(1)}, f32[80,128]{1,0:T(8,128)S(1)}, u32[]{:S(2)}, u32[]{:S(2)}) collective-permute-start(f32[80,128]{1,0:T(8,128)S(1)} %shard_map.117), channel_id=1, source_target_pairs={{0,14},{1,15},{2,12},{3,13},{4,10},{5,11},{6,8},{7,9},{8,6},{9,7},... | collective-permute-start | bytes 122888 | tf_op jit(solution)/shard_map/ppermute | solution.py:390
  39.7 2.0 %collective-permute-done.6.p3_ref = f32[80,128]{1,0:T(8,128)S(1)} collective-permute-done((f32[80,128]{1,0:T(8,128)S(1)}, f32[80,128]{1,0:T(8,128)S(1)}, u32[]{:S(2)}, u32[]{:S(2)}) %collective-permute-start.6) | collective-permute-done | bytes 40992 | tf_op jit(solution)/shard_map/ppermute | solution.py:390
  41.7 1.9 %shard_map.118 = (f32[40,16,128]{2,1,0:T(8,128)}, f32[40,16,128]{2,1,0:T(8,128)}) custom-call(f32[2,40,16,128]{3,2,1,0:T(8,128)S(1)} %get-tuple-element.14.rhs_ref, f32[2,40,16,128]{3,2,1,0:T(8,128)S(1)} %get-tuple-element.15.up_ref, f32[2,40,16,128]{3,2,1,0:T(8,128)S(1)} %get-tuple-element.16.down_ref, f32[16,640]{1,0:T(8,128)S(1)} %get-tuple-element.22.faces_ref, ...), custom_call_target="tpu_custom_call" | custom-call | tf_op jit(solution)/shard_map/pallas_call | solution.py:398
Async XLA Ops:
  0.6 1.0 %copy-start = (f32[40,16,128]{2,1,0:T(8,128)S(1)}, f32[40,16,128]{2,1,0:T(8,128)}, u32[]{:S(2)}) copy-start(f32[40,16,128]{2,1,0:T(8,128)} %w_ref.1) | copy-start | bytes 983044
  1.6 1.0 %copy-start.2 = (f32[40,16,128]{2,1,0:T(8,128)S(1)}, f32[40,16,128]{2,1,0:T(8,128)}, u32[]{:S(2)}) copy-start(f32[40,16,128]{2,1,0:T(8,128)} %t_ref.1) | copy-start | bytes 983044
  2.6 0.9 %copy-start.4 = (bf16[40,16,128]{2,1,0:T(8,128)(2,1)S(1)}, bf16[40,16,128]{2,1,0:T(8,128)(2,1)}, u32[]{:S(2)}) copy-start(bf16[40,16,128]{2,1,0:T(8,128)(2,1)} %east_ref.3) | copy-start | bytes 491524
  3.5 0.9 %copy-start.6 = (bf16[40,16,128]{2,1,0:T(8,128)(2,1)S(1)}, bf16[40,16,128]{2,1,0:T(8,128)(2,1)}, u32[]{:S(2)}) copy-start(bf16[40,16,128]{2,1,0:T(8,128)(2,1)} %visc_ref.3) | copy-start | bytes 491524
  4.4 5.5 %copy-start.1 = (f32[40,16,128]{2,1,0:T(8,128)S(1)}, f32[40,16,128]{2,1,0:T(8,128)}, u32[]{:S(2)}) copy-start(f32[40,16,128]{2,1,0:T(8,128)} %w_ref.1) | copy-start | bytes 983044
  4.4 5.5 %copy-start.3 = (f32[40,16,128]{2,1,0:T(8,128)S(1)}, f32[40,16,128]{2,1,0:T(8,128)}, u32[]{:S(2)}) copy-start(f32[40,16,128]{2,1,0:T(8,128)} %t_ref.1) | copy-start | bytes 983044
  4.4 5.5 %copy-start.5 = (bf16[40,16,128]{2,1,0:T(8,128)(2,1)S(1)}, bf16[40,16,128]{2,1,0:T(8,128)(2,1)}, u32[]{:S(2)}) copy-start(bf16[40,16,128]{2,1,0:T(8,128)(2,1)} %east_ref.3) | copy-start | bytes 491524
  4.4 5.5 %copy-start.7 = (bf16[40,16,128]{2,1,0:T(8,128)(2,1)S(1)}, bf16[40,16,128]{2,1,0:T(8,128)(2,1)}, u32[]{:S(2)}) copy-start(bf16[40,16,128]{2,1,0:T(8,128)(2,1)} %visc_ref.3) | copy-start | bytes 491524
  5.0 4.8 %copy-start.13 = (s32[16,1]{0,1:T(1,128)S(1)}, s32[16,1]{0,1:T(1,128)}, u32[]{:S(2)}) copy-start(s32[16,1]{0,1:T(1,128)} %param.19) | copy-start | bytes 196
  5.0 16.0 %collective-permute-start = (f32[8,640]{1,0:T(8,128)S(1)}, f32[8,640]{1,0:T(8,128)S(1)}, u32[]{:S(2)}, u32[]{:S(2)}) collective-permute-start(f32[8,640]{1,0:T(8,128)S(1)} %get-tuple-element.17), channel_id=1, source_target_pairs={{0,16},{16,0},{32,48},{48,32},{64,80},{80,64},{96,112},{112,96},{1... | collective-permute-start | bytes 61448 | tf_op jit(solution)/shard_map/ppermute | solution.py:372
  5.2 4.8 %copy-start.11 = (f32[40]{0:T(128)S(1)}, f32[40]{0:T(128)}, u32[]{:S(2)}) copy-start(f32[40]{0:T(128)} %dens_ref.1) | copy-start | bytes 484
  5.2 4.8 %copy-start.12 = (f32[40]{0:T(128)S(1)}, f32[40]{0:T(128)}, u32[]{:S(2)}) copy-start(f32[40]{0:T(128)} %coup_ref.1) | copy-start | bytes 484
  5.2 15.9 %collective-permute-start.1 = (f32[8,640]{1,0:T(8,128)S(1)}, f32[8,640]{1,0:T(8,128)S(1)}, u32[]{:S(2)}, u32[]{:S(2)}) collective-permute-start(f32[8,640]{1,0:T(8,128)S(1)} %get-tuple-element.18), channel_id=1, source_target_pairs={{0,240},{16,32},{32,16},{48,64},{64,48},{80,96},{96,80},{112,128},... | collective-permute-start | bytes 61448 | tf_op jit(solution)/shard_map/ppermute | solution.py:369
  10.0 1.0 %copy-start.8 = (f32[40,16,128]{2,1,0:T(8,128)S(1)}, f32[40,16,128]{2,1,0:T(8,128)}, u32[]{:S(2)}) copy-start(f32[40,16,128]{2,1,0:T(8,128)} %wn_ref.1) | copy-start | bytes 983044
  10.9 1.0 %copy-start.9 = (f32[40,16,128]{2,1,0:T(8,128)S(1)}, f32[40,16,128]{2,1,0:T(8,128)}, u32[]{:S(2)}) copy-start(f32[40,16,128]{2,1,0:T(8,128)} %tn_ref.1) | copy-start | bytes 983044
  11.9 0.9 %copy-start.10 = (bf16[40,16,128]{2,1,0:T(8,128)(2,1)S(1)}, bf16[40,16,128]{2,1,0:T(8,128)(2,1)}, u32[]{:S(2)}) copy-start(bf16[40,16,128]{2,1,0:T(8,128)(2,1)} %north_ref.1) | copy-start | bytes 491524
  21.4 5.0 %collective-permute-start.4 = (f32[80,128]{1,0:T(8,128)S(1)}, f32[80,128]{1,0:T(8,128)S(1)}, u32[]{:S(2)}, u32[]{:S(2)}) collective-permute-start(f32[80,128]{1,0:T(8,128)S(1)} %get-tuple-element.23.own_ref), channel_id=1, source_target_pairs={{0,3},{1,2},{2,1},{3,0},{4,7},{5,6},{6,5},{7,4},{8,11},{9,10},{10,... | collective-permute-start | bytes 122888 | tf_op jit(solution)/shard_map/ppermute | solution.py:390
  24.3 4.4 %collective-permute-start.3 = (f32[80,128]{1,0:T(8,128)S(1)}, f32[80,128]{1,0:T(8,128)S(1)}, u32[]{:S(2)}, u32[]{:S(2)}) collective-permute-start(f32[80,128]{1,0:T(8,128)S(1)} %get-tuple-element.23.own_ref), channel_id=1, source_target_pairs={{0,2},{1,3},{2,0},{3,1},{4,6},{5,7},{6,4},{7,5},{8,10},{9,11},{10,... | collective-permute-start | bytes 122888 | tf_op jit(solution)/shard_map/ppermute | solution.py:390
  24.4 4.2 %collective-permute-start.2 = (f32[80,128]{1,0:T(8,128)S(1)}, f32[80,128]{1,0:T(8,128)S(1)}, u32[]{:S(2)}, u32[]{:S(2)}) collective-permute-start(f32[80,128]{1,0:T(8,128)S(1)} %get-tuple-element.23.own_ref), channel_id=1, source_target_pairs={{0,1},{1,0},{2,3},{3,2},{4,5},{5,4},{6,7},{7,6},{8,9},{9,8},{10,11... | collective-permute-start | bytes 122888 | tf_op jit(solution)/shard_map/ppermute | solution.py:390
  28.9 5.1 %collective-permute-start.5 = (f32[80,128]{1,0:T(8,128)S(1)}, f32[80,128]{1,0:T(8,128)S(1)}, u32[]{:S(2)}, u32[]{:S(2)}) collective-permute-start(f32[80,128]{1,0:T(8,128)S(1)} %get-tuple-element.25.own_ref), channel_id=1, source_target_pairs={{0,4},{1,5},{2,6},{3,7},{4,0},{5,1},{6,2},{7,3},{8,12},{9,13},{10,... | collective-permute-start | bytes 122888 | tf_op jit(solution)/shard_map/ppermute | solution.py:390
  34.2 7.6 %collective-permute-start.6 = (f32[80,128]{1,0:T(8,128)S(1)}, f32[80,128]{1,0:T(8,128)S(1)}, u32[]{:S(2)}, u32[]{:S(2)}) collective-permute-start(f32[80,128]{1,0:T(8,128)S(1)} %shard_map.117), channel_id=1, source_target_pairs={{0,14},{1,15},{2,12},{3,13},{4,10},{5,11},{6,8},{7,9},{8,6},{9,7},... | collective-permute-start | bytes 122888 | tf_op jit(solution)/shard_map/ppermute | solution.py:390

commit v2 on v1

--- a/solution.py
+++ b/solution.py
@@ -16,6 +16,9 @@
 LANES = 128
 CELLS = LEVELS * ROWS
 STATE = 5 * ROWS
+PARTS = 5
+UNROLL = 4
+HBM = pl.BlockSpec(memory_space=pltpu.HBM)
 VMEM = pl.BlockSpec(memory_space=pltpu.VMEM)
 SMEM = pl.BlockSpec(memory_space=pltpu.SMEM)
 PARAMS = pltpu.CompilerParams(vmem_limit_bytes=32 * 1024 * 1024)
@@ -90,29 +93,41 @@
     return parts[0] + (parts[1] + parts[2])
 
 
-def pack_kernel(w_ref, t_ref, east_ref, visc_ref, near_ref, far_ref, own_ref):
-    odd = lax.rem(lax.axis_index("gx"), 2)
-    rows = strip_selectors()
-    total = None
-    for ref, lanes in zip((w_ref, t_ref, east_ref, visc_ref), rows):
-        part = pick_lanes(lane_selector(lanes), ref[...].reshape(CELLS, LANES))
-        total = part if total is None else total + part
-    left, right = total[0:8], total[8:16]
-    is_odd = odd == 1
-    near_ref[...] = jnp.where(is_odd, left, right)
-    far_ref[...] = jnp.where(is_odd, right, left)
-    own_ref[...] = total[16:]
-
-
-def main_kernel(
-    wn_ref, ws_ref, tn_ref, ts_ref, east_ref, north_ref, visc_ref, dens_ref, coup_ref, top_ref,
-    rhs_ref, up_ref, down_ref, sums_ref, dense_ref, packed_ref,
+def prep_kernel(
+    ws_hbm, ts_hbm, east_hbm, visc_hbm, wn_hbm, tn_hbm, north_hbm, dens_hbm, coup_hbm, top_hbm,
+    ws_ref, ts_ref, east_ref, visc_ref, wn_ref, tn_ref, north_ref,
+    near_ref, far_ref, own_ref, up_ref, down_ref, rho_ref, dense_ref, coef_ref,
+    packed_ref, dens_ref, coup_ref, top_ref, small_sem, big_sem,
 ):
+    small = [
+        pltpu.make_async_copy(src, dst, small_sem.at[i])
+        for i, (src, dst) in enumerate(
+            ((dens_hbm, dens_ref), (coup_hbm, coup_ref), (top_hbm, top_ref))
+        )
+    ]
+    big = []
+    for i, (src, dst) in enumerate((
+        (ws_hbm, ws_ref), (ts_hbm, ts_ref), (east_hbm, east_ref), (visc_hbm, visc_ref),
+        (wn_hbm, wn_ref), (tn_hbm, tn_ref), (north_hbm, north_ref),
+    )):
+        for part in range(PARTS):
+            levels = pl.ds(part * (LEVELS // PARTS), LEVELS // PARTS)
+            big.append(pltpu.make_async_copy(
+                src.at[levels], dst.at[levels], big_sem.at[i * PARTS + part]
+            ))
+    for copy in small + big:
+        copy.start()
+    for copy in small:
+        copy.wait()
+
     first = lax.axis_index("gz") * LEVELS
     tile = (ROWS, LANES)
-    top = jnp.broadcast_to(top_ref[...], tile)
     lane = iota(tile, 1)
+    row = iota(tile, 0)
     one = jnp.ones(tile, F32)
+    top = jnp.zeros(tile, jnp.int32)
+    for j in range(ROWS):
+        top = jnp.where(row == j, top_ref[0, j], top)
 
     def resist(k):
         boost = jnp.where(first + k <= top, 1.0 / (1.0 + MIXED_BOOST), 1.0)
@@ -122,6 +137,7 @@
     v = [one, one]
     n = [one * dens_ref[0]] * 2
     m = [one * dens_ref[LEVELS - 1]] * 2
+    rho_ref[0] = n[0]
     for f in range(2):
         up_ref[f, 0] = u[f]
         down_ref[f, LEVELS - 1] = v[f]
@@ -129,6 +145,7 @@
         j = LEVELS - 1 - k
         res_u = resist(k)
         res_v = resist(j + 1)
+        rho_ref[k] = one * dens_ref[k]
         for f in range(2):
             u[f] = u[f] + n[f] * (res_u * (1.0 / RATIOS[f]))
             n[f] = n[f] + dens_ref[k] * u[f]
@@ -142,12 +159,48 @@
         packed = jnp.where(lane < 16, up_ref[0, k] * inv[0], down_ref[0, k] * inv[0])
         packed = jnp.where(lane < 32, packed, up_ref[1, k] * inv[1])
         packed = jnp.where(lane < 48, packed, down_ref[1, k] * inv[1])
-        packed = jnp.where(lane < 64, packed, one * dens_ref[k])
-        packed_ref[k] = packed
+        packed_ref[k] = jnp.where(lane < 64, packed, rho_ref[k])
     dense_ref[...] = pick_lanes(
         lane_selector([0, 16, 32, 48, 64, -1, -1, -1]), packed_ref[...].reshape(CELLS, LANES)
     )
 
+    coef = jnp.zeros(tile, F32)
+    boost = jnp.where(first <= top, 1.0 + MIXED_BOOST, 1.0)
+    below = jnp.where(first >= 1, 1.0, 0.0)
+    for f in range(2):
+        values = (
+            down_ref[f, 0] * inv[f],
+            inv[f],
+            up_ref[f, LEVELS - 1] * inv[f],
+            boost * (coup_ref[0] * RATIOS[f] * below),
+        )
+        for i, value in enumerate(values):
+            coef = jnp.where(lane == 4 * f + i, value, coef)
+    coef_ref[...] = coef
+
+    for copy in big[:4 * PARTS]:
+        copy.wait()
+    odd = lax.rem(lax.axis_index("gx"), 2)
+    rows = strip_selectors()
+    total = None
+    for ref, lanes in zip((ws_ref, ts_ref, east_ref, visc_ref), rows):
+        part = pick_lanes(lane_selector(lanes), ref[...].reshape(CELLS, LANES))
+        total = part if total is None else total + part
+    left, right = total[0:8], total[8:16]
+    is_odd = odd == 1
+    near_ref[...] = jnp.where(is_odd, left, right)
+    far_ref[...] = jnp.where(is_odd, right, left)
+    own_ref[...] = total[16:]
+    for copy in big[4 * PARTS:]:
+        copy.wait()
+
+
+def main_kernel(
+    wn_ref, ws_ref, tn_ref, ts_ref, east_ref, north_ref, visc_ref, rho_ref, up_ref, down_ref, coef_ref,
+    rhs_ref, sums_ref,
+):
+    tile = (ROWS, LANES)
+    lane = iota(tile, 1)
     inside = (lane >= 2) & (lane <= LANES - 4)
 
     def level(k, carry):
@@ -158,7 +211,7 @@
         visc_x = jnp.where(inside, visc + pltpu.roll(visc, LANES - 1, 1), 0.0)
         north_sum = north + pltpu.roll(north, ROWS - 1, 0)
         visc_y = visc + pltpu.roll(visc, ROWS - 1, 0)
-        weight = dens_ref[k]
+        weight = rho_ref[k]
         out = []
         for f, (now_ref, sec_ref) in enumerate(((wn_ref, ws_ref), (tn_ref, ts_ref))):
             q = sec_ref[k]
@@ -174,23 +227,18 @@
             out.append(carry[2 * f + 1] + up_ref[f, k] * b)
         return tuple(out)
 
+    def levels(i, carry):
+        for step in range(UNROLL):
+            carry = level(i * UNROLL + step, carry)
+        return carry
+
     zero = jnp.zeros(tile, F32)
-    sums = lax.fori_loop(0, LEVELS, level, (zero,) * 4)
-    for f in range(2):
-        sums_ref[f * ROWS:(f + 1) * ROWS] = sums[2 * f] * inv[f]
-        sums_ref[(2 + f) * ROWS:(3 + f) * ROWS] = sums[2 * f + 1] * inv[f]
-    coef = jnp.zeros(tile, F32)
-    boost = jnp.where(first <= top, 1.0 + MIXED_BOOST, 1.0)
-    below = jnp.where(first >= 1, 1.0, 0.0)
-    for f in range(2):
-        values = (
-            down_ref[f, 0] * inv[f],
-            inv[f],
-            up_ref[f, LEVELS - 1] * inv[f],
-            boost * (coup_ref[0] * RATIOS[f] * below),
-        )
-        for i, value in enumerate(values):
-            coef = jnp.where(lane == 4 * f + i, value, coef)
+    sums = lax.fori_loop(0, LEVELS // UNROLL, levels, (zero,) * 4)
+    coef = coef_ref[...]
+    for f in range(2):
+        inv = jnp.broadcast_to(coef[:, 4 * f + 1:4 * f + 2], tile)
+        sums_ref[f * ROWS:(f + 1) * ROWS] = sums[2 * f] * inv
+        sums_ref[(2 + f) * ROWS:(3 + f) * ROWS] = sums[2 * f + 1] * inv
     sums_ref[4 * ROWS:] = coef
 
 
@@ -288,7 +336,38 @@
     total_ref[...] = join_pair(own_ref[...], other_ref[...], place)
 
 
-def final_kernel(rhs_ref, up_ref, down_ref, faces_ref, own_ref, p0_ref, p1_ref, p2_ref, p3_ref, w_ref, t_ref, b_ref):
+def local_kernel(rhs_ref, up_ref, down_ref, faces_ref, state_ref, y_ref, b_ref):
+    zero = jnp.zeros((ROWS, LANES), F32)
+    coef = state_ref[4 * ROWS:]
+    for f in range(2):
+        inv = jnp.broadcast_to(coef[:, 4 * f + 1:4 * f + 2], (ROWS, LANES))
+        spread = spread_faces(faces_ref[8 * f:8 * f + 8]).reshape(LEVELS, ROWS, LANES)
+        b_ref[f] = (rhs_ref[f] + spread) * inv[None]
+
+    def upward(i, carry):
+        carry = list(carry)
+        for step in range(UNROLL):
+            k = i * UNROLL + step
+            for f in range(2):
+                carry[f] = carry[f] + up_ref[f, k] * b_ref[f, k]
+                y_ref[f, k] = carry[f] * down_ref[f, k]
+        return tuple(carry)
+
+    lax.fori_loop(0, LEVELS // UNROLL, upward, (zero, zero))
+
+    def downward(i, carry):
+        carry = list(carry)
+        for step in range(UNROLL):
+            k = LEVELS - 1 - (i * UNROLL + step)
+            for f in range(2):
+                y_ref[f, k] = y_ref[f, k] + up_ref[f, k] * carry[f]
+                carry[f] = carry[f] + down_ref[f, k] * b_ref[f, k]
+        return tuple(carry)
+
+    lax.fori_loop(0, LEVELS // UNROLL, downward, (zero, zero))
+
+
+def final_kernel(y_ref, up_ref, down_ref, own_ref, p0_ref, p1_ref, p2_ref, p3_ref, w_hbm, t_hbm, out_ref, sem):
     zero = jnp.zeros((ROWS, LANES), F32)
     partners = [p0_ref[...], p1_ref[...], p2_ref[...], p3_ref[...]]
     own = own_ref[...]
@@ -317,40 +396,29 @@
         flows.append((
             (s_below * q - a * z12 * s_above) * scale,
             (s_above * p - a_above * z12 * s_below) * scale,
-            z12,
         ))
-    for f in range(2):
-        spread = spread_faces(faces_ref[8 * f:8 * f + 8]).reshape(LEVELS, ROWS, LANES)
-        b_ref[f] = (rhs_ref[f] + spread) * flows[f][2][None]
-    outs = (w_ref, t_ref)
-
-    def upward(k, carry):
-        new = []
-        for f in range(2):
-            s = carry[f] + up_ref[f, k] * b_ref[f, k]
-            outs[f][k] = s * down_ref[f, k]
-            new.append(s)
-        return tuple(new)
-
-    lax.fori_loop(0, LEVELS, upward, (flows[0][0], flows[1][0]))
-
-    def downward(i, carry):
-        k = LEVELS - 1 - i
-        new = []
-        for f in range(2):
-            outs[f][k] = outs[f][k] + up_ref[f, k] * carry[f]
-            new.append(carry[f] + down_ref[f, k] * b_ref[f, k])
-        return tuple(new)
-
-    lax.fori_loop(0, LEVELS, downward, (flows[0][1], flows[1][1]))
-
-
-def call(kernel, shapes, in_specs, scratch=(), flops=0):
+    chunk = LEVELS // PARTS
+    copies = []
+    for part in range(PARTS):
+        for f, out in enumerate((w_hbm, t_hbm)):
+            for k in range(part * chunk, (part + 1) * chunk):
+                out_ref[f, k] = y_ref[f, k] + (down_ref[f, k] * flows[f][0] + up_ref[f, k] * flows[f][1])
+            levels = pl.ds(part * chunk, chunk)
+            copies.append(pltpu.make_async_copy(
+                out_ref.at[f, levels], out.at[levels], sem.at[2 * part + f]
+            ))
+            copies[-1].start()
+    for copy in copies:
+        copy.wait()
+
+
+def call(kernel, shapes, in_specs, scratch=(), out_specs=None, flops=0):
+    shapes = [s if isinstance(s, jax.ShapeDtypeStruct) else jax.ShapeDtypeStruct(s, F32) for s in shapes]
     return pl.pallas_call(
         kernel,
-        out_shape=[jax.ShapeDtypeStruct(s, F32) for s in shapes],
+        out_shape=shapes,
         in_specs=in_specs,
-        out_specs=[VMEM] * len(shapes),
+        out_specs=out_specs or [VMEM] * len(shapes),
         scratch_shapes=list(scratch),
         compiler_params=PARAMS,
         cost_estimate=pl.CostEstimate(flops=flops, bytes_accessed=flops // 8, transcendentals=0),
@@ -363,25 +431,38 @@
 ):
     strip = (8, CELLS)
     count = 16
-    near, far, own = call(pack_kernel, [strip, strip, (48, CELLS)], [VMEM] * 4)(
-        vertical_section, theta_section, east_wind, eddy_viscosity
-    )
+    part = (LEVELS, ROWS, LANES)
+    block = (2, *part)
+    tile = (ROWS, LANES)
+    state_shape = (STATE, LANES)
+    wide = jax.ShapeDtypeStruct(part, F32)
+    half = jax.ShapeDtypeStruct(part, jnp.bfloat16)
+    (ws, ts, east, visc, wn, tn, north, near, far, own, up, down, rho, dense, coef) = call(
+        prep_kernel,
+        [wide, wide, half, half, wide, wide, half, strip, strip, (48, CELLS), block, block, part, strip, tile],
+        [HBM] * 10,
+        [
+            pltpu.VMEM(part, F32),
+            pltpu.SMEM((LEVELS,), F32),
+            pltpu.SMEM((LEVELS,), F32),
+            pltpu.SMEM((1, ROWS), jnp.int32),
+            pltpu.SemaphoreType.DMA((3,)),
+            pltpu.SemaphoreType.DMA((7 * PARTS,)),
+        ],
+    )(*(
+        pltpu.with_memory_space_constraint(x, pltpu.HBM) for x in (
+            vertical_section, theta_section, east_wind, eddy_viscosity,
+            vertical_now, theta_now, north_wind,
+            density, coupling, cloud_top.reshape(1, ROWS),
+        )
+    ))
     far = lax.ppermute(
         far, "gx", [(i, (i + 1) % count if i % 2 else (i - 1) % count) for i in range(count)]
     )
     near = lax.ppermute(near, "gx", [(i, i ^ 1) for i in range(count)])
-    block = (2, LEVELS, ROWS, LANES)
-    rhs, up, down, sums, dense = call(
-        main_kernel,
-        [block, block, block, (STATE, LANES), strip],
-        [VMEM] * 7 + [SMEM, SMEM, VMEM],
-        [pltpu.VMEM((LEVELS, ROWS, LANES), F32)],
-        flops=16_000_000,
-    )(
-        vertical_now, vertical_section, theta_now, theta_section,
-        east_wind, north_wind, eddy_viscosity, density, coupling, cloud_top,
-    )
-    state_shape = (STATE, LANES)
+    rhs, sums = call(main_kernel, [block, state_shape], [VMEM] * 11, flops=16_000_000)(
+        wn, ws, tn, ts, east, north, visc, rho, up, down, coef
+    )
     state, faces = call(
         edge_kernel, [state_shape, (16, CELLS)], [VMEM] * 5, [pltpu.VMEM((48, CELLS), F32)]
     )(near, far, own, sums, dense)
@@ -390,15 +471,20 @@
         return lax.ppermute(x, "gz", [(i, partner(i)) for i in range(count)])
 
     three, two, one = (swap(state, lambda i, k=k: i ^ k) for k in (3, 2, 1))
+    (y,) = call(
+        local_kernel, [block], [VMEM] * 5, [pltpu.VMEM(block, F32)], flops=4_000_000
+    )(rhs, up, down, faces, state)
     pair, four = call(four_kernel, [state_shape] * 2, [VMEM] * 4)(state, one, two, three)
     four_other = swap(four, lambda i: i ^ 4)
     (eight,) = call(functools.partial(two_kernel, 2), [state_shape], [VMEM] * 2)(four, four_other)
     eight_other = swap(eight, lambda i: (7 - i // 2) * 2 + i % 2)
-    part = (LEVELS, ROWS, LANES)
-    w_next, t_next = call(
-        final_kernel, [part, part], [VMEM] * 9, [pltpu.VMEM(block, F32)]
-    )(rhs, up, down, faces, state, one, pair, four_other, eight_other)
-    return (w_next, t_next)
+    return tuple(call(
+        final_kernel,
+        [part, part],
+        [VMEM] * 8,
+        [pltpu.VMEM(block, F32), pltpu.SemaphoreType.DMA((2 * PARTS,))],
+        [HBM] * 2,
+    )(y, up, down, state, one, pair, four_other, eight_other))
 
 
 def solution(mesh):

time: 44.3 us -> 33.3 us (0.75)
  local copies, waits for them, and re-layouts: 6.74 us -> 0 us
  Pallas kernels: 11.4 us -> 8.11 us
  waiting for transfers between devices: 7.63 us -> 6.94 us
    unnamed x29 -> x0, local copies, waits for them, and re-layouts: 6.74 us -> none
    pallas_call x3 -> x4, Pallas kernels: 10.7 us -> 7.35 us  [the longest x1 2.8 us: shards(): call(main_kernel, [block, state_shape], [VMEM] * 11, flops=16000000)]
    ppermute x5, waiting for transfers between devices: 7.62 us -> 6.93 us  [swap(): return lax.ppermute(x, 'gz', [(i, partner(i)) for i in range(count)])]
  transfers between devices with their start and end apart: 7 -> 7, of which waited for: 4 -> 5; matrix products, arithmetic and copies ran while one was open for 0% -> 0% of each run, Pallas kernels for 19% -> 11%
where the time goes in v2:
time: 33.3 us; the launch traced here: 32.8 us
  starting transfers between devices  17 us (51%)
  Pallas kernels  8.11 us (24%)
  waiting for transfers between devices  6.94 us (21%)
  between operations  0.69 us (2%)
    ppermute x5, starting transfers between devices, swap(): return lax.ppermute(x, 'gz', [(i, partner(i)) for i in range(count)])  12.3 us
    ppermute x5, waiting for transfers between devices, swap(): return lax.ppermute(x, 'gz', [(i, partner(i)) for i in range(count)])  6.93 us
    ppermute x1, starting transfers between devices, shards(): lax.ppermute(far, 'gx', [(i, (i + 1) % count if i % 2 else (i - 1) % coun...  4.67 us
    pallas_call x1, Pallas kernels, shards(): call(main_kernel, [block, state_shape], [VMEM] * 11, flops=16000000)  2.8 us
    pallas_call x1, Pallas kernels, shards(): call(prep_kernel, [wide, wide, half, half, wide, wide, half, strip, strip...  2.75 us
    pallas_call x1, Pallas kernels, shards(): call(final_kernel, [part, part], [VMEM] * 8, [pltpu.VMEM(block, F32), plt...  1.12 us
    pallas_call x1, Pallas kernels, shards(): call(local_kernel, [block], [VMEM] * 5, [pltpu.VMEM(block, F32)], flops=4...  0.69 us
  transfers between devices with their start and end apart: 7, of which 5 were waited for; matrix products, arithmetic and copies ran while one was open for 0% of the time, Pallas kernels for 11%

profile of v2, /device:TPU:2, one launch (start us, length us, event | category | flops | bytes accessed | tf_op | source)
XLA Modules:
  0.0 32.8 jit_solution(12774368597988082853)
XLA Ops:
  0.6 2.7 %shard_map.113 = (f32[40,16,128]{2,1,0:T(8,128)S(1)}, f32[40,16,128]{2,1,0:T(8,128)S(1)}, bf16[40,16,128]{2,1,0:T(8,128)(2,1)S(1)}, bf16[40,16,128]{2,1,0:T(8,12...) custom-call(f32[40,16,128]{2,1,0:T(8,128)} %ws_hbm.1, ...), custom_call_target="tpu_custom_call" | custom-call | tf_op jit(solution)/shard_map/pallas_call | solution.py:440
  3.4 0.1 collective-permute-start
  3.5 4.7 %collective-permute-start.1 = (f32[8,640]{1,0:T(8,128)S(1)}, f32[8,640]{1,0:T(8,128)S(1)}, u32[]{:S(2)}, u32[]{:S(2)}) collective-permute-start(f32[8,640]{1,0:T(8,128)S(1)} %get-tuple-element.36), channel_id=1, source_target_pairs={{0,240},{16,32},{32,16},{48,64},{64,48},{80,96},{96,80},{112,128},... | collective-permute-start | bytes 61448 | tf_op jit(solution)/shard_map/ppermute | solution.py:459
  8.2 2.8 %shard_map.114 = (f32[2,40,16,128]{3,2,1,0:T(8,128)S(1)}, f32[80,128]{1,0:T(8,128)S(1)}) custom-call(f32[40,16,128]{2,1,0:T(8,128)S(1)} %get-tuple-element.23.wn_ref, f32[40,16,128]{2,1,0:T(8,128)S(1)} %get-tuple-element.24.ws_ref, f32[40,16,128]{2,1,0:T(8,128)S(1)} %get-tuple-element.25.tn_ref, f32[40,16,128]{2,1,0:T(8,128)S(1)} %get-tuple-element.26.ts_ref, ...), custom_call_target="tpu_custom_call" | custom-call | flops 16000000 | bytes 2000000 | tf_op jit(solution)/shard_map/pallas_call | solution.py:463
  11.0 0.0 collective-permute-done.near_ref
  11.0 0.0 collective-permute-done.1.far_ref
  11.0 0.3 %shard_map.115 = (f32[80,128]{1,0:T(8,128)S(1)}, f32[16,640]{1,0:T(8,128)S(1)}) custom-call(f32[8,640]{1,0:T(8,128)S(1)} %collective-permute-done.near_ref, f32[8,640]{1,0:T(8,128)S(1)} %collective-permute-done.1.far_ref, f32[48,640]{1,0:T(8,128)S(1)} %get-tuple-element.37.own_ref, f32[80,128]{1,0:T(8,128)S(1)} %get-tuple-element.38.sums_ref, ...), custom_call_target="tpu_custom_call" | custom-call | tf_op jit(solution)/shard_map/pallas_call | solution.py:466
  11.3 2.9 %collective-permute-start.4 = (f32[80,128]{1,0:T(8,128)S(1)}, f32[80,128]{1,0:T(8,128)S(1)}, u32[]{:S(2)}, u32[]{:S(2)}) collective-permute-start(f32[80,128]{1,0:T(8,128)S(1)} %get-tuple-element.41.state_ref.own_ref), channel_id=1, source_target_pairs={{0,3},{1,2},{2,1},{3,0},{4,7},{5,6},{6,5},{7,4},{8,11},{9,10},{10,... | collective-permute-start | bytes 122888 | tf_op jit(solution)/shard_map/ppermute | solution.py:471
  14.2 0.4 %collective-permute-start.3 = (f32[80,128]{1,0:T(8,128)S(1)}, f32[80,128]{1,0:T(8,128)S(1)}, u32[]{:S(2)}, u32[]{:S(2)}) collective-permute-start(f32[80,128]{1,0:T(8,128)S(1)} %get-tuple-element.41.state_ref.own_ref), channel_id=1, source_target_pairs={{0,2},{1,3},{2,0},{3,1},{4,6},{5,7},{6,4},{7,5},{8,10},{9,11},{10,... | collective-permute-start | bytes 122888 | tf_op jit(solution)/shard_map/ppermute | solution.py:471
  14.6 0.3 %collective-permute-start.2 = (f32[80,128]{1,0:T(8,128)S(1)}, f32[80,128]{1,0:T(8,128)S(1)}, u32[]{:S(2)}, u32[]{:S(2)}) collective-permute-start(f32[80,128]{1,0:T(8,128)S(1)} %get-tuple-element.41.state_ref.own_ref), channel_id=1, source_target_pairs={{0,1},{1,0},{2,3},{3,2},{4,5},{5,4},{6,7},{7,6},{8,9},{9,8},{10,11... | collective-permute-start | bytes 122888 | tf_op jit(solution)/shard_map/ppermute | solution.py:471
  14.9 1.4 %collective-permute-done.4.three_ref = f32[80,128]{1,0:T(8,128)S(1)} collective-permute-done((f32[80,128]{1,0:T(8,128)S(1)}, f32[80,128]{1,0:T(8,128)S(1)}, u32[]{:S(2)}, u32[]{:S(2)}) %collective-permute-start.4) | collective-permute-done | bytes 40992 | tf_op jit(solution)/shard_map/ppermute | solution.py:471
  16.3 2.2 %collective-permute-done.3.two_ref = f32[80,128]{1,0:T(8,128)S(1)} collective-permute-done((f32[80,128]{1,0:T(8,128)S(1)}, f32[80,128]{1,0:T(8,128)S(1)}, u32[]{:S(2)}, u32[]{:S(2)}) %collective-permute-start.3) | collective-permute-done | bytes 40992 | tf_op jit(solution)/shard_map/ppermute | solution.py:471
  18.5 0.1 collective-permute-done.2.one_ref.p0_ref
  18.6 0.3 shard_map.117
  18.9 3.1 %collective-permute-start.5 = (f32[80,128]{1,0:T(8,128)S(1)}, f32[80,128]{1,0:T(8,128)S(1)}, u32[]{:S(2)}, u32[]{:S(2)}) collective-permute-start(f32[80,128]{1,0:T(8,128)S(1)} %get-tuple-element.43.own_ref), channel_id=1, source_target_pairs={{0,4},{1,5},{2,6},{3,7},{4,0},{5,1},{6,2},{7,3},{8,12},{9,13},{10,... | collective-permute-start | bytes 122888 | tf_op jit(solution)/shard_map/ppermute | solution.py:471
  22.0 2.0 %collective-permute-done.5.other_ref.p2_ref = f32[80,128]{1,0:T(8,128)S(1)} collective-permute-done((f32[80,128]{1,0:T(8,128)S(1)}, f32[80,128]{1,0:T(8,128)S(1)}, u32[]{:S(2)}, u32[]{:S(2)}) %collective-permute-start.5) | collective-permute-done | bytes 40992 | tf_op jit(solution)/shard_map/ppermute | solution.py:471
  23.9 0.1 shard_map.118
  24.1 5.6 %collective-permute-start.6 = (f32[80,128]{1,0:T(8,128)S(1)}, f32[80,128]{1,0:T(8,128)S(1)}, u32[]{:S(2)}, u32[]{:S(2)}) collective-permute-start(f32[80,128]{1,0:T(8,128)S(1)} %shard_map.118), channel_id=1, source_target_pairs={{0,14},{1,15},{2,12},{3,13},{4,10},{5,11},{6,8},{7,9},{8,6},{9,7},... | collective-permute-start | bytes 122888 | tf_op jit(solution)/shard_map/ppermute | solution.py:471
  29.7 0.7 %shard_map.116.y_ref = f32[2,40,16,128]{3,2,1,0:T(8,128)S(1)} custom-call(f32[2,40,16,128]{3,2,1,0:T(8,128)S(1)} %get-tuple-element.34.rhs_ref, f32[2,40,16,128]{3,2,1,0:T(8,128)S(1)} %get-tuple-element.31.up_ref, f32[2,40,16,128]{3,2,1,0:T(8,128)S(1)} %get-tuple-element.32.down_ref, f32[16,640]{1,0:T(8,128)S(1)} %get-tuple-element.40.faces_ref, ...), custom_call_target="tpu_custom_call" | custom-call | flops 4000000 | bytes 500000 | tf_op jit(solution)/shard_map/pallas_call | solution.py:474
  30.4 1.3 %collective-permute-done.6.p3_ref = f32[80,128]{1,0:T(8,128)S(1)} collective-permute-done((f32[80,128]{1,0:T(8,128)S(1)}, f32[80,128]{1,0:T(8,128)S(1)}, u32[]{:S(2)}, u32[]{:S(2)}) %collective-permute-start.6) | collective-permute-done | bytes 40992 | tf_op jit(solution)/shard_map/ppermute | solution.py:471
  31.7 1.1 %shard_map.119 = (f32[40,16,128]{2,1,0:T(8,128)}, f32[40,16,128]{2,1,0:T(8,128)}) custom-call(f32[2,40,16,128]{3,2,1,0:T(8,128)S(1)} %shard_map.116.y_ref, f32[2,40,16,128]{3,2,1,0:T(8,128)S(1)} %get-tuple-element.31.up_ref, f32[2,40,16,128]{3,2,1,0:T(8,128)S(1)} %get-tuple-element.32.down_ref, f32[80,128]{1,0:T(8,128)S(1)} %get-tuple-element.41.state_ref.own_ref, ...), custom_call_target="tpu_custom_call" | custom-call | tf_op jit(solution)/shard_map/pallas_call | solution.py:481
Async XLA Ops:
  3.4 7.6 %collective-permute-start = (f32[8,640]{1,0:T(8,128)S(1)}, f32[8,640]{1,0:T(8,128)S(1)}, u32[]{:S(2)}, u32[]{:S(2)}) collective-permute-start(f32[8,640]{1,0:T(8,128)S(1)} %get-tuple-element.35), channel_id=1, source_target_pairs={{0,16},{16,0},{32,48},{48,32},{64,80},{80,64},{96,112},{112,96},{1... | collective-permute-start | bytes 61448 | tf_op jit(solution)/shard_map/ppermute | solution.py:462
  3.5 7.5 %collective-permute-start.1 = (f32[8,640]{1,0:T(8,128)S(1)}, f32[8,640]{1,0:T(8,128)S(1)}, u32[]{:S(2)}, u32[]{:S(2)}) collective-permute-start(f32[8,640]{1,0:T(8,128)S(1)} %get-tuple-element.36), channel_id=1, source_target_pairs={{0,240},{16,32},{32,16},{48,64},{64,48},{80,96},{96,80},{112,128},... | collective-permute-start | bytes 61448 | tf_op jit(solution)/shard_map/ppermute | solution.py:459
  11.3 5.0 %collective-permute-start.4 = (f32[80,128]{1,0:T(8,128)S(1)}, f32[80,128]{1,0:T(8,128)S(1)}, u32[]{:S(2)}, u32[]{:S(2)}) collective-permute-start(f32[80,128]{1,0:T(8,128)S(1)} %get-tuple-element.41.state_ref.own_ref), channel_id=1, source_target_pairs={{0,3},{1,2},{2,1},{3,0},{4,7},{5,6},{6,5},{7,4},{8,11},{9,10},{10,... | collective-permute-start | bytes 122888 | tf_op jit(solution)/shard_map/ppermute | solution.py:471
  14.2 4.3 %collective-permute-start.3 = (f32[80,128]{1,0:T(8,128)S(1)}, f32[80,128]{1,0:T(8,128)S(1)}, u32[]{:S(2)}, u32[]{:S(2)}) collective-permute-start(f32[80,128]{1,0:T(8,128)S(1)} %get-tuple-element.41.state_ref.own_ref), channel_id=1, source_target_pairs={{0,2},{1,3},{2,0},{3,1},{4,6},{5,7},{6,4},{7,5},{8,10},{9,11},{10,... | collective-permute-start | bytes 122888 | tf_op jit(solution)/shard_map/ppermute | solution.py:471
  14.6 4.0 %collective-permute-start.2 = (f32[80,128]{1,0:T(8,128)S(1)}, f32[80,128]{1,0:T(8,128)S(1)}, u32[]{:S(2)}, u32[]{:S(2)}) collective-permute-start(f32[80,128]{1,0:T(8,128)S(1)} %get-tuple-element.41.state_ref.own_ref), channel_id=1, source_target_pairs={{0,1},{1,0},{2,3},{3,2},{4,5},{5,4},{6,7},{7,6},{8,9},{9,8},{10,11... | collective-permute-start | bytes 122888 | tf_op jit(solution)/shard_map/ppermute | solution.py:471
  18.9 5.1 %collective-permute-start.5 = (f32[80,128]{1,0:T(8,128)S(1)}, f32[80,128]{1,0:T(8,128)S(1)}, u32[]{:S(2)}, u32[]{:S(2)}) collective-permute-start(f32[80,128]{1,0:T(8,128)S(1)} %get-tuple-element.43.own_ref), channel_id=1, source_target_pairs={{0,4},{1,5},{2,6},{3,7},{4,0},{5,1},{6,2},{7,3},{8,12},{9,13},{10,... | collective-permute-start | bytes 122888 | tf_op jit(solution)/shard_map/ppermute | solution.py:471
  24.1 7.6 %collective-permute-start.6 = (f32[80,128]{1,0:T(8,128)S(1)}, f32[80,128]{1,0:T(8,128)S(1)}, u32[]{:S(2)}, u32[]{:S(2)}) collective-permute-start(f32[80,128]{1,0:T(8,128)S(1)} %shard_map.118), channel_id=1, source_target_pairs={{0,14},{1,15},{2,12},{3,13},{4,10},{5,11},{6,8},{7,9},{8,6},{9,7},... | collective-permute-start | bytes 122888 | tf_op jit(solution)/shard_map/ppermute | solution.py:471

commit v3 on v2

--- a/solution.py
+++ b/solution.py
@@ -1,5 +1,3 @@
-import functools
-
 import jax
 import jax.numpy as jnp
 from jax import lax
@@ -15,9 +13,11 @@
 ROWS = 16
 LANES = 128
 CELLS = LEVELS * ROWS
-STATE = 5 * ROWS
+COEF = 8
+STATE = 4 * ROWS + COEF
+PAD = 8
 PARTS = 5
-UNROLL = 4
+UNROLL = 5
 HBM = pl.BlockSpec(memory_space=pltpu.HBM)
 VMEM = pl.BlockSpec(memory_space=pltpu.VMEM)
 SMEM = pl.BlockSpec(memory_space=pltpu.SMEM)
@@ -93,11 +93,11 @@
     return parts[0] + (parts[1] + parts[2])
 
 
-def prep_kernel(
+def pack_kernel(
     ws_hbm, ts_hbm, east_hbm, visc_hbm, wn_hbm, tn_hbm, north_hbm, dens_hbm, coup_hbm, top_hbm,
-    ws_ref, ts_ref, east_ref, visc_ref, wn_ref, tn_ref, north_ref,
-    near_ref, far_ref, own_ref, up_ref, down_ref, rho_ref, dense_ref, coef_ref,
-    packed_ref, dens_ref, coup_ref, top_ref, small_sem, big_sem,
+    ws_ref, ts_ref, east_ref, visc_ref, wn_ref, tn_ref, north_ref, far_ref, near_ref, own_ref,
+    up_ref, down_ref, rho_ref, inv_ref, coef_ref,
+    dens_ref, coup_ref, top_ref, small_sem, sem,
 ):
     small = [
         pltpu.make_async_copy(src, dst, small_sem.at[i])
@@ -105,24 +105,27 @@
             ((dens_hbm, dens_ref), (coup_hbm, coup_ref), (top_hbm, top_ref))
         )
     ]
-    big = []
-    for i, (src, dst) in enumerate((
-        (ws_hbm, ws_ref), (ts_hbm, ts_ref), (east_hbm, east_ref), (visc_hbm, visc_ref),
-        (wn_hbm, wn_ref), (tn_hbm, tn_ref), (north_hbm, north_ref),
-    )):
-        for part in range(PARTS):
-            levels = pl.ds(part * (LEVELS // PARTS), LEVELS // PARTS)
-            big.append(pltpu.make_async_copy(
-                src.at[levels], dst.at[levels], big_sem.at[i * PARTS + part]
-            ))
-    for copy in small + big:
+    for copy in small:
         copy.start()
+    refs = (ws_ref, ts_ref, east_ref, visc_ref)
+    sources = (ws_hbm, ts_hbm, east_hbm, visc_hbm, wn_hbm, tn_hbm, north_hbm)
+    targets = (*refs, wn_ref, tn_ref, north_ref)
+    pairs = [
+        (src, dst.at[:, PAD:PAD + ROWS] if i < 2 else dst) for i, (src, dst) in enumerate(zip(sources, targets))
+    ]
+    for src, dst in zip(sources[:2], targets):
+        pairs.append((src.at[:, ROWS - PAD:], dst.at[:, :PAD]))
+        pairs.append((src.at[:, :PAD], dst.at[:, PAD + ROWS:]))
+    copies = [pltpu.make_async_copy(src, dst, sem.at[i]) for i, (src, dst) in enumerate(pairs)]
+    for copy in copies:
+        copy.start()
+    selects = [lane_selector(lanes) for lanes in strip_selectors()]
+    is_odd = lax.rem(lax.axis_index("gx"), 2) == 1
     for copy in small:
         copy.wait()
 
     first = lax.axis_index("gz") * LEVELS
     tile = (ROWS, LANES)
-    lane = iota(tile, 1)
     row = iota(tile, 0)
     one = jnp.ones(tile, F32)
     top = jnp.zeros(tile, jnp.int32)
@@ -155,6 +158,53 @@
             down_ref[f, j] = v[f]
     inv = [1.0 / n[f] for f in range(2)]
 
+    boost = jnp.where(first <= top, 1.0 + MIXED_BOOST, 1.0)
+    below = jnp.where(first >= 1, 1.0, 0.0)
+    values = []
+    for f in range(2):
+        values += [
+            down_ref[f, 0] * inv[f],
+            inv[f],
+            up_ref[f, LEVELS - 1] * inv[f],
+            boost * (coup_ref[0] * RATIOS[f] * below),
+        ]
+    coef_ref[...] = pack_coef(values)
+    for f in range(2):
+        inv_ref[f] = inv[f]
+    for copy in copies[:4]:
+        copy.wait()
+    left_parts, right_parts = [], []
+    for ref, select in zip(refs, selects):
+        x = ref[:, PAD:PAD + ROWS] if ref.shape[1] > ROWS else ref[...]
+        x = x.reshape(CELLS, LANES)
+        parts = [x]
+        if x.dtype == F32:
+            high = x.astype(jnp.bfloat16)
+            rest = x - high.astype(F32)
+            mid = rest.astype(jnp.bfloat16)
+            parts = [high, mid, (rest - mid.astype(F32)).astype(jnp.bfloat16)]
+        left_parts += [select] * len(parts)
+        right_parts += parts
+    total = lax.dot_general(
+        jnp.concatenate(left_parts, axis=1), jnp.concatenate(right_parts, axis=1),
+        (((1,), (1,)), ((), ())), preferred_element_type=F32,
+    )
+    left, right = total[0:8], total[8:16]
+    far_ref[...] = jnp.where(is_odd, right, left)
+    near_ref[...] = jnp.where(is_odd, left, right)
+    own_ref[...] = total[16:]
+    for copy in copies[4:]:
+        copy.wait()
+
+
+def main_kernel(
+    wn_ref, tn_ref, north_ref, ws_ref, ts_ref, east_ref, visc_ref, up_ref, down_ref, rho_ref, inv_ref, coef_ref,
+    rhs_ref, sums_ref, dense_ref, packed_ref,
+):
+    tile = (ROWS, LANES)
+    lane = iota(tile, 1)
+    inv = [inv_ref[f] for f in range(2)]
+
     for k in range(LEVELS):
         packed = jnp.where(lane < 16, up_ref[0, k] * inv[0], down_ref[0, k] * inv[0])
         packed = jnp.where(lane < 32, packed, up_ref[1, k] * inv[1])
@@ -164,43 +214,6 @@
         lane_selector([0, 16, 32, 48, 64, -1, -1, -1]), packed_ref[...].reshape(CELLS, LANES)
     )
 
-    coef = jnp.zeros(tile, F32)
-    boost = jnp.where(first <= top, 1.0 + MIXED_BOOST, 1.0)
-    below = jnp.where(first >= 1, 1.0, 0.0)
-    for f in range(2):
-        values = (
-            down_ref[f, 0] * inv[f],
-            inv[f],
-            up_ref[f, LEVELS - 1] * inv[f],
-            boost * (coup_ref[0] * RATIOS[f] * below),
-        )
-        for i, value in enumerate(values):
-            coef = jnp.where(lane == 4 * f + i, value, coef)
-    coef_ref[...] = coef
-
-    for copy in big[:4 * PARTS]:
-        copy.wait()
-    odd = lax.rem(lax.axis_index("gx"), 2)
-    rows = strip_selectors()
-    total = None
-    for ref, lanes in zip((ws_ref, ts_ref, east_ref, visc_ref), rows):
-        part = pick_lanes(lane_selector(lanes), ref[...].reshape(CELLS, LANES))
-        total = part if total is None else total + part
-    left, right = total[0:8], total[8:16]
-    is_odd = odd == 1
-    near_ref[...] = jnp.where(is_odd, left, right)
-    far_ref[...] = jnp.where(is_odd, right, left)
-    own_ref[...] = total[16:]
-    for copy in big[4 * PARTS:]:
-        copy.wait()
-
-
-def main_kernel(
-    wn_ref, ws_ref, tn_ref, ts_ref, east_ref, north_ref, visc_ref, rho_ref, up_ref, down_ref, coef_ref,
-    rhs_ref, sums_ref,
-):
-    tile = (ROWS, LANES)
-    lane = iota(tile, 1)
     inside = (lane >= 2) & (lane <= LANES - 4)
 
     def level(k, carry):
@@ -214,10 +227,10 @@
         weight = rho_ref[k]
         out = []
         for f, (now_ref, sec_ref) in enumerate(((wn_ref, ws_ref), (tn_ref, ts_ref))):
-            q = sec_ref[k]
+            q = sec_ref[k, PAD:PAD + ROWS]
             qx = [q if s == 0 else pltpu.roll(q, (-s) % LANES, 1) for s in range(-2, 4)]
             fx = flux(qx, east_sum, visc_x)
-            qy = [q if s == 0 else pltpu.roll(q, (-s) % ROWS, 0) for s in range(-2, 4)]
+            qy = [q if s == 0 else sec_ref[k, PAD + s:PAD + s + ROWS] for s in range(-2, 4)]
             fy = flux(qy, north_sum, visc_y)
             change = (pltpu.roll(fx, 1, 1) - fx) + (pltpu.roll(fy, 1, 0) - fy)
             explicit = now_ref[k] * (1.0 / 3.0) + (q + change) * (2.0 / 3.0)
@@ -234,12 +247,10 @@
 
     zero = jnp.zeros(tile, F32)
     sums = lax.fori_loop(0, LEVELS // UNROLL, levels, (zero,) * 4)
-    coef = coef_ref[...]
-    for f in range(2):
-        inv = jnp.broadcast_to(coef[:, 4 * f + 1:4 * f + 2], tile)
-        sums_ref[f * ROWS:(f + 1) * ROWS] = sums[2 * f] * inv
-        sums_ref[(2 + f) * ROWS:(3 + f) * ROWS] = sums[2 * f + 1] * inv
-    sums_ref[4 * ROWS:] = coef
+    for f in range(2):
+        sums_ref[f * ROWS:(f + 1) * ROWS] = sums[2 * f] * inv[f]
+        sums_ref[(2 + f) * ROWS:(3 + f) * ROWS] = sums[2 * f + 1] * inv[f]
+    sums_ref[4 * ROWS:] = coef_ref[...]
 
 
 def face_spread():
@@ -256,7 +267,7 @@
     )
 
 
-def edge_kernel(near_ref, far_ref, own_ref, sums_ref, dense_ref, state_ref, faces_ref, strip_ref):
+def edge_kernel(far_ref, near_ref, own_ref, sums_ref, dense_ref, state_ref, faces_ref, strip_ref):
     odd = lax.rem(lax.axis_index("gx"), 2) == 1
     near, far = near_ref[...], far_ref[...]
     left = jnp.where(odd, near, far)
@@ -291,18 +302,32 @@
     state_ref[4 * ROWS:] = sums_ref[4 * ROWS:]
 
 
+def spread_coef(coef, f, i):
+    at = 4 * f + i
+    return jnp.concatenate([
+        jnp.broadcast_to(coef[:, at:at + 1], (COEF, LANES)),
+        jnp.broadcast_to(coef[:, at + LANES // 2:at + LANES // 2 + 1], (COEF, LANES)),
+    ], axis=0)
+
+
+def pack_coef(values):
+    lane = iota((COEF, LANES), 1)
+    coef = jnp.zeros((COEF, LANES), F32)
+    for i, value in enumerate(values):
+        coef = jnp.where(lane == i, value[:COEF], coef)
+        coef = jnp.where(lane == i + LANES // 2, value[COEF:], coef)
+    return coef
+
+
 def unpack(state, f):
     yf = state[f * ROWS:(f + 1) * ROWS]
     yl = state[(2 + f) * ROWS:(3 + f) * ROWS]
     coef = state[4 * ROWS:]
-    z = [jnp.broadcast_to(coef[:, 4 * f + i:4 * f + i + 1], (ROWS, LANES)) for i in range(4)]
-    return (yf, yl, *z)
+    return (yf, yl, *(spread_coef(coef, f, i) for i in range(4)))
 
 
 def join(lower, upper):
-    lane = iota((ROWS, LANES), 1)
-    firsts, lasts = [], []
-    coef = jnp.zeros((ROWS, LANES), F32)
+    firsts, lasts, values = [], [], []
     for f in range(2):
         yf_a, yl_a, z11_a, z12_a, z22_a, a_a = unpack(lower, f)
         yf_b, yl_b, z11_b, z12_b, z22_b, a_b = unpack(upper, f)
@@ -310,10 +335,8 @@
         flow = g * (yl_a - yf_b)
         firsts.append(yf_a - z12_a * flow)
         lasts.append(yl_b + z12_b * flow)
-        values = (z11_a - z12_a * z12_a * g, z12_a * g * z12_b, z22_b - z12_b * z12_b * g, a_a)
-        for i, value in enumerate(values):
-            coef = jnp.where(lane == 4 * f + i, value, coef)
-    return jnp.concatenate(firsts + lasts + [coef], axis=0)
+        values += [z11_a - z12_a * z12_a * g, z12_a * g * z12_b, z22_b - z12_b * z12_b * g, a_a]
+    return jnp.concatenate(firsts + lasts + [pack_coef(values)], axis=0)
 
 
 def bit(place):
@@ -332,15 +355,17 @@
     total_ref[...] = join_pair(mine, other, 1)
 
 
-def two_kernel(place, own_ref, other_ref, total_ref):
-    total_ref[...] = join_pair(own_ref[...], other_ref[...], place)
+def half_kernel(own_ref, other_ref, send_ref):
+    total = join_pair(own_ref[...], other_ref[...], 2)
+    send_ref[:2 * ROWS] = jnp.where(bit(3), total[:2 * ROWS], total[2 * ROWS:4 * ROWS])
+    send_ref[2 * ROWS:] = total[4 * ROWS:]
 
 
 def local_kernel(rhs_ref, up_ref, down_ref, faces_ref, state_ref, y_ref, b_ref):
     zero = jnp.zeros((ROWS, LANES), F32)
     coef = state_ref[4 * ROWS:]
     for f in range(2):
-        inv = jnp.broadcast_to(coef[:, 4 * f + 1:4 * f + 2], (ROWS, LANES))
+        inv = spread_coef(coef, f, 1)
         spread = spread_faces(faces_ref[8 * f:8 * f + 8]).reshape(LEVELS, ROWS, LANES)
         b_ref[f] = (rhs_ref[f] + spread) * inv[None]
 
@@ -369,13 +394,19 @@
 
 def final_kernel(y_ref, up_ref, down_ref, own_ref, p0_ref, p1_ref, p2_ref, p3_ref, w_hbm, t_hbm, out_ref, sem):
     zero = jnp.zeros((ROWS, LANES), F32)
-    partners = [p0_ref[...], p1_ref[...], p2_ref[...], p3_ref[...]]
+    partners = [p0_ref[...], p1_ref[...], p2_ref[...]]
+    half = p3_ref[...]
+    upper = bit(3)
     own = own_ref[...]
     flows = []
     for f in range(2):
-        yf_above, z_above, a_above = zero, zero, zero
-        yl_below, z_below = zero, zero
-        for place in (3, 2, 1, 0):
+        y = half[f * ROWS:(f + 1) * ROWS]
+        z11, z22, a = (
+            spread_coef(half[2 * ROWS:], f, i) for i in (0, 2, 3)
+        )
+        yf_above, z_above, a_above = (jnp.where(upper, zero, x) for x in (y, z11, a))
+        yl_below, z_below = (jnp.where(upper, x, zero) for x in (y, z22))
+        for place in (2, 1, 0):
             yf, yl, z11, z12, z22, a = unpack(partners[place], f)
             below = bit(place)
             g = a_above / (1.0 + a_above * (z_above + z22))
@@ -433,39 +464,48 @@
     count = 16
     part = (LEVELS, ROWS, LANES)
     block = (2, *part)
-    tile = (ROWS, LANES)
     state_shape = (STATE, LANES)
     wide = jax.ShapeDtypeStruct(part, F32)
     half = jax.ShapeDtypeStruct(part, jnp.bfloat16)
-    (ws, ts, east, visc, wn, tn, north, near, far, own, up, down, rho, dense, coef) = call(
-        prep_kernel,
-        [wide, wide, half, half, wide, wide, half, strip, strip, (48, CELLS), block, block, part, strip, tile],
+    tall = jax.ShapeDtypeStruct((LEVELS, ROWS + 2 * PAD, LANES), F32)
+
+    def in_hbm(*arrays):
+        return [pltpu.with_memory_space_constraint(x, pltpu.HBM) for x in arrays]
+
+    tile = (ROWS, LANES)
+    ws, ts, east, visc, wn, tn, north, far, near, own, up, down, rho, inv, coef = call(
+        pack_kernel,
+        [tall, tall, half, half, wide, wide, half, strip, strip, (48, CELLS), block, block, part, (2, *tile), (COEF, LANES)],
         [HBM] * 10,
         [
-            pltpu.VMEM(part, F32),
             pltpu.SMEM((LEVELS,), F32),
             pltpu.SMEM((LEVELS,), F32),
             pltpu.SMEM((1, ROWS), jnp.int32),
             pltpu.SemaphoreType.DMA((3,)),
-            pltpu.SemaphoreType.DMA((7 * PARTS,)),
+            pltpu.SemaphoreType.DMA((11,)),
         ],
-    )(*(
-        pltpu.with_memory_space_constraint(x, pltpu.HBM) for x in (
-            vertical_section, theta_section, east_wind, eddy_viscosity,
-            vertical_now, theta_now, north_wind,
-            density, coupling, cloud_top.reshape(1, ROWS),
-        )
+    )(*in_hbm(
+        vertical_section, theta_section, east_wind, eddy_viscosity, vertical_now, theta_now, north_wind,
+        density, coupling, cloud_top.reshape(1, ROWS),
     ))
     far = lax.ppermute(
         far, "gx", [(i, (i + 1) % count if i % 2 else (i - 1) % count) for i in range(count)]
     )
     near = lax.ppermute(near, "gx", [(i, i ^ 1) for i in range(count)])
-    rhs, sums = call(main_kernel, [block, state_shape], [VMEM] * 11, flops=16_000_000)(
-        wn, ws, tn, ts, east, north, visc, rho, up, down, coef
+    rhs, sums, dense = call(
+        main_kernel,
+        [block, state_shape, strip],
+        [VMEM] * 12,
+        [
+            pltpu.VMEM(part, F32),
+        ],
+        flops=16_000_000,
+    )(
+        wn, tn, north, ws, ts, east, visc, up, down, rho, inv, coef,
     )
     state, faces = call(
         edge_kernel, [state_shape, (16, CELLS)], [VMEM] * 5, [pltpu.VMEM((48, CELLS), F32)]
-    )(near, far, own, sums, dense)
+    )(far, near, own, sums, dense)
 
     def swap(x, partner):
         return lax.ppermute(x, "gz", [(i, partner(i)) for i in range(count)])
@@ -476,8 +516,8 @@
     )(rhs, up, down, faces, state)
     pair, four = call(four_kernel, [state_shape] * 2, [VMEM] * 4)(state, one, two, three)
     four_other = swap(four, lambda i: i ^ 4)
-    (eight,) = call(functools.partial(two_kernel, 2), [state_shape], [VMEM] * 2)(four, four_other)
-    eight_other = swap(eight, lambda i: (7 - i // 2) * 2 + i % 2)
+    (eight,) = call(half_kernel, [(2 * ROWS + COEF, LANES)], [VMEM] * 2)(four, four_other)
+    eight_other = swap(eight, lambda i: (i + 4 if i & 4 else i - 4) % count)
     return tuple(call(
         final_kernel,
         [part, part],

time: 33.3 us -> 31.6 us (0.949); the launches traced: 32.8 us -> 31.5 us
  starting transfers between devices: 17 us -> 16.2 us
  Pallas kernels: 8.11 us -> 7.38 us
    pallas_call x3, Pallas kernels: 5.66 us -> 4.93 us  [the longest x1 2.97 us: shards(): call(main_kernel, [block, state_shape, strip], [VMEM] * 12, [pltpu.VMEM(p...]
    ppermute x1, starting transfers between devices: 4.67 us -> 4.1 us  [shards(): lax.ppermute(far, 'gx', [(i, (i + 1) % count if i % 2 else (i - 1) % coun...]
  transfers between devices with their start and end apart: 7 -> 7, of which waited for: 5 -> 5; matrix products, arithmetic and copies ran while one was open for 0% -> 0% of each run, Pallas kernels for 11% -> 12%
where the time goes in v3:
time: 31.6 us; the launch traced here: 31.5 us
  starting transfers between devices  16.2 us (51%)
  Pallas kernels  7.38 us (23%)
  waiting for transfers between devices  7.25 us (23%)
  between operations  0.7 us (2%)
    ppermute x5, starting transfers between devices, swap(): return lax.ppermute(x, 'gz', [(i, partner(i)) for i in range(count)])  12.1 us
    ppermute x5, waiting for transfers between devices, swap(): return lax.ppermute(x, 'gz', [(i, partner(i)) for i in range(count)])  7.25 us
    ppermute x1, starting transfers between devices, shards(): lax.ppermute(far, 'gx', [(i, (i + 1) % count if i % 2 else (i - 1) % coun...  4.1 us
    pallas_call x1, Pallas kernels, shards(): call(main_kernel, [block, state_shape, strip], [VMEM] * 12, [pltpu.VMEM(p...  2.97 us
    pallas_call x1, Pallas kernels, shards(): call(pack_kernel, [tall, tall, half, half, wide, wide, half, strip, strip...  1.83 us
    pallas_call x1, Pallas kernels, shards(): call(final_kernel, [part, part], [VMEM] * 8, [pltpu.VMEM(block, F32), plt...  1.12 us
    pallas_call x1, Pallas kernels, shards(): call(local_kernel, [block], [VMEM] * 5, [pltpu.VMEM(block, F32)], flops=4...  0.69 us
  transfers between devices with their start and end apart: 7, of which 5 were waited for; matrix products, arithmetic and copies ran while one was open for 0% of the time, Pallas kernels for 12%

profile of v3, /device:TPU:2, one launch (start us, length us, event | category | flops | bytes accessed | tf_op | source)
XLA Modules:
  0.0 31.5 jit_solution(6780565433996261608)
XLA Ops:
  0.6 1.8 %shard_map.113 = (f32[40,32,128]{2,1,0:T(8,128)S(1)}, f32[40,32,128]{2,1,0:T(8,128)S(1)}, bf16[40,16,128]{2,1,0:T(8,128)(2,1)S(1)}, bf16[40,16,128]{2,1,0:T(8,12...) custom-call(f32[40,16,128]{2,1,0:T(8,128)} %ws_hbm.1, ...), custom_call_target="tpu_custom_call" | custom-call | tf_op jit(solution)/shard_map/pallas_call | solution.py:476
  2.5 4.1 %collective-permute-start = (f32[8,640]{1,0:T(8,128)S(1)}, f32[8,640]{1,0:T(8,128)S(1)}, u32[]{:S(2)}, u32[]{:S(2)}) collective-permute-start(f32[8,640]{1,0:T(8,128)S(1)} %get-tuple-element.37), channel_id=1, source_target_pairs={{0,240},{16,32},{32,16},{48,64},{64,48},{80,96},{96,80},{112,128},... | collective-permute-start | bytes 61448 | tf_op jit(solution)/shard_map/ppermute | solution.py:491
  6.6 0.0 collective-permute-start.1
  6.6 3.0 %shard_map.114 = (f32[2,40,16,128]{3,2,1,0:T(8,128)S(1)}, f32[72,128]{1,0:T(8,128)S(1)}, f32[8,640]{1,0:T(8,128)S(1)}) custom-call(f32[40,16,128]{2,1,0:T(8,128)S(1)} %get-tuple-element.24.wn_ref, f32[40,16,128]{2,1,0:T(8,128)S(1)} %get-tuple-element.25.tn_ref, bf16[40,16,128]{2,1,0:T(8,128)(2,1)S(1)} %get-tuple-element.26.north_ref, ...), custom_call_target="tpu_custom_call" | custom-call | flops 16000000 | bytes 2000000 | tf_op jit(solution)/shard_map/pallas_call | solution.py:495
  9.6 0.0 collective-permute-done.far_ref
  9.6 0.0 collective-permute-done.1.near_ref
  9.6 0.3 %shard_map.115 = (f32[72,128]{1,0:T(8,128)S(1)}, f32[16,640]{1,0:T(8,128)S(1)}) custom-call(f32[8,640]{1,0:T(8,128)S(1)} %collective-permute-done.far_ref, f32[8,640]{1,0:T(8,128)S(1)} %collective-permute-done.1.near_ref, f32[48,640]{1,0:T(8,128)S(1)} %get-tuple-element.39.own_ref, f32[72,128]{1,0:T(8,128)S(1)} %get-tuple-element.40.sums_ref, ...), custom_call_target="tpu_custom_call" | custom-call | tf_op jit(solution)/shard_map/pallas_call | solution.py:506
  9.9 2.9 %collective-permute-start.4 = (f32[72,128]{1,0:T(8,128)S(1)}, f32[72,128]{1,0:T(8,128)S(1)}, u32[]{:S(2)}, u32[]{:S(2)}) collective-permute-start(f32[72,128]{1,0:T(8,128)S(1)} %get-tuple-element.43.state_ref.own_ref), channel_id=1, source_target_pairs={{0,3},{1,2},{2,1},{3,0},{4,7},{5,6},{6,5},{7,4},{8,11},{9,10},{10,... | collective-permute-start | bytes 110600 | tf_op jit(solution)/shard_map/ppermute | solution.py:511
  12.8 0.8 %collective-permute-start.3 = (f32[72,128]{1,0:T(8,128)S(1)}, f32[72,128]{1,0:T(8,128)S(1)}, u32[]{:S(2)}, u32[]{:S(2)}) collective-permute-start(f32[72,128]{1,0:T(8,128)S(1)} %get-tuple-element.43.state_ref.own_ref), channel_id=1, source_target_pairs={{0,2},{1,3},{2,0},{3,1},{4,6},{5,7},{6,4},{7,5},{8,10},{9,11},{10,... | collective-permute-start | bytes 110600 | tf_op jit(solution)/shard_map/ppermute | solution.py:511
  13.6 0.0 collective-permute-start.2
  13.6 1.4 %collective-permute-done.4.three_ref = f32[72,128]{1,0:T(8,128)S(1)} collective-permute-done((f32[72,128]{1,0:T(8,128)S(1)}, f32[72,128]{1,0:T(8,128)S(1)}, u32[]{:S(2)}, u32[]{:S(2)}) %collective-permute-start.4) | collective-permute-done | bytes 36896 | tf_op jit(solution)/shard_map/ppermute | solution.py:511
  15.0 1.8 %collective-permute-done.3.two_ref = f32[72,128]{1,0:T(8,128)S(1)} collective-permute-done((f32[72,128]{1,0:T(8,128)S(1)}, f32[72,128]{1,0:T(8,128)S(1)}, u32[]{:S(2)}, u32[]{:S(2)}) %collective-permute-start.3) | collective-permute-done | bytes 36896 | tf_op jit(solution)/shard_map/ppermute | solution.py:511
  16.8 0.8 %collective-permute-done.2.one_ref.p0_ref = f32[72,128]{1,0:T(8,128)S(1)} collective-permute-done((f32[72,128]{1,0:T(8,128)S(1)}, f32[72,128]{1,0:T(8,128)S(1)}, u32[]{:S(2)}, u32[]{:S(2)}) %collective-permute-start.2) | collective-permute-done | bytes 36896 | tf_op jit(solution)/shard_map/ppermute | solution.py:511
  17.5 0.3 shard_map.117
  17.8 2.7 %collective-permute-start.5 = (f32[72,128]{1,0:T(8,128)S(1)}, f32[72,128]{1,0:T(8,128)S(1)}, u32[]{:S(2)}, u32[]{:S(2)}) collective-permute-start(f32[72,128]{1,0:T(8,128)S(1)} %get-tuple-element.45.own_ref), channel_id=1, source_target_pairs={{0,4},{1,5},{2,6},{3,7},{4,0},{5,1},{6,2},{7,3},{8,12},{9,13},{10,... | collective-permute-start | bytes 110600 | tf_op jit(solution)/shard_map/ppermute | solution.py:511
  20.5 2.2 %collective-permute-done.5.other_ref.p2_ref = f32[72,128]{1,0:T(8,128)S(1)} collective-permute-done((f32[72,128]{1,0:T(8,128)S(1)}, f32[72,128]{1,0:T(8,128)S(1)}, u32[]{:S(2)}, u32[]{:S(2)}) %collective-permute-start.5) | collective-permute-done | bytes 36896 | tf_op jit(solution)/shard_map/ppermute | solution.py:511
  22.8 0.1 shard_map.118
  22.9 5.7 %collective-permute-start.6 = (f32[40,128]{1,0:T(8,128)S(1)}, f32[40,128]{1,0:T(8,128)S(1)}, u32[]{:S(2)}, u32[]{:S(2)}) collective-permute-start(f32[40,128]{1,0:T(8,128)S(1)} %shard_map.118), channel_id=1, source_target_pairs={{0,12},{1,13},{2,14},{3,15},{4,8},{5,9},{6,10},{7,11},{8,4},{9,5},... | collective-permute-start | bytes 61448 | tf_op jit(solution)/shard_map/ppermute | solution.py:511
  28.6 0.7 %shard_map.116.y_ref = f32[2,40,16,128]{3,2,1,0:T(8,128)S(1)} custom-call(f32[2,40,16,128]{3,2,1,0:T(8,128)S(1)} %get-tuple-element.36.rhs_ref, f32[2,40,16,128]{3,2,1,0:T(8,128)S(1)} %get-tuple-element.31.up_ref, f32[2,40,16,128]{3,2,1,0:T(8,128)S(1)} %get-tuple-element.32.down_ref, f32[16,640]{1,0:T(8,128)S(1)} %get-tuple-element.42.faces_ref, ...), custom_call_target="tpu_custom_call" | custom-call | flops 4000000 | bytes 500000 | tf_op jit(solution)/shard_map/pallas_call | solution.py:514
  29.3 1.1 %collective-permute-done.6.p3_ref = f32[40,128]{1,0:T(8,128)S(1)} collective-permute-done((f32[40,128]{1,0:T(8,128)S(1)}, f32[40,128]{1,0:T(8,128)S(1)}, u32[]{:S(2)}, u32[]{:S(2)}) %collective-permute-start.6) | collective-permute-done | bytes 20512 | tf_op jit(solution)/shard_map/ppermute | solution.py:511
  30.4 1.1 %shard_map.119 = (f32[40,16,128]{2,1,0:T(8,128)}, f32[40,16,128]{2,1,0:T(8,128)}) custom-call(f32[2,40,16,128]{3,2,1,0:T(8,128)S(1)} %shard_map.116.y_ref, f32[2,40,16,128]{3,2,1,0:T(8,128)S(1)} %get-tuple-element.31.up_ref, f32[2,40,16,128]{3,2,1,0:T(8,128)S(1)} %get-tuple-element.32.down_ref, f32[72,128]{1,0:T(8,128)S(1)} %get-tuple-element.43.state_ref.own_ref, ...), custom_call_target="tpu_custom_call" | custom-call | tf_op jit(solution)/shard_map/pallas_call | solution.py:521
Async XLA Ops:
  2.5 7.1 %collective-permute-start = (f32[8,640]{1,0:T(8,128)S(1)}, f32[8,640]{1,0:T(8,128)S(1)}, u32[]{:S(2)}, u32[]{:S(2)}) collective-permute-start(f32[8,640]{1,0:T(8,128)S(1)} %get-tuple-element.37), channel_id=1, source_target_pairs={{0,240},{16,32},{32,16},{48,64},{64,48},{80,96},{96,80},{112,128},... | collective-permute-start | bytes 61448 | tf_op jit(solution)/shard_map/ppermute | solution.py:491
  6.6 3.0 %collective-permute-start.1 = (f32[8,640]{1,0:T(8,128)S(1)}, f32[8,640]{1,0:T(8,128)S(1)}, u32[]{:S(2)}, u32[]{:S(2)}) collective-permute-start(f32[8,640]{1,0:T(8,128)S(1)} %get-tuple-element.38), channel_id=1, source_target_pairs={{0,16},{16,0},{32,48},{48,32},{64,80},{80,64},{96,112},{112,96},{1... | collective-permute-start | bytes 61448 | tf_op jit(solution)/shard_map/ppermute | solution.py:494
  9.9 5.0 %collective-permute-start.4 = (f32[72,128]{1,0:T(8,128)S(1)}, f32[72,128]{1,0:T(8,128)S(1)}, u32[]{:S(2)}, u32[]{:S(2)}) collective-permute-start(f32[72,128]{1,0:T(8,128)S(1)} %get-tuple-element.43.state_ref.own_ref), channel_id=1, source_target_pairs={{0,3},{1,2},{2,1},{3,0},{4,7},{5,6},{6,5},{7,4},{8,11},{9,10},{10,... | collective-permute-start | bytes 110600 | tf_op jit(solution)/shard_map/ppermute | solution.py:511
  12.8 4.0 %collective-permute-start.3 = (f32[72,128]{1,0:T(8,128)S(1)}, f32[72,128]{1,0:T(8,128)S(1)}, u32[]{:S(2)}, u32[]{:S(2)}) collective-permute-start(f32[72,128]{1,0:T(8,128)S(1)} %get-tuple-element.43.state_ref.own_ref), channel_id=1, source_target_pairs={{0,2},{1,3},{2,0},{3,1},{4,6},{5,7},{6,4},{7,5},{8,10},{9,11},{10,... | collective-permute-start | bytes 110600 | tf_op jit(solution)/shard_map/ppermute | solution.py:511
  13.6 4.0 %collective-permute-start.2 = (f32[72,128]{1,0:T(8,128)S(1)}, f32[72,128]{1,0:T(8,128)S(1)}, u32[]{:S(2)}, u32[]{:S(2)}) collective-permute-start(f32[72,128]{1,0:T(8,128)S(1)} %get-tuple-element.43.state_ref.own_ref), channel_id=1, source_target_pairs={{0,1},{1,0},{2,3},{3,2},{4,5},{5,4},{6,7},{7,6},{8,9},{9,8},{10,11... | collective-permute-start | bytes 110600 | tf_op jit(solution)/shard_map/ppermute | solution.py:511
  17.8 4.9 %collective-permute-start.5 = (f32[72,128]{1,0:T(8,128)S(1)}, f32[72,128]{1,0:T(8,128)S(1)}, u32[]{:S(2)}, u32[]{:S(2)}) collective-permute-start(f32[72,128]{1,0:T(8,128)S(1)} %get-tuple-element.45.own_ref), channel_id=1, source_target_pairs={{0,4},{1,5},{2,6},{3,7},{4,0},{5,1},{6,2},{7,3},{8,12},{9,13},{10,... | collective-permute-start | bytes 110600 | tf_op jit(solution)/shard_map/ppermute | solution.py:511
  22.9 7.5 %collective-permute-start.6 = (f32[40,128]{1,0:T(8,128)S(1)}, f32[40,128]{1,0:T(8,128)S(1)}, u32[]{:S(2)}, u32[]{:S(2)}) collective-permute-start(f32[40,128]{1,0:T(8,128)S(1)} %shard_map.118), channel_id=1, source_target_pairs={{0,12},{1,13},{2,14},{3,15},{4,8},{5,9},{6,10},{7,11},{8,4},{9,5},... | collective-permute-start | bytes 61448 | tf_op jit(solution)/shard_map/ppermute | solution.py:511

commit v4 on v3

--- a/solution.py
+++ b/solution.py
@@ -16,8 +16,9 @@
 COEF = 8
 STATE = 4 * ROWS + COEF
 PAD = 8
-PARTS = 5
-UNROLL = 5
+FAR_GROUP = (5, 4, 7, 6, 1, 0, 3, 2)
+PARTS = 2
+UNROLL = 8
 HBM = pl.BlockSpec(memory_space=pltpu.HBM)
 VMEM = pl.BlockSpec(memory_space=pltpu.VMEM)
 SMEM = pl.BlockSpec(memory_space=pltpu.SMEM)
@@ -37,13 +38,35 @@
     return jnp.concatenate([high, mid, low], axis=axis)
 
 
+MEAN = (1.0, -8.0, 37.0, 37.0, -8.0, 1.0)
+SKEW = (1.0, -5.0, 10.0, -10.0, 5.0, -1.0)
+STEP = (0.0, 0.0, 1.0, -1.0, 0.0, 0.0)
+
+
+def face_flux(mean, skew, step, speed_sum, mixing_sum):
+    speed = speed_sum * (0.5 * COURANT / 60.0)
+    return speed * mean + jnp.abs(speed) * skew + (0.5 * mixing_sum) * step
+
+
 def flux(qs, speed_sum, mixing_sum):
     qm2, qm1, q0, q1, q2, q3 = qs
-    speed = speed_sum * (0.5 * COURANT / 60.0)
     step = q0 - q1
     mean = (qm2 + q3) - 8.0 * (qm1 + q2) + 37.0 * (q0 + q1)
     skew = (qm2 - q3) - 5.0 * (qm1 - q2) + 10.0 * step
-    return speed * mean + jnp.abs(speed) * skew + (0.5 * mixing_sum) * step
+    return face_flux(mean, skew, step, speed_sum, mixing_sum)
+
+
+def stencil(coefs, first):
+    offset = iota((LANES, LANES), 0) - iota((LANES, LANES), 1) - first
+    out = jnp.zeros((LANES, LANES), F32)
+    for s, coef in enumerate(coefs):
+        if coef:
+            out = jnp.where(offset == s, coef, out)
+    return out
+
+
+def dot(x, y):
+    return lax.dot_general(x, y, (((1,), (0,)), ((), ())), preferred_element_type=F32)
 
 
 def strip_selectors():
@@ -95,7 +118,7 @@
 
 def pack_kernel(
     ws_hbm, ts_hbm, east_hbm, visc_hbm, wn_hbm, tn_hbm, north_hbm, dens_hbm, coup_hbm, top_hbm,
-    ws_ref, ts_ref, east_ref, visc_ref, wn_ref, tn_ref, north_ref, far_ref, near_ref, own_ref,
+    ws_ref, ts_ref, east_ref, visc_ref, wn_ref, tn_ref, north_ref, parts_ref, far_ref, near_ref, own_ref,
     up_ref, down_ref, rho_ref, inv_ref, coef_ref,
     dens_ref, coup_ref, top_ref, small_sem, sem,
 ):
@@ -174,7 +197,7 @@
     for copy in copies[:4]:
         copy.wait()
     left_parts, right_parts = [], []
-    for ref, select in zip(refs, selects):
+    for index, (ref, select) in enumerate(zip(refs, selects)):
         x = ref[:, PAD:PAD + ROWS] if ref.shape[1] > ROWS else ref[...]
         x = x.reshape(CELLS, LANES)
         parts = [x]
@@ -183,6 +206,8 @@
             rest = x - high.astype(F32)
             mid = rest.astype(jnp.bfloat16)
             parts = [high, mid, (rest - mid.astype(F32)).astype(jnp.bfloat16)]
+            for j, value in enumerate(parts):
+                parts_ref[index, :, j * LANES:(j + 1) * LANES] = value
         left_parts += [select] * len(parts)
         right_parts += parts
     total = lax.dot_general(
@@ -198,8 +223,9 @@
 
 
 def main_kernel(
-    wn_ref, tn_ref, north_ref, ws_ref, ts_ref, east_ref, visc_ref, up_ref, down_ref, rho_ref, inv_ref, coef_ref,
-    rhs_ref, sums_ref, dense_ref, packed_ref,
+    wn_ref, tn_ref, north_ref, ws_ref, ts_ref, east_ref, visc_ref, parts_ref,
+    up_ref, down_ref, rho_ref, inv_ref, coef_ref,
+    rhs_ref, sums_ref, dense_ref, packed_ref, face_ref, stencil_ref,
 ):
     tile = (ROWS, LANES)
     lane = iota(tile, 1)
@@ -214,26 +240,34 @@
         lane_selector([0, 16, 32, 48, 64, -1, -1, -1]), packed_ref[...].reshape(CELLS, LANES)
     )
 
-    inside = (lane >= 2) & (lane <= LANES - 4)
+    column = iota((LANES, LANES), 1)
+    pair = jnp.where((column >= 2) & (column <= LANES - 4), stencil((1.0, 1.0), 0), 0.0).astype(jnp.bfloat16)
+    row, column = iota((LANES, LANES), 0), iota((LANES, LANES), 1)
+    near = (row == column) | ((row // ROWS == column // ROWS) & (lax.rem(row + 1, ROWS) == lax.rem(column, ROWS)))
+    pair_y = jnp.where(near, 1.0, 0.0).astype(jnp.bfloat16)
+    chunk = LANES // ROWS
+    face_ref[0] = dot(east_ref[...].reshape(CELLS, LANES), pair).reshape(LEVELS, ROWS, LANES)
+    face_ref[1] = dot(visc_ref[...].reshape(CELLS, LANES), pair).reshape(LEVELS, ROWS, LANES)
+    for i, ref in enumerate((north_ref, visc_ref)):
+        for k in range(0, LEVELS, chunk):
+            x = ref[k:k + chunk].reshape(LANES, LANES)
+            face_ref[2 + i, k:k + chunk] = dot(pair_y, x).reshape(chunk, ROWS, LANES)
+    weights = jnp.concatenate([stencil(c, -2) for c in (MEAN, SKEW, STEP)], axis=1).astype(jnp.bfloat16)
+    weights = jnp.concatenate([weights] * 3, axis=0)
+    for f in range(2):
+        product = dot(parts_ref[f], weights)
+        for j in range(3):
+            stencil_ref[f, j] = product[:, j * LANES:(j + 1) * LANES].reshape(LEVELS, ROWS, LANES)
 
     def level(k, carry):
-        east = east_ref[k].astype(F32)
-        north = north_ref[k].astype(F32)
-        visc = visc_ref[k].astype(F32)
-        east_sum = jnp.where(inside, east + pltpu.roll(east, LANES - 1, 1), 0.0)
-        visc_x = jnp.where(inside, visc + pltpu.roll(visc, LANES - 1, 1), 0.0)
-        north_sum = north + pltpu.roll(north, ROWS - 1, 0)
-        visc_y = visc + pltpu.roll(visc, ROWS - 1, 0)
         weight = rho_ref[k]
         out = []
         for f, (now_ref, sec_ref) in enumerate(((wn_ref, ws_ref), (tn_ref, ts_ref))):
-            q = sec_ref[k, PAD:PAD + ROWS]
-            qx = [q if s == 0 else pltpu.roll(q, (-s) % LANES, 1) for s in range(-2, 4)]
-            fx = flux(qx, east_sum, visc_x)
-            qy = [q if s == 0 else sec_ref[k, PAD + s:PAD + s + ROWS] for s in range(-2, 4)]
-            fy = flux(qy, north_sum, visc_y)
+            fx = face_flux(*(stencil_ref[f, j, k] for j in range(3)), face_ref[0, k], face_ref[1, k])
+            qy = [sec_ref[k, PAD + s:PAD + s + ROWS] for s in range(-2, 4)]
+            fy = flux(qy, face_ref[2, k], face_ref[3, k])
             change = (pltpu.roll(fx, 1, 1) - fx) + (pltpu.roll(fy, 1, 0) - fy)
-            explicit = now_ref[k] * (1.0 / 3.0) + (q + change) * (2.0 / 3.0)
+            explicit = now_ref[k] * (1.0 / 3.0) + (qy[2] + change) * (2.0 / 3.0)
             b = explicit * weight
             rhs_ref[f, k] = b
             out.append(carry[2 * f] + down_ref[f, k] * b)
@@ -289,16 +323,16 @@
             at = 16 * f + 8 * side
             qs = [strip_ref[at + s:at + s + 3] for s in range(6)]
             faces_ref[8 * f + 3 * side:8 * f + 3 * side + 3] = flux(qs, speed, mixing) * weight
-    for f in range(2):
-        faces = faces_ref[8 * f:8 * f + 8]
-        for part in range(2):
-            product = faces * dense_ref[2 * f + part:2 * f + part + 1]
+    folds = []
+    for part in range(2):
+        for f in range(2):
+            product = faces_ref[8 * f:8 * f + 8] * dense_ref[2 * f + 1 - part:2 * f + 2 - part]
             folded = product[:, :LANES]
             for i in range(1, CELLS // LANES):
                 folded = folded + product[:, i * LANES:(i + 1) * LANES]
-            total = jnp.sum(spread_faces(folded).reshape(LANES // ROWS, ROWS, LANES), axis=0)
-            at = (2 * (1 - part) + f) * ROWS
-            state_ref[at:at + ROWS] = sums_ref[at:at + ROWS] + total
+            folds.append(folded)
+    total = spread_faces(jnp.concatenate(folds, axis=1)).reshape(4, LANES // ROWS, ROWS, LANES)
+    state_ref[:4 * ROWS] = sums_ref[:4 * ROWS] + jnp.sum(total, axis=1).reshape(4 * ROWS, LANES)
     state_ref[4 * ROWS:] = sums_ref[4 * ROWS:]
 
 
@@ -327,16 +361,15 @@
 
 
 def join(lower, upper):
-    firsts, lasts, values = [], [], []
-    for f in range(2):
-        yf_a, yl_a, z11_a, z12_a, z22_a, a_a = unpack(lower, f)
-        yf_b, yl_b, z11_b, z12_b, z22_b, a_b = unpack(upper, f)
-        g = a_b / (1.0 + a_b * (z22_a + z11_b))
-        flow = g * (yl_a - yf_b)
-        firsts.append(yf_a - z12_a * flow)
-        lasts.append(yl_b + z12_b * flow)
-        values += [z11_a - z12_a * z12_a * g, z12_a * g * z12_b, z22_b - z12_b * z12_b * g, a_a]
-    return jnp.concatenate(firsts + lasts + [pack_coef(values)], axis=0)
+    yf_a, yl_a, z11_a, z12_a, z22_a, a_a = lower
+    yf_b, yl_b, z11_b, z12_b, z22_b, a_b = upper
+    g = a_b / (1.0 + a_b * (z22_a + z11_b))
+    flow = g * (yl_a - yf_b)
+    step_a, step_b = z12_a * g, z12_b * g
+    return (
+        yf_a - z12_a * flow, yl_b + z12_b * flow,
+        z11_a - z12_a * step_a, z12_a * step_b, z22_b - z12_b * step_b, a_a,
+    )
 
 
 def bit(place):
@@ -345,23 +378,47 @@
 
 def join_pair(own, other, place):
     high = bit(place)
-    return join(jnp.where(high, other, own), jnp.where(high, own, other))
+    lower = tuple(jnp.where(high, y, x) for x, y in zip(own, other))
+    upper = tuple(jnp.where(high, x, y) for x, y in zip(own, other))
+    return join(lower, upper)
+
+
+def store(state_ref, blocks):
+    values = []
+    for f, (yf, yl, *coefs) in enumerate(blocks):
+        state_ref[f * ROWS:(f + 1) * ROWS] = yf
+        state_ref[(2 + f) * ROWS:(3 + f) * ROWS] = yl
+        values += coefs
+    state_ref[4 * ROWS:] = pack_coef(values)
 
 
 def four_kernel(own_ref, one_ref, two_ref, three_ref, pair_ref, total_ref):
-    mine = join_pair(own_ref[...], one_ref[...], 0)
-    other = join_pair(two_ref[...], three_ref[...], 0)
-    pair_ref[...] = other
-    total_ref[...] = join_pair(mine, other, 1)
-
-
-def half_kernel(own_ref, other_ref, send_ref):
-    total = join_pair(own_ref[...], other_ref[...], 2)
-    send_ref[:2 * ROWS] = jnp.where(bit(3), total[:2 * ROWS], total[2 * ROWS:4 * ROWS])
-    send_ref[2 * ROWS:] = total[4 * ROWS:]
-
-
-def local_kernel(rhs_ref, up_ref, down_ref, faces_ref, state_ref, y_ref, b_ref):
+    pairs, totals = [], []
+    for f in range(2):
+        own, one, two, three = (unpack(ref[...], f) for ref in (own_ref, one_ref, two_ref, three_ref))
+        pairs.append(join_pair(two, three, 0))
+        totals.append(join_pair(join_pair(own, one, 0), pairs[f], 1))
+    store(total_ref, totals)
+    store(pair_ref, pairs)
+
+
+def local_kernel(
+    rhs_ref, up_ref, down_ref, faces_ref, state_ref, one_ref, pair_ref, y_ref, above_ref, below_ref, b_ref
+):
+    aboves, belows = [], []
+    for f in range(2):
+        one, pair = unpack(one_ref[...], f), unpack(pair_ref[...], f)
+        near, outer = bit(0), bit(1)
+        both = join(one, pair)
+        aboves.append(tuple(
+            jnp.where(near, y, jnp.where(outer, x, z)) for x, y, z in zip(one, pair, both)
+        ))
+        both = join(pair, one)
+        belows.append(tuple(
+            jnp.where(near, jnp.where(outer, z, x), y) for x, y, z in zip(one, pair, both)
+        ))
+    store(above_ref, aboves)
+    store(below_ref, belows)
     zero = jnp.zeros((ROWS, LANES), F32)
     coef = state_ref[4 * ROWS:]
     for f in range(2):
@@ -392,32 +449,48 @@
     lax.fori_loop(0, LEVELS // UNROLL, downward, (zero, zero))
 
 
-def final_kernel(y_ref, up_ref, down_ref, own_ref, p0_ref, p1_ref, p2_ref, p3_ref, w_hbm, t_hbm, out_ref, sem):
+def above(chain, block, here):
+    y, z, a = chain
+    yf, yl, z11, z12, z22, a_block = block
+    g = a / (1.0 + a * (z + z22))
+    new = (yf + z12 * (g * (y - yl)), z11 - z12 * z12 * g, a_block)
+    return tuple(jnp.where(here, x, old) for x, old in zip(new, chain))
+
+
+def below(chain, block, here):
+    y, z = chain
+    yf, yl, z11, z12, z22, a = block
+    g = a / (1.0 + a * (z + z11))
+    new = (yl + z12 * (g * (y - yf)), z22 - z12 * z12 * g)
+    return tuple(jnp.where(here, x, old) for x, old in zip(new, chain))
+
+
+def final_kernel(
+    y_ref, up_ref, down_ref, own_ref, above_ref, below_ref, a_ref, b_ref, c_ref, w_hbm, t_hbm, out_ref, sem
+):
     zero = jnp.zeros((ROWS, LANES), F32)
-    partners = [p0_ref[...], p1_ref[...], p2_ref[...]]
-    half = p3_ref[...]
-    upper = bit(3)
     own = own_ref[...]
+    group = lax.div(lax.axis_index("gz"), 4)
+    place = lax.rem(lax.axis_index("gz"), 4)
+    others = (a_ref[...], c_ref[...], b_ref[...])
+    groups = []
+    for j in range(4):
+        slot = lax.rem(group, 2) * (1 - 2 * (j % 2)) + j % 2
+        slot = slot + 2 * (lax.div(group, 2) * (1 - 2 * (j // 2)) + j // 2)
+        groups.append(jnp.where(slot == 1, others[0], jnp.where(slot == 2, others[1], others[2])))
     flows = []
     for f in range(2):
-        y = half[f * ROWS:(f + 1) * ROWS]
-        z11, z22, a = (
-            spread_coef(half[2 * ROWS:], f, i) for i in (0, 2, 3)
-        )
-        yf_above, z_above, a_above = (jnp.where(upper, zero, x) for x in (y, z11, a))
-        yl_below, z_below = (jnp.where(upper, x, zero) for x in (y, z22))
-        for place in (2, 1, 0):
-            yf, yl, z11, z12, z22, a = unpack(partners[place], f)
-            below = bit(place)
-            g = a_above / (1.0 + a_above * (z_above + z22))
-            flow = g * (yf_above - yl)
-            yf_above = jnp.where(below, yf_above, yf + z12 * flow)
-            z_above = jnp.where(below, z_above, z11 - z12 * z12 * g)
-            a_above = jnp.where(below, a_above, a)
-            g = a / (1.0 + a * (z_below + z11))
-            flow = g * (yl_below - yf)
-            yl_below = jnp.where(below, yl + z12 * flow, yl_below)
-            z_below = jnp.where(below, z22 - z12 * z12 * g, z_below)
+        blocks = [unpack(g, f) for g in groups]
+        inner_above, inner_below = unpack(above_ref[...], f), unpack(below_ref[...], f)
+        upper, lower = (zero, zero, zero), (zero, zero)
+        for j in (3, 2, 1):
+            upper = above(upper, blocks[j], j > group)
+        for j in (0, 1, 2):
+            lower = below(lower, blocks[j], j < group)
+        upper = above(upper, inner_above, place < 3)
+        lower = below(lower, inner_below, place > 0)
+        yf_above, z_above, a_above = upper
+        yl_below, z_below = lower
         yf, yl, z11, z12, z22, a = unpack(own, f)
         p = 1.0 + a * (z_below + z11)
         q = 1.0 + a_above * (z_above + z22)
@@ -467,15 +540,16 @@
     state_shape = (STATE, LANES)
     wide = jax.ShapeDtypeStruct(part, F32)
     half = jax.ShapeDtypeStruct(part, jnp.bfloat16)
+    split = jax.ShapeDtypeStruct((2, CELLS, 3 * LANES), jnp.bfloat16)
     tall = jax.ShapeDtypeStruct((LEVELS, ROWS + 2 * PAD, LANES), F32)
 
     def in_hbm(*arrays):
         return [pltpu.with_memory_space_constraint(x, pltpu.HBM) for x in arrays]
 
     tile = (ROWS, LANES)
-    ws, ts, east, visc, wn, tn, north, far, near, own, up, down, rho, inv, coef = call(
+    ws, ts, east, visc, wn, tn, north, parts, far, near, own, up, down, rho, inv, coef = call(
         pack_kernel,
-        [tall, tall, half, half, wide, wide, half, strip, strip, (48, CELLS), block, block, part, (2, *tile), (COEF, LANES)],
+        [tall, tall, half, half, wide, wide, half, split, strip, strip, (48, CELLS), block, block, part, (2, *tile), (COEF, LANES)],
         [HBM] * 10,
         [
             pltpu.SMEM((LEVELS,), F32),
@@ -495,13 +569,11 @@
     rhs, sums, dense = call(
         main_kernel,
         [block, state_shape, strip],
-        [VMEM] * 12,
-        [
-            pltpu.VMEM(part, F32),
-        ],
+        [VMEM] * 13,
+        [pltpu.VMEM(part, F32), pltpu.VMEM((4, *part), F32), pltpu.VMEM((2, 3, *part), F32)],
         flops=16_000_000,
     )(
-        wn, tn, north, ws, ts, east, visc, up, down, rho, inv, coef,
+        wn, tn, north, ws, ts, east, visc, parts, up, down, rho, inv, coef,
     )
     state, faces = call(
         edge_kernel, [state_shape, (16, CELLS)], [VMEM] * 5, [pltpu.VMEM((48, CELLS), F32)]
@@ -511,20 +583,20 @@
         return lax.ppermute(x, "gz", [(i, partner(i)) for i in range(count)])
 
     three, two, one = (swap(state, lambda i, k=k: i ^ k) for k in (3, 2, 1))
-    (y,) = call(
-        local_kernel, [block], [VMEM] * 5, [pltpu.VMEM(block, F32)], flops=4_000_000
-    )(rhs, up, down, faces, state)
     pair, four = call(four_kernel, [state_shape] * 2, [VMEM] * 4)(state, one, two, three)
-    four_other = swap(four, lambda i: i ^ 4)
-    (eight,) = call(half_kernel, [(2 * ROWS + COEF, LANES)], [VMEM] * 2)(four, four_other)
-    eight_other = swap(eight, lambda i: (i + 4 if i & 4 else i - 4) % count)
+    y, inner_above, inner_below = call(
+        local_kernel, [block, state_shape, state_shape], [VMEM] * 7, [pltpu.VMEM(block, F32)], flops=4_000_000
+    )(rhs, up, down, faces, state, one, pair)
+    side_a = swap(four, lambda i: i ^ 4)
+    side_b = swap(four, lambda i: (i + 4 if i & 4 else i - 4) % count)
+    side_c = swap(four, lambda i: FAR_GROUP[i // 2] * 2 + i % 2)
     return tuple(call(
         final_kernel,
         [part, part],
-        [VMEM] * 8,
+        [VMEM] * 9,
         [pltpu.VMEM(block, F32), pltpu.SemaphoreType.DMA((2 * PARTS,))],
         [HBM] * 2,
-    )(y, up, down, state, one, pair, four_other, eight_other))
+    )(y, up, down, state, inner_above, inner_below, side_a, side_b, side_c))
 
 
 def solution(mesh):

time: 31.6 us -> 30.8 us (0.975); the launches traced: 31.5 us -> 30.3 us
  starting transfers between devices: 16.2 us -> 14.8 us
  waiting for transfers between devices: 7.25 us -> 8.44 us
  Pallas kernels: 7.38 us -> 6.38 us
    ppermute x5 -> x6, starting transfers between devices: 12.1 us -> 10.7 us  [swap(): return lax.ppermute(x, 'gz', [(i, partner(i)) for i in range(count)])]
    pallas_call x5 -> x4, Pallas kernels: 6.74 us -> 5.85 us  [the longest x1 2.2 us: shards(): call(main_kernel, [block, state_shape, strip], [VMEM] * 13, [pltpu.VMEM(p...]
    ppermute x1, waiting for transfers between devices: 0.01 us -> 0.6 us  [shards(): lax.ppermute(far, 'gx', [(i, (i + 1) % count if i % 2 else (i - 1) % coun...]
    ppermute x5 -> x6, waiting for transfers between devices: 7.25 us -> 7.84 us  [swap(): return lax.ppermute(x, 'gz', [(i, partner(i)) for i in range(count)])]
  transfers between devices with their start and end apart: 7 -> 8, of which waited for: 5 -> 5; matrix products, arithmetic and copies ran while one was open for 0% -> 0% of each run, Pallas kernels for 12% -> 10%
where the time goes in v4:
time: 30.8 us; the launch traced here: 30.3 us
  starting transfers between devices  14.8 us (48%)
  waiting for transfers between devices  8.44 us (27%)
  Pallas kernels  6.38 us (21%)
  between operations  0.68 us (2%)
    ppermute x6, starting transfers between devices, swap(): return lax.ppermute(x, 'gz', [(i, partner(i)) for i in range(count)])  10.7 us
    ppermute x6, waiting for transfers between devices, swap(): return lax.ppermute(x, 'gz', [(i, partner(i)) for i in range(count)])  7.84 us
    ppermute x1, starting transfers between devices, shards(): lax.ppermute(far, 'gx', [(i, (i + 1) % count if i % 2 else (i - 1) % coun...  4.1 us
    pallas_call x1, Pallas kernels, shards(): call(main_kernel, [block, state_shape, strip], [VMEM] * 13, [pltpu.VMEM(p...  2.2 us
    pallas_call x1, Pallas kernels, shards(): call(pack_kernel, [tall, tall, half, half, wide, wide, half, split, strip...  1.83 us
    pallas_call x1, Pallas kernels, shards(): call(final_kernel, [part, part], [VMEM] * 9, [pltpu.VMEM(block, F32), plt...  1.13 us
    pallas_call x1, Pallas kernels, shards(): call(local_kernel, [block, state_shape, state_shape], [VMEM] * 7, [pltpu....  0.7 us
  transfers between devices with their start and end apart: 8, of which 5 were waited for; matrix products, arithmetic and copies ran while one was open for 0% of the time, Pallas kernels for 10%

profile of v4, /device:TPU:2, one launch (start us, length us, event | category | flops | bytes accessed | tf_op | source)
XLA Modules:
  0.0 30.3 jit_solution(12227038903430849162)
XLA Ops:
  0.6 1.8 %shard_map.113 = (f32[40,32,128]{2,1,0:T(8,128)S(1)}, f32[40,32,128]{2,1,0:T(8,128)S(1)}, bf16[40,16,128]{2,1,0:T(8,128)(2,1)S(1)}, bf16[40,16,128]{2,1,0:T(8,12...) custom-call(f32[40,16,128]{2,1,0:T(8,128)} %ws_hbm.1, ...), custom_call_target="tpu_custom_call" | custom-call | tf_op jit(solution)/shard_map/pallas_call | solution.py:550
  2.5 4.1 %collective-permute-start = (f32[8,640]{1,0:T(8,128)S(1)}, f32[8,640]{1,0:T(8,128)S(1)}, u32[]{:S(2)}, u32[]{:S(2)}) collective-permute-start(f32[8,640]{1,0:T(8,128)S(1)} %get-tuple-element.42), channel_id=1, source_target_pairs={{0,240},{16,32},{32,16},{48,64},{64,48},{80,96},{96,80},{112,128},... | collective-permute-start | bytes 61448 | tf_op jit(solution)/shard_map/ppermute | solution.py:565
  6.6 0.0 collective-permute-start.1
  6.6 2.2 %shard_map.114 = (f32[2,40,16,128]{3,2,1,0:T(8,128)S(1)}, f32[72,128]{1,0:T(8,128)S(1)}, f32[8,640]{1,0:T(8,128)S(1)}) custom-call(f32[40,16,128]{2,1,0:T(8,128)S(1)} %get-tuple-element.28.wn_ref, f32[40,16,128]{2,1,0:T(8,128)S(1)} %get-tuple-element.29.tn_ref, bf16[40,16,128]{2,1,0:T(8,128)(2,1)S(1)} %get-tuple-element.30.north_ref, ...), custom_call_target="tpu_custom_call" | custom-call | flops 16000000 | bytes 2000000 | tf_op jit(solution)/shard_map/pallas_call | solution.py:569
  8.8 0.6 %collective-permute-done.far_ref = f32[8,640]{1,0:T(8,128)S(1)} collective-permute-done((f32[8,640]{1,0:T(8,128)S(1)}, f32[8,640]{1,0:T(8,128)S(1)}, u32[]{:S(2)}, u32[]{:S(2)}) %collective-permute-start) | collective-permute-done | bytes 20512 | tf_op jit(solution)/shard_map/ppermute | solution.py:565
  9.4 0.0 collective-permute-done.1.near_ref
  9.4 0.3 %shard_map.115 = (f32[72,128]{1,0:T(8,128)S(1)}, f32[16,640]{1,0:T(8,128)S(1)}) custom-call(f32[8,640]{1,0:T(8,128)S(1)} %collective-permute-done.far_ref, f32[8,640]{1,0:T(8,128)S(1)} %collective-permute-done.1.near_ref, f32[48,640]{1,0:T(8,128)S(1)} %get-tuple-element.44.own_ref, f32[72,128]{1,0:T(8,128)S(1)} %get-tuple-element.45.sums_ref, ...), custom_call_target="tpu_custom_call" | custom-call | tf_op jit(solution)/shard_map/pallas_call | solution.py:578
  9.7 2.3 %collective-permute-start.4 = (f32[72,128]{1,0:T(8,128)S(1)}, f32[72,128]{1,0:T(8,128)S(1)}, u32[]{:S(2)}, u32[]{:S(2)}) collective-permute-start(f32[72,128]{1,0:T(8,128)S(1)} %get-tuple-element.48.own_ref.state_ref), channel_id=1, source_target_pairs={{0,3},{1,2},{2,1},{3,0},{4,7},{5,6},{6,5},{7,4},{8,11},{9,10},{10,... | collective-permute-start | bytes 110600 | tf_op jit(solution)/shard_map/ppermute | solution.py:583
  12.0 1.5 %collective-permute-start.3 = (f32[72,128]{1,0:T(8,128)S(1)}, f32[72,128]{1,0:T(8,128)S(1)}, u32[]{:S(2)}, u32[]{:S(2)}) collective-permute-start(f32[72,128]{1,0:T(8,128)S(1)} %get-tuple-element.48.own_ref.state_ref), channel_id=1, source_target_pairs={{0,2},{1,3},{2,0},{3,1},{4,6},{5,7},{6,4},{7,5},{8,10},{9,11},{10,... | collective-permute-start | bytes 110600 | tf_op jit(solution)/shard_map/ppermute | solution.py:583
  13.6 0.0 collective-permute-start.2
  13.6 1.1 %collective-permute-done.4.three_ref = f32[72,128]{1,0:T(8,128)S(1)} collective-permute-done((f32[72,128]{1,0:T(8,128)S(1)}, f32[72,128]{1,0:T(8,128)S(1)}, u32[]{:S(2)}, u32[]{:S(2)}) %collective-permute-start.4) | collective-permute-done | bytes 36896 | tf_op jit(solution)/shard_map/ppermute | solution.py:583
  14.7 1.3 %collective-permute-done.3.two_ref = f32[72,128]{1,0:T(8,128)S(1)} collective-permute-done((f32[72,128]{1,0:T(8,128)S(1)}, f32[72,128]{1,0:T(8,128)S(1)}, u32[]{:S(2)}, u32[]{:S(2)}) %collective-permute-start.3) | collective-permute-done | bytes 36896 | tf_op jit(solution)/shard_map/ppermute | solution.py:583
  16.0 1.5 %collective-permute-done.2.one_ref = f32[72,128]{1,0:T(8,128)S(1)} collective-permute-done((f32[72,128]{1,0:T(8,128)S(1)}, f32[72,128]{1,0:T(8,128)S(1)}, u32[]{:S(2)}, u32[]{:S(2)}) %collective-permute-start.2) | collective-permute-done | bytes 36896 | tf_op jit(solution)/shard_map/ppermute | solution.py:583
  17.5 0.2 shard_map.116
  17.7 5.4 %collective-permute-start.7 = (f32[72,128]{1,0:T(8,128)S(1)}, f32[72,128]{1,0:T(8,128)S(1)}, u32[]{:S(2)}, u32[]{:S(2)}) collective-permute-start(f32[72,128]{1,0:T(8,128)S(1)} %get-tuple-element.53), channel_id=1, source_target_pairs={{0,10},{1,11},{2,8},{3,9},{4,14},{5,15},{6,12},{7,13},{8,2},{9,3},... | collective-permute-start | bytes 110600 | tf_op jit(solution)/shard_map/ppermute | solution.py:583
  23.1 0.6 %collective-permute-start.6 = (f32[72,128]{1,0:T(8,128)S(1)}, f32[72,128]{1,0:T(8,128)S(1)}, u32[]{:S(2)}, u32[]{:S(2)}) collective-permute-start(f32[72,128]{1,0:T(8,128)S(1)} %get-tuple-element.53), channel_id=1, source_target_pairs={{0,12},{1,13},{2,14},{3,15},{4,8},{5,9},{6,10},{7,11},{8,4},{9,5},... | collective-permute-start | bytes 110600 | tf_op jit(solution)/shard_map/ppermute | solution.py:583
  23.7 0.9 %collective-permute-start.5 = (f32[72,128]{1,0:T(8,128)S(1)}, f32[72,128]{1,0:T(8,128)S(1)}, u32[]{:S(2)}, u32[]{:S(2)}) collective-permute-start(f32[72,128]{1,0:T(8,128)S(1)} %get-tuple-element.53), channel_id=1, source_target_pairs={{0,4},{1,5},{2,6},{3,7},{4,0},{5,1},{6,2},{7,3},{8,12},{9,13},{10,... | collective-permute-start | bytes 110600 | tf_op jit(solution)/shard_map/ppermute | solution.py:583
  24.6 0.7 %shard_map.117 = (f32[2,40,16,128]{3,2,1,0:T(8,128)S(1)}, f32[72,128]{1,0:T(8,128)S(1)}, f32[72,128]{1,0:T(8,128)S(1)}) custom-call(f32[2,40,16,128]{3,2,1,0:T(8,128)S(1)} %get-tuple-element.41.rhs_ref, f32[2,40,16,128]{3,2,1,0:T(8,128)S(1)} %get-tuple-element.36.up_ref, f32[2,40,16,128]{3,2,1,0:T(8,128)S(1)} %get-tuple-element.37.down_ref, ...), custom_call_target="tpu_custom_call" | custom-call | flops 4000000 | bytes 500000 | tf_op jit(solution)/shard_map/pallas_call | solution.py:587
  25.3 0.0 collective-permute-done.7.c_ref
  25.3 3.9 %collective-permute-done.6.b_ref = f32[72,128]{1,0:T(8,128)S(1)} collective-permute-done((f32[72,128]{1,0:T(8,128)S(1)}, f32[72,128]{1,0:T(8,128)S(1)}, u32[]{:S(2)}, u32[]{:S(2)}) %collective-permute-start.6) | collective-permute-done | bytes 36896 | tf_op jit(solution)/shard_map/ppermute | solution.py:583
  29.2 0.0 collective-permute-done.5.a_ref
  29.2 1.1 %shard_map.118 = (f32[40,16,128]{2,1,0:T(8,128)}, f32[40,16,128]{2,1,0:T(8,128)}) custom-call(f32[2,40,16,128]{3,2,1,0:T(8,128)S(1)} %get-tuple-element.50.y_ref, f32[2,40,16,128]{3,2,1,0:T(8,128)S(1)} %get-tuple-element.36.up_ref, f32[2,40,16,128]{3,2,1,0:T(8,128)S(1)} %get-tuple-element.37.down_ref, f32[72,128]{1,0:T(8,128)S(1)} %get-tuple-element.48.own_ref.state_ref, ...), custom_call_target="tpu_custom_call" | custom-call | tf_op jit(solution)/shard_map/pallas_call | solution.py:593
Async XLA Ops:
  2.5 6.9 %collective-permute-start = (f32[8,640]{1,0:T(8,128)S(1)}, f32[8,640]{1,0:T(8,128)S(1)}, u32[]{:S(2)}, u32[]{:S(2)}) collective-permute-start(f32[8,640]{1,0:T(8,128)S(1)} %get-tuple-element.42), channel_id=1, source_target_pairs={{0,240},{16,32},{32,16},{48,64},{64,48},{80,96},{96,80},{112,128},... | collective-permute-start | bytes 61448 | tf_op jit(solution)/shard_map/ppermute | solution.py:565
  6.6 2.8 %collective-permute-start.1 = (f32[8,640]{1,0:T(8,128)S(1)}, f32[8,640]{1,0:T(8,128)S(1)}, u32[]{:S(2)}, u32[]{:S(2)}) collective-permute-start(f32[8,640]{1,0:T(8,128)S(1)} %get-tuple-element.43), channel_id=1, source_target_pairs={{0,16},{16,0},{32,48},{48,32},{64,80},{80,64},{96,112},{112,96},{1... | collective-permute-start | bytes 61448 | tf_op jit(solution)/shard_map/ppermute | solution.py:568
  9.7 4.9 %collective-permute-start.4 = (f32[72,128]{1,0:T(8,128)S(1)}, f32[72,128]{1,0:T(8,128)S(1)}, u32[]{:S(2)}, u32[]{:S(2)}) collective-permute-start(f32[72,128]{1,0:T(8,128)S(1)} %get-tuple-element.48.own_ref.state_ref), channel_id=1, source_target_pairs={{0,3},{1,2},{2,1},{3,0},{4,7},{5,6},{6,5},{7,4},{8,11},{9,10},{10,... | collective-permute-start | bytes 110600 | tf_op jit(solution)/shard_map/ppermute | solution.py:583
  12.0 4.0 %collective-permute-start.3 = (f32[72,128]{1,0:T(8,128)S(1)}, f32[72,128]{1,0:T(8,128)S(1)}, u32[]{:S(2)}, u32[]{:S(2)}) collective-permute-start(f32[72,128]{1,0:T(8,128)S(1)} %get-tuple-element.48.own_ref.state_ref), channel_id=1, source_target_pairs={{0,2},{1,3},{2,0},{3,1},{4,6},{5,7},{6,4},{7,5},{8,10},{9,11},{10,... | collective-permute-start | bytes 110600 | tf_op jit(solution)/shard_map/ppermute | solution.py:583
  13.6 4.0 %collective-permute-start.2 = (f32[72,128]{1,0:T(8,128)S(1)}, f32[72,128]{1,0:T(8,128)S(1)}, u32[]{:S(2)}, u32[]{:S(2)}) collective-permute-start(f32[72,128]{1,0:T(8,128)S(1)} %get-tuple-element.48.own_ref.state_ref), channel_id=1, source_target_pairs={{0,1},{1,0},{2,3},{3,2},{4,5},{5,4},{6,7},{7,6},{8,9},{9,8},{10,11... | collective-permute-start | bytes 110600 | tf_op jit(solution)/shard_map/ppermute | solution.py:583
  17.7 7.6 %collective-permute-start.7 = (f32[72,128]{1,0:T(8,128)S(1)}, f32[72,128]{1,0:T(8,128)S(1)}, u32[]{:S(2)}, u32[]{:S(2)}) collective-permute-start(f32[72,128]{1,0:T(8,128)S(1)} %get-tuple-element.53), channel_id=1, source_target_pairs={{0,10},{1,11},{2,8},{3,9},{4,14},{5,15},{6,12},{7,13},{8,2},{9,3},... | collective-permute-start | bytes 110600 | tf_op jit(solution)/shard_map/ppermute | solution.py:583
  23.1 6.1 %collective-permute-start.6 = (f32[72,128]{1,0:T(8,128)S(1)}, f32[72,128]{1,0:T(8,128)S(1)}, u32[]{:S(2)}, u32[]{:S(2)}) collective-permute-start(f32[72,128]{1,0:T(8,128)S(1)} %get-tuple-element.53), channel_id=1, source_target_pairs={{0,12},{1,13},{2,14},{3,15},{4,8},{5,9},{6,10},{7,11},{8,4},{9,5},... | collective-permute-start | bytes 110600 | tf_op jit(solution)/shard_map/ppermute | solution.py:583
  23.7 5.5 %collective-permute-start.5 = (f32[72,128]{1,0:T(8,128)S(1)}, f32[72,128]{1,0:T(8,128)S(1)}, u32[]{:S(2)}, u32[]{:S(2)}) collective-permute-start(f32[72,128]{1,0:T(8,128)S(1)} %get-tuple-element.53), channel_id=1, source_target_pairs={{0,4},{1,5},{2,6},{3,7},{4,0},{5,1},{6,2},{7,3},{8,12},{9,13},{10,... | collective-permute-start | bytes 110600 | tf_op jit(solution)/shard_map/ppermute | solution.py:583

commit v5 on v4

--- a/solution.py
+++ b/solution.py
@@ -205,7 +205,7 @@
             high = x.astype(jnp.bfloat16)
             rest = x - high.astype(F32)
             mid = rest.astype(jnp.bfloat16)
-            parts = [high, mid, (rest - mid.astype(F32)).astype(jnp.bfloat16)]
+            parts = [high, mid]
             for j, value in enumerate(parts):
                 parts_ref[index, :, j * LANES:(j + 1) * LANES] = value
         left_parts += [select] * len(parts)
@@ -253,7 +253,7 @@
             x = ref[k:k + chunk].reshape(LANES, LANES)
             face_ref[2 + i, k:k + chunk] = dot(pair_y, x).reshape(chunk, ROWS, LANES)
     weights = jnp.concatenate([stencil(c, -2) for c in (MEAN, SKEW, STEP)], axis=1).astype(jnp.bfloat16)
-    weights = jnp.concatenate([weights] * 3, axis=0)
+    weights = jnp.concatenate([weights] * 2, axis=0)
     for f in range(2):
         product = dot(parts_ref[f], weights)
         for j in range(3):
@@ -540,7 +540,7 @@
     state_shape = (STATE, LANES)
     wide = jax.ShapeDtypeStruct(part, F32)
     half = jax.ShapeDtypeStruct(part, jnp.bfloat16)
-    split = jax.ShapeDtypeStruct((2, CELLS, 3 * LANES), jnp.bfloat16)
+    split = jax.ShapeDtypeStruct((2, CELLS, 2 * LANES), jnp.bfloat16)
     tall = jax.ShapeDtypeStruct((LEVELS, ROWS + 2 * PAD, LANES), F32)
 
     def in_hbm(*arrays):

time: 30.8 us -> 30.7 us (level)
  the two profiles are of different devices: /device:TPU:2 before, /device:TPU:4 now
where the time goes in v5:
time: 30.7 us; the launch traced here: 30.6 us
  starting transfers between devices  14.4 us (47%)
  waiting for transfers between devices  9.5 us (31%)
  Pallas kernels  6.04 us (20%)
  between operations  0.68 us (2%)
    ppermute x6, starting transfers between devices, swap(): return lax.ppermute(x, 'gz', [(i, partner(i)) for i in range(count)])  11.9 us
    ppermute x6, waiting for transfers between devices, swap(): return lax.ppermute(x, 'gz', [(i, partner(i)) for i in range(count)])  7.02 us
    ppermute x1, starting transfers between devices, shards(): lax.ppermute(far, 'gx', [(i, (i + 1) % count if i % 2 else (i - 1) % coun...  2.48 us
    ppermute x1, waiting for transfers between devices, shards(): lax.ppermute(far, 'gx', [(i, (i + 1) % count if i % 2 else (i - 1) % coun...  2.48 us
    pallas_call x1, Pallas kernels, shards(): call(main_kernel, [block, state_shape, strip], [VMEM] * 13, [pltpu.VMEM(p...  1.94 us
    pallas_call x1, Pallas kernels, shards(): call(pack_kernel, [tall, tall, half, half, wide, wide, half, split, strip...  1.75 us
    pallas_call x1, Pallas kernels, shards(): call(final_kernel, [part, part], [VMEM] * 9, [pltpu.VMEM(block, F32), plt...  1.12 us
    pallas_call x1, Pallas kernels, shards(): call(local_kernel, [block, state_shape, state_shape], [VMEM] * 7, [pltpu....  0.7 us
  transfers between devices with their start and end apart: 8, of which 6 were waited for; matrix products, arithmetic and copies ran while one was open for 0% of the time, Pallas kernels for 9%

profile of v5, /device:TPU:4, one launch (start us, length us, event | category | flops | bytes accessed | tf_op | source)
XLA Modules:
  0.0 30.6 jit_solution(5416861825692388539)
XLA Ops:
  0.6 1.8 %shard_map.113 = (f32[40,32,128]{2,1,0:T(8,128)S(1)}, f32[40,32,128]{2,1,0:T(8,128)S(1)}, bf16[40,16,128]{2,1,0:T(8,128)(2,1)S(1)}, bf16[40,16,128]{2,1,0:T(8,12...) custom-call(f32[40,16,128]{2,1,0:T(8,128)} %ws_hbm.1, ...), custom_call_target="tpu_custom_call" | custom-call | tf_op jit(solution)/shard_map/pallas_call | solution.py:550
  2.4 2.5 %collective-permute-start = (f32[8,640]{1,0:T(8,128)S(1)}, f32[8,640]{1,0:T(8,128)S(1)}, u32[]{:S(2)}, u32[]{:S(2)}) collective-permute-start(f32[8,640]{1,0:T(8,128)S(1)} %get-tuple-element.42), channel_id=1, source_target_pairs={{0,240},{16,32},{32,16},{48,64},{64,48},{80,96},{96,80},{112,128},... | collective-permute-start | bytes 61448 | tf_op jit(solution)/shard_map/ppermute | solution.py:565
  4.9 0.0 collective-permute-start.1
  4.9 1.9 %shard_map.114 = (f32[2,40,16,128]{3,2,1,0:T(8,128)S(1)}, f32[72,128]{1,0:T(8,128)S(1)}, f32[8,640]{1,0:T(8,128)S(1)}) custom-call(f32[40,16,128]{2,1,0:T(8,128)S(1)} %get-tuple-element.28.wn_ref, f32[40,16,128]{2,1,0:T(8,128)S(1)} %get-tuple-element.29.tn_ref, bf16[40,16,128]{2,1,0:T(8,128)(2,1)S(1)} %get-tuple-element.30.north_ref, ...), custom_call_target="tpu_custom_call" | custom-call | flops 16000000 | bytes 2000000 | tf_op jit(solution)/shard_map/pallas_call | solution.py:569
  6.8 2.5 %collective-permute-done.far_ref = f32[8,640]{1,0:T(8,128)S(1)} collective-permute-done((f32[8,640]{1,0:T(8,128)S(1)}, f32[8,640]{1,0:T(8,128)S(1)}, u32[]{:S(2)}, u32[]{:S(2)}) %collective-permute-start) | collective-permute-done | bytes 20512 | tf_op jit(solution)/shard_map/ppermute | solution.py:565
  9.3 0.0 collective-permute-done.1.near_ref
  9.3 0.3 %shard_map.115 = (f32[72,128]{1,0:T(8,128)S(1)}, f32[16,640]{1,0:T(8,128)S(1)}) custom-call(f32[8,640]{1,0:T(8,128)S(1)} %collective-permute-done.far_ref, f32[8,640]{1,0:T(8,128)S(1)} %collective-permute-done.1.near_ref, f32[48,640]{1,0:T(8,128)S(1)} %get-tuple-element.44.own_ref, f32[72,128]{1,0:T(8,128)S(1)} %get-tuple-element.45.sums_ref, ...), custom_call_target="tpu_custom_call" | custom-call | tf_op jit(solution)/shard_map/pallas_call | solution.py:578
  9.7 2.6 %collective-permute-start.4 = (f32[72,128]{1,0:T(8,128)S(1)}, f32[72,128]{1,0:T(8,128)S(1)}, u32[]{:S(2)}, u32[]{:S(2)}) collective-permute-start(f32[72,128]{1,0:T(8,128)S(1)} %get-tuple-element.48.own_ref.state_ref), channel_id=1, source_target_pairs={{0,3},{1,2},{2,1},{3,0},{4,7},{5,6},{6,5},{7,4},{8,11},{9,10},{10,... | collective-permute-start | bytes 110600 | tf_op jit(solution)/shard_map/ppermute | solution.py:583
  12.3 0.1 collective-permute-start.3
  12.4 0.8 %collective-permute-start.2 = (f32[72,128]{1,0:T(8,128)S(1)}, f32[72,128]{1,0:T(8,128)S(1)}, u32[]{:S(2)}, u32[]{:S(2)}) collective-permute-start(f32[72,128]{1,0:T(8,128)S(1)} %get-tuple-element.48.own_ref.state_ref), channel_id=1, source_target_pairs={{0,1},{1,0},{2,3},{3,2},{4,5},{5,4},{6,7},{7,6},{8,9},{9,8},{10,11... | collective-permute-start | bytes 110600 | tf_op jit(solution)/shard_map/ppermute | solution.py:583
  13.2 1.4 %collective-permute-done.4.three_ref = f32[72,128]{1,0:T(8,128)S(1)} collective-permute-done((f32[72,128]{1,0:T(8,128)S(1)}, f32[72,128]{1,0:T(8,128)S(1)}, u32[]{:S(2)}, u32[]{:S(2)}) %collective-permute-start.4) | collective-permute-done | bytes 36896 | tf_op jit(solution)/shard_map/ppermute | solution.py:583
  14.6 1.7 %collective-permute-done.3.two_ref = f32[72,128]{1,0:T(8,128)S(1)} collective-permute-done((f32[72,128]{1,0:T(8,128)S(1)}, f32[72,128]{1,0:T(8,128)S(1)}, u32[]{:S(2)}, u32[]{:S(2)}) %collective-permute-start.3) | collective-permute-done | bytes 36896 | tf_op jit(solution)/shard_map/ppermute | solution.py:583
  16.3 0.1 collective-permute-done.2.one_ref
  16.4 0.2 shard_map.116
  16.6 6.8 %collective-permute-start.7 = (f32[72,128]{1,0:T(8,128)S(1)}, f32[72,128]{1,0:T(8,128)S(1)}, u32[]{:S(2)}, u32[]{:S(2)}) collective-permute-start(f32[72,128]{1,0:T(8,128)S(1)} %get-tuple-element.53), channel_id=1, source_target_pairs={{0,10},{1,11},{2,8},{3,9},{4,14},{5,15},{6,12},{7,13},{8,2},{9,3},... | collective-permute-start | bytes 110600 | tf_op jit(solution)/shard_map/ppermute | solution.py:583
  23.4 0.6 %collective-permute-start.6 = (f32[72,128]{1,0:T(8,128)S(1)}, f32[72,128]{1,0:T(8,128)S(1)}, u32[]{:S(2)}, u32[]{:S(2)}) collective-permute-start(f32[72,128]{1,0:T(8,128)S(1)} %get-tuple-element.53), channel_id=1, source_target_pairs={{0,12},{1,13},{2,14},{3,15},{4,8},{5,9},{6,10},{7,11},{8,4},{9,5},... | collective-permute-start | bytes 110600 | tf_op jit(solution)/shard_map/ppermute | solution.py:583
  23.9 0.9 %collective-permute-start.5 = (f32[72,128]{1,0:T(8,128)S(1)}, f32[72,128]{1,0:T(8,128)S(1)}, u32[]{:S(2)}, u32[]{:S(2)}) collective-permute-start(f32[72,128]{1,0:T(8,128)S(1)} %get-tuple-element.53), channel_id=1, source_target_pairs={{0,4},{1,5},{2,6},{3,7},{4,0},{5,1},{6,2},{7,3},{8,12},{9,13},{10,... | collective-permute-start | bytes 110600 | tf_op jit(solution)/shard_map/ppermute | solution.py:583
  24.9 0.7 %shard_map.117 = (f32[2,40,16,128]{3,2,1,0:T(8,128)S(1)}, f32[72,128]{1,0:T(8,128)S(1)}, f32[72,128]{1,0:T(8,128)S(1)}) custom-call(f32[2,40,16,128]{3,2,1,0:T(8,128)S(1)} %get-tuple-element.41.rhs_ref, f32[2,40,16,128]{3,2,1,0:T(8,128)S(1)} %get-tuple-element.36.up_ref, f32[2,40,16,128]{3,2,1,0:T(8,128)S(1)} %get-tuple-element.37.down_ref, ...), custom_call_target="tpu_custom_call" | custom-call | flops 4000000 | bytes 500000 | tf_op jit(solution)/shard_map/pallas_call | solution.py:587
  25.6 0.2 collective-permute-done.7.c_ref
  25.8 3.7 %collective-permute-done.6.b_ref = f32[72,128]{1,0:T(8,128)S(1)} collective-permute-done((f32[72,128]{1,0:T(8,128)S(1)}, f32[72,128]{1,0:T(8,128)S(1)}, u32[]{:S(2)}, u32[]{:S(2)}) %collective-permute-start.6) | collective-permute-done | bytes 36896 | tf_op jit(solution)/shard_map/ppermute | solution.py:583
  29.5 0.0 collective-permute-done.5.a_ref
  29.5 1.1 %shard_map.118 = (f32[40,16,128]{2,1,0:T(8,128)}, f32[40,16,128]{2,1,0:T(8,128)}) custom-call(f32[2,40,16,128]{3,2,1,0:T(8,128)S(1)} %get-tuple-element.50.y_ref, f32[2,40,16,128]{3,2,1,0:T(8,128)S(1)} %get-tuple-element.36.up_ref, f32[2,40,16,128]{3,2,1,0:T(8,128)S(1)} %get-tuple-element.37.down_ref, f32[72,128]{1,0:T(8,128)S(1)} %get-tuple-element.48.own_ref.state_ref, ...), custom_call_target="tpu_custom_call" | custom-call | tf_op jit(solution)/shard_map/pallas_call | solution.py:593
Async XLA Ops:
  2.4 6.9 %collective-permute-start = (f32[8,640]{1,0:T(8,128)S(1)}, f32[8,640]{1,0:T(8,128)S(1)}, u32[]{:S(2)}, u32[]{:S(2)}) collective-permute-start(f32[8,640]{1,0:T(8,128)S(1)} %get-tuple-element.42), channel_id=1, source_target_pairs={{0,240},{16,32},{32,16},{48,64},{64,48},{80,96},{96,80},{112,128},... | collective-permute-start | bytes 61448 | tf_op jit(solution)/shard_map/ppermute | solution.py:565
  4.9 4.4 %collective-permute-start.1 = (f32[8,640]{1,0:T(8,128)S(1)}, f32[8,640]{1,0:T(8,128)S(1)}, u32[]{:S(2)}, u32[]{:S(2)}) collective-permute-start(f32[8,640]{1,0:T(8,128)S(1)} %get-tuple-element.43), channel_id=1, source_target_pairs={{0,16},{16,0},{32,48},{48,32},{64,80},{80,64},{96,112},{112,96},{1... | collective-permute-start | bytes 61448 | tf_op jit(solution)/shard_map/ppermute | solution.py:568
  9.7 4.9 %collective-permute-start.4 = (f32[72,128]{1,0:T(8,128)S(1)}, f32[72,128]{1,0:T(8,128)S(1)}, u32[]{:S(2)}, u32[]{:S(2)}) collective-permute-start(f32[72,128]{1,0:T(8,128)S(1)} %get-tuple-element.48.own_ref.state_ref), channel_id=1, source_target_pairs={{0,3},{1,2},{2,1},{3,0},{4,7},{5,6},{6,5},{7,4},{8,11},{9,10},{10,... | collective-permute-start | bytes 110600 | tf_op jit(solution)/shard_map/ppermute | solution.py:583
  12.3 4.0 %collective-permute-start.3 = (f32[72,128]{1,0:T(8,128)S(1)}, f32[72,128]{1,0:T(8,128)S(1)}, u32[]{:S(2)}, u32[]{:S(2)}) collective-permute-start(f32[72,128]{1,0:T(8,128)S(1)} %get-tuple-element.48.own_ref.state_ref), channel_id=1, source_target_pairs={{0,2},{1,3},{2,0},{3,1},{4,6},{5,7},{6,4},{7,5},{8,10},{9,11},{10,... | collective-permute-start | bytes 110600 | tf_op jit(solution)/shard_map/ppermute | solution.py:583
  12.4 4.0 %collective-permute-start.2 = (f32[72,128]{1,0:T(8,128)S(1)}, f32[72,128]{1,0:T(8,128)S(1)}, u32[]{:S(2)}, u32[]{:S(2)}) collective-permute-start(f32[72,128]{1,0:T(8,128)S(1)} %get-tuple-element.48.own_ref.state_ref), channel_id=1, source_target_pairs={{0,1},{1,0},{2,3},{3,2},{4,5},{5,4},{6,7},{7,6},{8,9},{9,8},{10,11... | collective-permute-start | bytes 110600 | tf_op jit(solution)/shard_map/ppermute | solution.py:583
  16.6 9.2 %collective-permute-start.7 = (f32[72,128]{1,0:T(8,128)S(1)}, f32[72,128]{1,0:T(8,128)S(1)}, u32[]{:S(2)}, u32[]{:S(2)}) collective-permute-start(f32[72,128]{1,0:T(8,128)S(1)} %get-tuple-element.53), channel_id=1, source_target_pairs={{0,10},{1,11},{2,8},{3,9},{4,14},{5,15},{6,12},{7,13},{8,2},{9,3},... | collective-permute-start | bytes 110600 | tf_op jit(solution)/shard_map/ppermute | solution.py:583
  23.4 6.1 %collective-permute-start.6 = (f32[72,128]{1,0:T(8,128)S(1)}, f32[72,128]{1,0:T(8,128)S(1)}, u32[]{:S(2)}, u32[]{:S(2)}) collective-permute-start(f32[72,128]{1,0:T(8,128)S(1)} %get-tuple-element.53), channel_id=1, source_target_pairs={{0,12},{1,13},{2,14},{3,15},{4,8},{5,9},{6,10},{7,11},{8,4},{9,5},... | collective-permute-start | bytes 110600 | tf_op jit(solution)/shard_map/ppermute | solution.py:583
  23.9 5.5 %collective-permute-start.5 = (f32[72,128]{1,0:T(8,128)S(1)}, f32[72,128]{1,0:T(8,128)S(1)}, u32[]{:S(2)}, u32[]{:S(2)}) collective-permute-start(f32[72,128]{1,0:T(8,128)S(1)} %get-tuple-element.53), channel_id=1, source_target_pairs={{0,4},{1,5},{2,6},{3,7},{4,0},{5,1},{6,2},{7,3},{8,12},{9,13},{10,... | collective-permute-start | bytes 110600 | tf_op jit(solution)/shard_map/ppermute | solution.py:583

commit v6 on v5

--- a/solution.py
+++ b/solution.py
@@ -133,13 +133,9 @@
     refs = (ws_ref, ts_ref, east_ref, visc_ref)
     sources = (ws_hbm, ts_hbm, east_hbm, visc_hbm, wn_hbm, tn_hbm, north_hbm)
     targets = (*refs, wn_ref, tn_ref, north_ref)
-    pairs = [
-        (src, dst.at[:, PAD:PAD + ROWS] if i < 2 else dst) for i, (src, dst) in enumerate(zip(sources, targets))
+    copies = [
+        pltpu.make_async_copy(src, dst, sem.at[i]) for i, (src, dst) in enumerate(zip(sources, targets))
     ]
-    for src, dst in zip(sources[:2], targets):
-        pairs.append((src.at[:, ROWS - PAD:], dst.at[:, :PAD]))
-        pairs.append((src.at[:, :PAD], dst.at[:, PAD + ROWS:]))
-    copies = [pltpu.make_async_copy(src, dst, sem.at[i]) for i, (src, dst) in enumerate(pairs)]
     for copy in copies:
         copy.start()
     selects = [lane_selector(lanes) for lanes in strip_selectors()]
@@ -198,8 +194,7 @@
         copy.wait()
     left_parts, right_parts = [], []
     for index, (ref, select) in enumerate(zip(refs, selects)):
-        x = ref[:, PAD:PAD + ROWS] if ref.shape[1] > ROWS else ref[...]
-        x = x.reshape(CELLS, LANES)
+        x = ref[...].reshape(CELLS, LANES)
         parts = [x]
         if x.dtype == F32:
             high = x.astype(jnp.bfloat16)
@@ -223,10 +218,18 @@
 
 
 def main_kernel(
-    wn_ref, tn_ref, north_ref, ws_ref, ts_ref, east_ref, visc_ref, parts_ref,
+    wn_ref, tn_ref, north_ref, w_ref, t_ref, east_ref, visc_ref, parts_ref,
     up_ref, down_ref, rho_ref, inv_ref, coef_ref,
-    rhs_ref, sums_ref, dense_ref, packed_ref, face_ref, stencil_ref,
+    rhs_ref, sums_ref, dense_ref, packed_ref, face_ref, stencil_ref, ws_ref, ts_ref, sem,
 ):
+    pairs = []
+    for src, dst in ((w_ref, ws_ref), (t_ref, ts_ref)):
+        pairs.append((src, dst.at[:, PAD:PAD + ROWS]))
+        pairs.append((src.at[:, ROWS - PAD:], dst.at[:, :PAD]))
+        pairs.append((src.at[:, :PAD], dst.at[:, PAD + ROWS:]))
+    copies = [pltpu.make_async_copy(src, dst, sem.at[i]) for i, (src, dst) in enumerate(pairs)]
+    for copy in copies:
+        copy.start()
     tile = (ROWS, LANES)
     lane = iota(tile, 1)
     inv = [inv_ref[f] for f in range(2)]
@@ -258,6 +261,9 @@
         product = dot(parts_ref[f], weights)
         for j in range(3):
             stencil_ref[f, j] = product[:, j * LANES:(j + 1) * LANES].reshape(LEVELS, ROWS, LANES)
+
+    for copy in copies:
+        copy.wait()
 
     def level(k, carry):
         weight = rho_ref[k]
@@ -541,7 +547,7 @@
     wide = jax.ShapeDtypeStruct(part, F32)
     half = jax.ShapeDtypeStruct(part, jnp.bfloat16)
     split = jax.ShapeDtypeStruct((2, CELLS, 2 * LANES), jnp.bfloat16)
-    tall = jax.ShapeDtypeStruct((LEVELS, ROWS + 2 * PAD, LANES), F32)
+    tall = (LEVELS, ROWS + 2 * PAD, LANES)
 
     def in_hbm(*arrays):
         return [pltpu.with_memory_space_constraint(x, pltpu.HBM) for x in arrays]
@@ -549,14 +555,14 @@
     tile = (ROWS, LANES)
     ws, ts, east, visc, wn, tn, north, parts, far, near, own, up, down, rho, inv, coef = call(
         pack_kernel,
-        [tall, tall, half, half, wide, wide, half, split, strip, strip, (48, CELLS), block, block, part, (2, *tile), (COEF, LANES)],
+        [wide, wide, half, half, wide, wide, half, split, strip, strip, (48, CELLS), block, block, part, (2, *tile), (COEF, LANES)],
         [HBM] * 10,
         [
             pltpu.SMEM((LEVELS,), F32),
             pltpu.SMEM((LEVELS,), F32),
             pltpu.SMEM((1, ROWS), jnp.int32),
             pltpu.SemaphoreType.DMA((3,)),
-            pltpu.SemaphoreType.DMA((11,)),
+            pltpu.SemaphoreType.DMA((7,)),
         ],
     )(*in_hbm(
         vertical_section, theta_section, east_wind, eddy_viscosity, vertical_now, theta_now, north_wind,
@@ -570,7 +576,14 @@
         main_kernel,
         [block, state_shape, strip],
         [VMEM] * 13,
-        [pltpu.VMEM(part, F32), pltpu.VMEM((4, *part), F32), pltpu.VMEM((2, 3, *part), F32)],
+        [
+            pltpu.VMEM(part, F32),
+            pltpu.VMEM((4, *part), F32),
+            pltpu.VMEM((2, 3, *part), F32),
+            pltpu.VMEM(tall, F32),
+            pltpu.VMEM(tall, F32),
+            pltpu.SemaphoreType.DMA((6,)),
+        ],
         flops=16_000_000,
     )(
         wn, tn, north, ws, ts, east, visc, parts, up, down, rho, inv, coef,

time: 30.7 us -> 30.6 us (level)
  the two profiles are of different devices: /device:TPU:4 before, /device:TPU:2 now
where the time goes in v6:
time: 30.6 us; the launch traced here: 30.1 us
  starting transfers between devices  14.7 us (48%)
  waiting for transfers between devices  8.53 us (28%)
  Pallas kernels  6.17 us (20%)
  between operations  0.69 us (2%)
    ppermute x6, starting transfers between devices, swap(): return lax.ppermute(x, 'gz', [(i, partner(i)) for i in range(count)])  10.6 us
    ppermute x6, waiting for transfers between devices, swap(): return lax.ppermute(x, 'gz', [(i, partner(i)) for i in range(count)])  7.85 us
    ppermute x1, starting transfers between devices, shards(): lax.ppermute(far, 'gx', [(i, (i + 1) % count if i % 2 else (i - 1) % coun...  4.1 us
    pallas_call x1, Pallas kernels, shards(): call(main_kernel, [block, state_shape, strip], [VMEM] * 13, [pltpu.VMEM(p...  2.12 us
    pallas_call x1, Pallas kernels, shards(): call(pack_kernel, [wide, wide, half, half, wide, wide, half, split, strip...  1.71 us
    pallas_call x1, Pallas kernels, shards(): call(final_kernel, [part, part], [VMEM] * 9, [pltpu.VMEM(block, F32), plt...  1.13 us
    pallas_call x1, Pallas kernels, shards(): call(local_kernel, [block, state_shape, state_shape], [VMEM] * 7, [pltpu....  0.68 us
    ppermute x1, waiting for transfers between devices, shards(): lax.ppermute(far, 'gx', [(i, (i + 1) % count if i % 2 else (i - 1) % coun...  0.67 us
  transfers between devices with their start and end apart: 8, of which 5 were waited for; matrix products, arithmetic and copies ran while one was open for 0% of the time, Pallas kernels for 9%

profile of v6, /device:TPU:2, one launch (start us, length us, event | category | flops | bytes accessed | tf_op | source)
XLA Modules:
  0.0 30.1 jit_solution(6147950240609244610)
XLA Ops:
  0.6 1.7 %shard_map.113 = (f32[40,16,128]{2,1,0:T(8,128)S(1)}, f32[40,16,128]{2,1,0:T(8,128)S(1)}, bf16[40,16,128]{2,1,0:T(8,128)(2,1)S(1)}, bf16[40,16,128]{2,1,0:T(8,12...) custom-call(f32[40,16,128]{2,1,0:T(8,128)} %ws_hbm.1, ...), custom_call_target="tpu_custom_call" | custom-call | tf_op jit(solution)/shard_map/pallas_call | solution.py:556
  2.4 4.1 %collective-permute-start = (f32[8,640]{1,0:T(8,128)S(1)}, f32[8,640]{1,0:T(8,128)S(1)}, u32[]{:S(2)}, u32[]{:S(2)}) collective-permute-start(f32[8,640]{1,0:T(8,128)S(1)} %get-tuple-element.42), channel_id=1, source_target_pairs={{0,240},{16,32},{32,16},{48,64},{64,48},{80,96},{96,80},{112,128},... | collective-permute-start | bytes 61448 | tf_op jit(solution)/shard_map/ppermute | solution.py:571
  6.5 0.0 collective-permute-start.1
  6.5 2.1 %shard_map.114 = (f32[2,40,16,128]{3,2,1,0:T(8,128)S(1)}, f32[72,128]{1,0:T(8,128)S(1)}, f32[8,640]{1,0:T(8,128)S(1)}) custom-call(f32[40,16,128]{2,1,0:T(8,128)S(1)} %get-tuple-element.28.wn_ref, f32[40,16,128]{2,1,0:T(8,128)S(1)} %get-tuple-element.29.tn_ref, bf16[40,16,128]{2,1,0:T(8,128)(2,1)S(1)} %get-tuple-element.30.north_ref, ...), custom_call_target="tpu_custom_call" | custom-call | flops 16000000 | bytes 2000000 | tf_op jit(solution)/shard_map/pallas_call | solution.py:575
  8.6 0.7 %collective-permute-done.far_ref = f32[8,640]{1,0:T(8,128)S(1)} collective-permute-done((f32[8,640]{1,0:T(8,128)S(1)}, f32[8,640]{1,0:T(8,128)S(1)}, u32[]{:S(2)}, u32[]{:S(2)}) %collective-permute-start) | collective-permute-done | bytes 20512 | tf_op jit(solution)/shard_map/ppermute | solution.py:571
  9.3 0.0 collective-permute-done.1.near_ref
  9.3 0.3 %shard_map.115 = (f32[72,128]{1,0:T(8,128)S(1)}, f32[16,640]{1,0:T(8,128)S(1)}) custom-call(f32[8,640]{1,0:T(8,128)S(1)} %collective-permute-done.far_ref, f32[8,640]{1,0:T(8,128)S(1)} %collective-permute-done.1.near_ref, f32[48,640]{1,0:T(8,128)S(1)} %get-tuple-element.44.own_ref, f32[72,128]{1,0:T(8,128)S(1)} %get-tuple-element.45.sums_ref, ...), custom_call_target="tpu_custom_call" | custom-call | tf_op jit(solution)/shard_map/pallas_call | solution.py:591
  9.6 2.2 %collective-permute-start.4 = (f32[72,128]{1,0:T(8,128)S(1)}, f32[72,128]{1,0:T(8,128)S(1)}, u32[]{:S(2)}, u32[]{:S(2)}) collective-permute-start(f32[72,128]{1,0:T(8,128)S(1)} %get-tuple-element.48.own_ref.state_ref), channel_id=1, source_target_pairs={{0,3},{1,2},{2,1},{3,0},{4,7},{5,6},{6,5},{7,4},{8,11},{9,10},{10,... | collective-permute-start | bytes 110600 | tf_op jit(solution)/shard_map/ppermute | solution.py:596
  11.8 1.6 %collective-permute-start.3 = (f32[72,128]{1,0:T(8,128)S(1)}, f32[72,128]{1,0:T(8,128)S(1)}, u32[]{:S(2)}, u32[]{:S(2)}) collective-permute-start(f32[72,128]{1,0:T(8,128)S(1)} %get-tuple-element.48.own_ref.state_ref), channel_id=1, source_target_pairs={{0,2},{1,3},{2,0},{3,1},{4,6},{5,7},{6,4},{7,5},{8,10},{9,11},{10,... | collective-permute-start | bytes 110600 | tf_op jit(solution)/shard_map/ppermute | solution.py:596
  13.4 0.0 collective-permute-start.2
  13.4 1.1 %collective-permute-done.4.three_ref = f32[72,128]{1,0:T(8,128)S(1)} collective-permute-done((f32[72,128]{1,0:T(8,128)S(1)}, f32[72,128]{1,0:T(8,128)S(1)}, u32[]{:S(2)}, u32[]{:S(2)}) %collective-permute-start.4) | collective-permute-done | bytes 36896 | tf_op jit(solution)/shard_map/ppermute | solution.py:596
  14.6 1.3 %collective-permute-done.3.two_ref = f32[72,128]{1,0:T(8,128)S(1)} collective-permute-done((f32[72,128]{1,0:T(8,128)S(1)}, f32[72,128]{1,0:T(8,128)S(1)}, u32[]{:S(2)}, u32[]{:S(2)}) %collective-permute-start.3) | collective-permute-done | bytes 36896 | tf_op jit(solution)/shard_map/ppermute | solution.py:596
  15.8 1.6 %collective-permute-done.2.one_ref = f32[72,128]{1,0:T(8,128)S(1)} collective-permute-done((f32[72,128]{1,0:T(8,128)S(1)}, f32[72,128]{1,0:T(8,128)S(1)}, u32[]{:S(2)}, u32[]{:S(2)}) %collective-permute-start.2) | collective-permute-done | bytes 36896 | tf_op jit(solution)/shard_map/ppermute | solution.py:596
  17.4 0.2 shard_map.116
  17.6 5.3 %collective-permute-start.7 = (f32[72,128]{1,0:T(8,128)S(1)}, f32[72,128]{1,0:T(8,128)S(1)}, u32[]{:S(2)}, u32[]{:S(2)}) collective-permute-start(f32[72,128]{1,0:T(8,128)S(1)} %get-tuple-element.53), channel_id=1, source_target_pairs={{0,10},{1,11},{2,8},{3,9},{4,14},{5,15},{6,12},{7,13},{8,2},{9,3},... | collective-permute-start | bytes 110600 | tf_op jit(solution)/shard_map/ppermute | solution.py:596
  22.9 0.6 %collective-permute-start.6 = (f32[72,128]{1,0:T(8,128)S(1)}, f32[72,128]{1,0:T(8,128)S(1)}, u32[]{:S(2)}, u32[]{:S(2)}) collective-permute-start(f32[72,128]{1,0:T(8,128)S(1)} %get-tuple-element.53), channel_id=1, source_target_pairs={{0,12},{1,13},{2,14},{3,15},{4,8},{5,9},{6,10},{7,11},{8,4},{9,5},... | collective-permute-start | bytes 110600 | tf_op jit(solution)/shard_map/ppermute | solution.py:596
  23.5 0.9 %collective-permute-start.5 = (f32[72,128]{1,0:T(8,128)S(1)}, f32[72,128]{1,0:T(8,128)S(1)}, u32[]{:S(2)}, u32[]{:S(2)}) collective-permute-start(f32[72,128]{1,0:T(8,128)S(1)} %get-tuple-element.53), channel_id=1, source_target_pairs={{0,4},{1,5},{2,6},{3,7},{4,0},{5,1},{6,2},{7,3},{8,12},{9,13},{10,... | collective-permute-start | bytes 110600 | tf_op jit(solution)/shard_map/ppermute | solution.py:596
  24.4 0.7 %shard_map.117 = (f32[2,40,16,128]{3,2,1,0:T(8,128)S(1)}, f32[72,128]{1,0:T(8,128)S(1)}, f32[72,128]{1,0:T(8,128)S(1)}) custom-call(f32[2,40,16,128]{3,2,1,0:T(8,128)S(1)} %get-tuple-element.41.rhs_ref, f32[2,40,16,128]{3,2,1,0:T(8,128)S(1)} %get-tuple-element.36.up_ref, f32[2,40,16,128]{3,2,1,0:T(8,128)S(1)} %get-tuple-element.37.down_ref, ...), custom_call_target="tpu_custom_call" | custom-call | flops 4000000 | bytes 500000 | tf_op jit(solution)/shard_map/pallas_call | solution.py:600
  25.1 0.0 collective-permute-done.7.c_ref
  25.1 3.9 %collective-permute-done.6.b_ref = f32[72,128]{1,0:T(8,128)S(1)} collective-permute-done((f32[72,128]{1,0:T(8,128)S(1)}, f32[72,128]{1,0:T(8,128)S(1)}, u32[]{:S(2)}, u32[]{:S(2)}) %collective-permute-start.6) | collective-permute-done | bytes 36896 | tf_op jit(solution)/shard_map/ppermute | solution.py:596
  29.0 0.0 collective-permute-done.5.a_ref
  29.0 1.1 %shard_map.118 = (f32[40,16,128]{2,1,0:T(8,128)}, f32[40,16,128]{2,1,0:T(8,128)}) custom-call(f32[2,40,16,128]{3,2,1,0:T(8,128)S(1)} %get-tuple-element.50.y_ref, f32[2,40,16,128]{3,2,1,0:T(8,128)S(1)} %get-tuple-element.36.up_ref, f32[2,40,16,128]{3,2,1,0:T(8,128)S(1)} %get-tuple-element.37.down_ref, f32[72,128]{1,0:T(8,128)S(1)} %get-tuple-element.48.own_ref.state_ref, ...), custom_call_target="tpu_custom_call" | custom-call | tf_op jit(solution)/shard_map/pallas_call | solution.py:606
Async XLA Ops:
  2.4 6.9 %collective-permute-start = (f32[8,640]{1,0:T(8,128)S(1)}, f32[8,640]{1,0:T(8,128)S(1)}, u32[]{:S(2)}, u32[]{:S(2)}) collective-permute-start(f32[8,640]{1,0:T(8,128)S(1)} %get-tuple-element.42), channel_id=1, source_target_pairs={{0,240},{16,32},{32,16},{48,64},{64,48},{80,96},{96,80},{112,128},... | collective-permute-start | bytes 61448 | tf_op jit(solution)/shard_map/ppermute | solution.py:571
  6.5 2.8 %collective-permute-start.1 = (f32[8,640]{1,0:T(8,128)S(1)}, f32[8,640]{1,0:T(8,128)S(1)}, u32[]{:S(2)}, u32[]{:S(2)}) collective-permute-start(f32[8,640]{1,0:T(8,128)S(1)} %get-tuple-element.43), channel_id=1, source_target_pairs={{0,16},{16,0},{32,48},{48,32},{64,80},{80,64},{96,112},{112,96},{1... | collective-permute-start | bytes 61448 | tf_op jit(solution)/shard_map/ppermute | solution.py:574
  9.6 4.9 %collective-permute-start.4 = (f32[72,128]{1,0:T(8,128)S(1)}, f32[72,128]{1,0:T(8,128)S(1)}, u32[]{:S(2)}, u32[]{:S(2)}) collective-permute-start(f32[72,128]{1,0:T(8,128)S(1)} %get-tuple-element.48.own_ref.state_ref), channel_id=1, source_target_pairs={{0,3},{1,2},{2,1},{3,0},{4,7},{5,6},{6,5},{7,4},{8,11},{9,10},{10,... | collective-permute-start | bytes 110600 | tf_op jit(solution)/shard_map/ppermute | solution.py:596
  11.8 4.0 %collective-permute-start.3 = (f32[72,128]{1,0:T(8,128)S(1)}, f32[72,128]{1,0:T(8,128)S(1)}, u32[]{:S(2)}, u32[]{:S(2)}) collective-permute-start(f32[72,128]{1,0:T(8,128)S(1)} %get-tuple-element.48.own_ref.state_ref), channel_id=1, source_target_pairs={{0,2},{1,3},{2,0},{3,1},{4,6},{5,7},{6,4},{7,5},{8,10},{9,11},{10,... | collective-permute-start | bytes 110600 | tf_op jit(solution)/shard_map/ppermute | solution.py:596
  13.4 4.0 %collective-permute-start.2 = (f32[72,128]{1,0:T(8,128)S(1)}, f32[72,128]{1,0:T(8,128)S(1)}, u32[]{:S(2)}, u32[]{:S(2)}) collective-permute-start(f32[72,128]{1,0:T(8,128)S(1)} %get-tuple-element.48.own_ref.state_ref), channel_id=1, source_target_pairs={{0,1},{1,0},{2,3},{3,2},{4,5},{5,4},{6,7},{7,6},{8,9},{9,8},{10,11... | collective-permute-start | bytes 110600 | tf_op jit(solution)/shard_map/ppermute | solution.py:596
  17.6 7.5 %collective-permute-start.7 = (f32[72,128]{1,0:T(8,128)S(1)}, f32[72,128]{1,0:T(8,128)S(1)}, u32[]{:S(2)}, u32[]{:S(2)}) collective-permute-start(f32[72,128]{1,0:T(8,128)S(1)} %get-tuple-element.53), channel_id=1, source_target_pairs={{0,10},{1,11},{2,8},{3,9},{4,14},{5,15},{6,12},{7,13},{8,2},{9,3},... | collective-permute-start | bytes 110600 | tf_op jit(solution)/shard_map/ppermute | solution.py:596
  22.9 6.1 %collective-permute-start.6 = (f32[72,128]{1,0:T(8,128)S(1)}, f32[72,128]{1,0:T(8,128)S(1)}, u32[]{:S(2)}, u32[]{:S(2)}) collective-permute-start(f32[72,128]{1,0:T(8,128)S(1)} %get-tuple-element.53), channel_id=1, source_target_pairs={{0,12},{1,13},{2,14},{3,15},{4,8},{5,9},{6,10},{7,11},{8,4},{9,5},... | collective-permute-start | bytes 110600 | tf_op jit(solution)/shard_map/ppermute | solution.py:596
  23.5 5.5 %collective-permute-start.5 = (f32[72,128]{1,0:T(8,128)S(1)}, f32[72,128]{1,0:T(8,128)S(1)}, u32[]{:S(2)}, u32[]{:S(2)}) collective-permute-start(f32[72,128]{1,0:T(8,128)S(1)} %get-tuple-element.53), channel_id=1, source_target_pairs={{0,4},{1,5},{2,6},{3,7},{4,0},{5,1},{6,2},{7,3},{8,12},{9,13},{10,... | collective-permute-start | bytes 110600 | tf_op jit(solution)/shard_map/ppermute | solution.py:596

commit v7 on v6

--- a/solution.py
+++ b/solution.py
@@ -18,7 +18,7 @@
 PAD = 8
 FAR_GROUP = (5, 4, 7, 6, 1, 0, 3, 2)
 PARTS = 2
-UNROLL = 8
+UNROLL = 20
 HBM = pl.BlockSpec(memory_space=pltpu.HBM)
 VMEM = pl.BlockSpec(memory_space=pltpu.VMEM)
 SMEM = pl.BlockSpec(memory_space=pltpu.SMEM)
@@ -118,7 +118,7 @@
 
 def pack_kernel(
     ws_hbm, ts_hbm, east_hbm, visc_hbm, wn_hbm, tn_hbm, north_hbm, dens_hbm, coup_hbm, top_hbm,
-    ws_ref, ts_ref, east_ref, visc_ref, wn_ref, tn_ref, north_ref, parts_ref, far_ref, near_ref, own_ref,
+    ws_ref, ts_ref, east_ref, visc_ref, wn_ref, tn_ref, north_ref, far_ref, near_ref, own_ref,
     up_ref, down_ref, rho_ref, inv_ref, coef_ref,
     dens_ref, coup_ref, top_ref, small_sem, sem,
 ):
@@ -201,8 +201,6 @@
             rest = x - high.astype(F32)
             mid = rest.astype(jnp.bfloat16)
             parts = [high, mid]
-            for j, value in enumerate(parts):
-                parts_ref[index, :, j * LANES:(j + 1) * LANES] = value
         left_parts += [select] * len(parts)
         right_parts += parts
     total = lax.dot_general(
@@ -218,7 +216,7 @@
 
 
 def main_kernel(
-    wn_ref, tn_ref, north_ref, w_ref, t_ref, east_ref, visc_ref, parts_ref,
+    wn_ref, tn_ref, north_ref, w_ref, t_ref, east_ref, visc_ref,
     up_ref, down_ref, rho_ref, inv_ref, coef_ref,
     rhs_ref, sums_ref, dense_ref, packed_ref, face_ref, stencil_ref, ws_ref, ts_ref, sem,
 ):
@@ -257,8 +255,11 @@
             face_ref[2 + i, k:k + chunk] = dot(pair_y, x).reshape(chunk, ROWS, LANES)
     weights = jnp.concatenate([stencil(c, -2) for c in (MEAN, SKEW, STEP)], axis=1).astype(jnp.bfloat16)
     weights = jnp.concatenate([weights] * 2, axis=0)
-    for f in range(2):
-        product = dot(parts_ref[f], weights)
+    for f, ref in enumerate((w_ref, t_ref)):
+        x = ref[...].reshape(CELLS, LANES)
+        high = x.astype(jnp.bfloat16)
+        low = (x - high.astype(F32)).astype(jnp.bfloat16)
+        product = dot(jnp.concatenate([high, low], axis=1), weights)
         for j in range(3):
             stencil_ref[f, j] = product[:, j * LANES:(j + 1) * LANES].reshape(LEVELS, ROWS, LANES)
 
@@ -546,16 +547,15 @@
     state_shape = (STATE, LANES)
     wide = jax.ShapeDtypeStruct(part, F32)
     half = jax.ShapeDtypeStruct(part, jnp.bfloat16)
-    split = jax.ShapeDtypeStruct((2, CELLS, 2 * LANES), jnp.bfloat16)
     tall = (LEVELS, ROWS + 2 * PAD, LANES)
 
     def in_hbm(*arrays):
         return [pltpu.with_memory_space_constraint(x, pltpu.HBM) for x in arrays]
 
     tile = (ROWS, LANES)
-    ws, ts, east, visc, wn, tn, north, parts, far, near, own, up, down, rho, inv, coef = call(
+    ws, ts, east, visc, wn, tn, north, far, near, own, up, down, rho, inv, coef = call(
         pack_kernel,
-        [wide, wide, half, half, wide, wide, half, split, strip, strip, (48, CELLS), block, block, part, (2, *tile), (COEF, LANES)],
+        [wide, wide, half, half, wide, wide, half, strip, strip, (48, CELLS), block, block, part, (2, *tile), (COEF, LANES)],
         [HBM] * 10,
         [
             pltpu.SMEM((LEVELS,), F32),
@@ -575,7 +575,7 @@
     rhs, sums, dense = call(
         main_kernel,
         [block, state_shape, strip],
-        [VMEM] * 13,
+        [VMEM] * 12,
         [
             pltpu.VMEM(part, F32),
             pltpu.VMEM((4, *part), F32),
@@ -586,7 +586,7 @@
         ],
         flops=16_000_000,
     )(
-        wn, tn, north, ws, ts, east, visc, parts, up, down, rho, inv, coef,
+        wn, tn, north, ws, ts, east, visc, up, down, rho, inv, coef,
     )
     state, faces = call(
         edge_kernel, [state_shape, (16, CELLS)], [VMEM] * 5, [pltpu.VMEM((48, CELLS), F32)]

time: 30.6 us -> 30.6 us (level)
  no operation moved by 1% of the time
where the time goes in v7:
time: 30.6 us; the launch traced here: 30.1 us
  starting transfers between devices  14.7 us (48%)
  waiting for transfers between devices  8.59 us (28%)
  Pallas kernels  6.1 us (20%)
  between operations  0.68 us (2%)
    ppermute x6, starting transfers between devices, swap(): return lax.ppermute(x, 'gz', [(i, partner(i)) for i in range(count)])  10.6 us
    ppermute x6, waiting for transfers between devices, swap(): return lax.ppermute(x, 'gz', [(i, partner(i)) for i in range(count)])  7.88 us
    ppermute x1, starting transfers between devices, shards(): lax.ppermute(far, 'gx', [(i, (i + 1) % count if i % 2 else (i - 1) % coun...  4.1 us
    pallas_call x1, Pallas kernels, shards(): call(main_kernel, [block, state_shape, strip], [VMEM] * 12, [pltpu.VMEM(p...  2.09 us
    pallas_call x1, Pallas kernels, shards(): call(pack_kernel, [wide, wide, half, half, wide, wide, half, strip, strip...  1.7 us
    pallas_call x1, Pallas kernels, shards(): call(final_kernel, [part, part], [VMEM] * 9, [pltpu.VMEM(block, F32), plt...  1.12 us
    ppermute x1, waiting for transfers between devices, shards(): lax.ppermute(far, 'gx', [(i, (i + 1) % count if i % 2 else (i - 1) % coun...  0.71 us
    pallas_call x1, Pallas kernels, shards(): call(local_kernel, [block, state_shape, state_shape], [VMEM] * 7, [pltpu....  0.66 us
  transfers between devices with their start and end apart: 8, of which 5 were waited for; matrix products, arithmetic and copies ran while one was open for 0% of the time, Pallas kernels for 9%

profile of v7, /device:TPU:2, one launch (start us, length us, event | category | flops | bytes accessed | tf_op | source)
XLA Modules:
  0.0 30.1 jit_solution(17039691678427111051)
XLA Ops:
  0.6 1.7 %shard_map.113 = (f32[40,16,128]{2,1,0:T(8,128)S(1)}, f32[40,16,128]{2,1,0:T(8,128)S(1)}, bf16[40,16,128]{2,1,0:T(8,128)(2,1)S(1)}, bf16[40,16,128]{2,1,0:T(8,12...) custom-call(f32[40,16,128]{2,1,0:T(8,128)} %ws_hbm.1, ...), custom_call_target="tpu_custom_call" | custom-call | tf_op jit(solution)/shard_map/pallas_call | solution.py:556
  2.3 4.1 %collective-permute-start = (f32[8,640]{1,0:T(8,128)S(1)}, f32[8,640]{1,0:T(8,128)S(1)}, u32[]{:S(2)}, u32[]{:S(2)}) collective-permute-start(f32[8,640]{1,0:T(8,128)S(1)} %get-tuple-element.40), channel_id=1, source_target_pairs={{0,240},{16,32},{32,16},{48,64},{64,48},{80,96},{96,80},{112,128},... | collective-permute-start | bytes 61448 | tf_op jit(solution)/shard_map/ppermute | solution.py:571
  6.4 0.0 collective-permute-start.1
  6.5 2.1 %shard_map.114 = (f32[2,40,16,128]{3,2,1,0:T(8,128)S(1)}, f32[72,128]{1,0:T(8,128)S(1)}, f32[8,640]{1,0:T(8,128)S(1)}) custom-call(f32[40,16,128]{2,1,0:T(8,128)S(1)} %get-tuple-element.27.wn_ref, f32[40,16,128]{2,1,0:T(8,128)S(1)} %get-tuple-element.28.tn_ref, bf16[40,16,128]{2,1,0:T(8,128)(2,1)S(1)} %get-tuple-element.29.north_ref, ...), custom_call_target="tpu_custom_call" | custom-call | flops 16000000 | bytes 2000000 | tf_op jit(solution)/shard_map/pallas_call | solution.py:575
  8.5 0.7 %collective-permute-done.far_ref = f32[8,640]{1,0:T(8,128)S(1)} collective-permute-done((f32[8,640]{1,0:T(8,128)S(1)}, f32[8,640]{1,0:T(8,128)S(1)}, u32[]{:S(2)}, u32[]{:S(2)}) %collective-permute-start) | collective-permute-done | bytes 20512 | tf_op jit(solution)/shard_map/ppermute | solution.py:571
  9.3 0.0 collective-permute-done.1.near_ref
  9.3 0.3 %shard_map.115 = (f32[72,128]{1,0:T(8,128)S(1)}, f32[16,640]{1,0:T(8,128)S(1)}) custom-call(f32[8,640]{1,0:T(8,128)S(1)} %collective-permute-done.far_ref, f32[8,640]{1,0:T(8,128)S(1)} %collective-permute-done.1.near_ref, f32[48,640]{1,0:T(8,128)S(1)} %get-tuple-element.42.own_ref, f32[72,128]{1,0:T(8,128)S(1)} %get-tuple-element.43.sums_ref, ...), custom_call_target="tpu_custom_call" | custom-call | tf_op jit(solution)/shard_map/pallas_call | solution.py:591
  9.6 2.2 %collective-permute-start.4 = (f32[72,128]{1,0:T(8,128)S(1)}, f32[72,128]{1,0:T(8,128)S(1)}, u32[]{:S(2)}, u32[]{:S(2)}) collective-permute-start(f32[72,128]{1,0:T(8,128)S(1)} %get-tuple-element.46.own_ref.state_ref), channel_id=1, source_target_pairs={{0,3},{1,2},{2,1},{3,0},{4,7},{5,6},{6,5},{7,4},{8,11},{9,10},{10,... | collective-permute-start | bytes 110600 | tf_op jit(solution)/shard_map/ppermute | solution.py:596
  11.8 1.6 %collective-permute-start.3 = (f32[72,128]{1,0:T(8,128)S(1)}, f32[72,128]{1,0:T(8,128)S(1)}, u32[]{:S(2)}, u32[]{:S(2)}) collective-permute-start(f32[72,128]{1,0:T(8,128)S(1)} %get-tuple-element.46.own_ref.state_ref), channel_id=1, source_target_pairs={{0,2},{1,3},{2,0},{3,1},{4,6},{5,7},{6,4},{7,5},{8,10},{9,11},{10,... | collective-permute-start | bytes 110600 | tf_op jit(solution)/shard_map/ppermute | solution.py:596
  13.4 0.0 collective-permute-start.2
  13.4 1.1 %collective-permute-done.4.three_ref = f32[72,128]{1,0:T(8,128)S(1)} collective-permute-done((f32[72,128]{1,0:T(8,128)S(1)}, f32[72,128]{1,0:T(8,128)S(1)}, u32[]{:S(2)}, u32[]{:S(2)}) %collective-permute-start.4) | collective-permute-done | bytes 36896 | tf_op jit(solution)/shard_map/ppermute | solution.py:596
  14.5 1.2 %collective-permute-done.3.two_ref = f32[72,128]{1,0:T(8,128)S(1)} collective-permute-done((f32[72,128]{1,0:T(8,128)S(1)}, f32[72,128]{1,0:T(8,128)S(1)}, u32[]{:S(2)}, u32[]{:S(2)}) %collective-permute-start.3) | collective-permute-done | bytes 36896 | tf_op jit(solution)/shard_map/ppermute | solution.py:596
  15.8 1.6 %collective-permute-done.2.one_ref = f32[72,128]{1,0:T(8,128)S(1)} collective-permute-done((f32[72,128]{1,0:T(8,128)S(1)}, f32[72,128]{1,0:T(8,128)S(1)}, u32[]{:S(2)}, u32[]{:S(2)}) %collective-permute-start.2) | collective-permute-done | bytes 36896 | tf_op jit(solution)/shard_map/ppermute | solution.py:596
  17.4 0.2 shard_map.116
  17.6 5.3 %collective-permute-start.7 = (f32[72,128]{1,0:T(8,128)S(1)}, f32[72,128]{1,0:T(8,128)S(1)}, u32[]{:S(2)}, u32[]{:S(2)}) collective-permute-start(f32[72,128]{1,0:T(8,128)S(1)} %get-tuple-element.51), channel_id=1, source_target_pairs={{0,10},{1,11},{2,8},{3,9},{4,14},{5,15},{6,12},{7,13},{8,2},{9,3},... | collective-permute-start | bytes 110600 | tf_op jit(solution)/shard_map/ppermute | solution.py:596
  22.9 0.6 %collective-permute-start.6 = (f32[72,128]{1,0:T(8,128)S(1)}, f32[72,128]{1,0:T(8,128)S(1)}, u32[]{:S(2)}, u32[]{:S(2)}) collective-permute-start(f32[72,128]{1,0:T(8,128)S(1)} %get-tuple-element.51), channel_id=1, source_target_pairs={{0,12},{1,13},{2,14},{3,15},{4,8},{5,9},{6,10},{7,11},{8,4},{9,5},... | collective-permute-start | bytes 110600 | tf_op jit(solution)/shard_map/ppermute | solution.py:596
  23.4 0.9 %collective-permute-start.5 = (f32[72,128]{1,0:T(8,128)S(1)}, f32[72,128]{1,0:T(8,128)S(1)}, u32[]{:S(2)}, u32[]{:S(2)}) collective-permute-start(f32[72,128]{1,0:T(8,128)S(1)} %get-tuple-element.51), channel_id=1, source_target_pairs={{0,4},{1,5},{2,6},{3,7},{4,0},{5,1},{6,2},{7,3},{8,12},{9,13},{10,... | collective-permute-start | bytes 110600 | tf_op jit(solution)/shard_map/ppermute | solution.py:596
  24.4 0.7 %shard_map.117 = (f32[2,40,16,128]{3,2,1,0:T(8,128)S(1)}, f32[72,128]{1,0:T(8,128)S(1)}, f32[72,128]{1,0:T(8,128)S(1)}) custom-call(f32[2,40,16,128]{3,2,1,0:T(8,128)S(1)} %get-tuple-element.39.rhs_ref, f32[2,40,16,128]{3,2,1,0:T(8,128)S(1)} %get-tuple-element.34.up_ref, f32[2,40,16,128]{3,2,1,0:T(8,128)S(1)} %get-tuple-element.35.down_ref, ...), custom_call_target="tpu_custom_call" | custom-call | flops 4000000 | bytes 500000 | tf_op jit(solution)/shard_map/pallas_call | solution.py:600
  25.0 0.0 collective-permute-done.7.c_ref
  25.0 3.9 %collective-permute-done.6.b_ref = f32[72,128]{1,0:T(8,128)S(1)} collective-permute-done((f32[72,128]{1,0:T(8,128)S(1)}, f32[72,128]{1,0:T(8,128)S(1)}, u32[]{:S(2)}, u32[]{:S(2)}) %collective-permute-start.6) | collective-permute-done | bytes 36896 | tf_op jit(solution)/shard_map/ppermute | solution.py:596
  28.9 0.0 collective-permute-done.5.a_ref
  29.0 1.1 %shard_map.118 = (f32[40,16,128]{2,1,0:T(8,128)}, f32[40,16,128]{2,1,0:T(8,128)}) custom-call(f32[2,40,16,128]{3,2,1,0:T(8,128)S(1)} %get-tuple-element.48.y_ref, f32[2,40,16,128]{3,2,1,0:T(8,128)S(1)} %get-tuple-element.34.up_ref, f32[2,40,16,128]{3,2,1,0:T(8,128)S(1)} %get-tuple-element.35.down_ref, f32[72,128]{1,0:T(8,128)S(1)} %get-tuple-element.46.own_ref.state_ref, ...), custom_call_target="tpu_custom_call" | custom-call | tf_op jit(solution)/shard_map/pallas_call | solution.py:606
Async XLA Ops:
  2.3 6.9 %collective-permute-start = (f32[8,640]{1,0:T(8,128)S(1)}, f32[8,640]{1,0:T(8,128)S(1)}, u32[]{:S(2)}, u32[]{:S(2)}) collective-permute-start(f32[8,640]{1,0:T(8,128)S(1)} %get-tuple-element.40), channel_id=1, source_target_pairs={{0,240},{16,32},{32,16},{48,64},{64,48},{80,96},{96,80},{112,128},... | collective-permute-start | bytes 61448 | tf_op jit(solution)/shard_map/ppermute | solution.py:571
  6.4 2.8 %collective-permute-start.1 = (f32[8,640]{1,0:T(8,128)S(1)}, f32[8,640]{1,0:T(8,128)S(1)}, u32[]{:S(2)}, u32[]{:S(2)}) collective-permute-start(f32[8,640]{1,0:T(8,128)S(1)} %get-tuple-element.41), channel_id=1, source_target_pairs={{0,16},{16,0},{32,48},{48,32},{64,80},{80,64},{96,112},{112,96},{1... | collective-permute-start | bytes 61448 | tf_op jit(solution)/shard_map/ppermute | solution.py:574
  9.6 4.9 %collective-permute-start.4 = (f32[72,128]{1,0:T(8,128)S(1)}, f32[72,128]{1,0:T(8,128)S(1)}, u32[]{:S(2)}, u32[]{:S(2)}) collective-permute-start(f32[72,128]{1,0:T(8,128)S(1)} %get-tuple-element.46.own_ref.state_ref), channel_id=1, source_target_pairs={{0,3},{1,2},{2,1},{3,0},{4,7},{5,6},{6,5},{7,4},{8,11},{9,10},{10,... | collective-permute-start | bytes 110600 | tf_op jit(solution)/shard_map/ppermute | solution.py:596
  11.8 4.0 %collective-permute-start.3 = (f32[72,128]{1,0:T(8,128)S(1)}, f32[72,128]{1,0:T(8,128)S(1)}, u32[]{:S(2)}, u32[]{:S(2)}) collective-permute-start(f32[72,128]{1,0:T(8,128)S(1)} %get-tuple-element.46.own_ref.state_ref), channel_id=1, source_target_pairs={{0,2},{1,3},{2,0},{3,1},{4,6},{5,7},{6,4},{7,5},{8,10},{9,11},{10,... | collective-permute-start | bytes 110600 | tf_op jit(solution)/shard_map/ppermute | solution.py:596
  13.4 4.0 %collective-permute-start.2 = (f32[72,128]{1,0:T(8,128)S(1)}, f32[72,128]{1,0:T(8,128)S(1)}, u32[]{:S(2)}, u32[]{:S(2)}) collective-permute-start(f32[72,128]{1,0:T(8,128)S(1)} %get-tuple-element.46.own_ref.state_ref), channel_id=1, source_target_pairs={{0,1},{1,0},{2,3},{3,2},{4,5},{5,4},{6,7},{7,6},{8,9},{9,8},{10,11... | collective-permute-start | bytes 110600 | tf_op jit(solution)/shard_map/ppermute | solution.py:596
  17.6 7.4 %collective-permute-start.7 = (f32[72,128]{1,0:T(8,128)S(1)}, f32[72,128]{1,0:T(8,128)S(1)}, u32[]{:S(2)}, u32[]{:S(2)}) collective-permute-start(f32[72,128]{1,0:T(8,128)S(1)} %get-tuple-element.51), channel_id=1, source_target_pairs={{0,10},{1,11},{2,8},{3,9},{4,14},{5,15},{6,12},{7,13},{8,2},{9,3},... | collective-permute-start | bytes 110600 | tf_op jit(solution)/shard_map/ppermute | solution.py:596
  22.9 6.1 %collective-permute-start.6 = (f32[72,128]{1,0:T(8,128)S(1)}, f32[72,128]{1,0:T(8,128)S(1)}, u32[]{:S(2)}, u32[]{:S(2)}) collective-permute-start(f32[72,128]{1,0:T(8,128)S(1)} %get-tuple-element.51), channel_id=1, source_target_pairs={{0,12},{1,13},{2,14},{3,15},{4,8},{5,9},{6,10},{7,11},{8,4},{9,5},... | collective-permute-start | bytes 110600 | tf_op jit(solution)/shard_map/ppermute | solution.py:596
  23.4 5.5 %collective-permute-start.5 = (f32[72,128]{1,0:T(8,128)S(1)}, f32[72,128]{1,0:T(8,128)S(1)}, u32[]{:S(2)}, u32[]{:S(2)}) collective-permute-start(f32[72,128]{1,0:T(8,128)S(1)} %get-tuple-element.51), channel_id=1, source_target_pairs={{0,4},{1,5},{2,6},{3,7},{4,0},{5,1},{6,2},{7,3},{8,12},{9,13},{10,... | collective-permute-start | bytes 110600 | tf_op jit(solution)/shard_map/ppermute | solution.py:596

commit v8 on v6

--- a/solution.py
+++ b/solution.py
@@ -18,7 +18,7 @@
 PAD = 8
 FAR_GROUP = (5, 4, 7, 6, 1, 0, 3, 2)
 PARTS = 2
-UNROLL = 8
+UNROLL = 20
 HBM = pl.BlockSpec(memory_space=pltpu.HBM)
 VMEM = pl.BlockSpec(memory_space=pltpu.VMEM)
 SMEM = pl.BlockSpec(memory_space=pltpu.SMEM)
@@ -409,7 +409,7 @@
 
 
 def local_kernel(
-    rhs_ref, up_ref, down_ref, faces_ref, state_ref, one_ref, pair_ref, y_ref, above_ref, below_ref, b_ref
+    rhs_ref, up_ref, down_ref, faces_ref, state_ref, one_ref, pair_ref, y_ref, above_ref, below_ref, own_ref, b_ref
 ):
     aboves, belows = [], []
     for f in range(2):
@@ -423,8 +423,11 @@
         belows.append(tuple(
             jnp.where(near, jnp.where(outer, z, x), y) for x, y, z in zip(one, pair, both)
         ))
-    store(above_ref, aboves)
-    store(below_ref, belows)
+    owns = [unpack(state_ref[...], f) for f in range(2)]
+    for ref, blocks in ((above_ref, aboves), (below_ref, belows), (own_ref, owns)):
+        for f in range(2):
+            for i in range(6):
+                ref[f, i] = blocks[f][i]
     zero = jnp.zeros((ROWS, LANES), F32)
     coef = state_ref[4 * ROWS:]
     for f in range(2):
@@ -475,19 +478,20 @@
     y_ref, up_ref, down_ref, own_ref, above_ref, below_ref, a_ref, b_ref, c_ref, w_hbm, t_hbm, out_ref, sem
 ):
     zero = jnp.zeros((ROWS, LANES), F32)
-    own = own_ref[...]
     group = lax.div(lax.axis_index("gz"), 4)
     place = lax.rem(lax.axis_index("gz"), 4)
-    others = (a_ref[...], c_ref[...], b_ref[...])
-    groups = []
+    slots = []
     for j in range(4):
         slot = lax.rem(group, 2) * (1 - 2 * (j % 2)) + j % 2
-        slot = slot + 2 * (lax.div(group, 2) * (1 - 2 * (j // 2)) + j // 2)
-        groups.append(jnp.where(slot == 1, others[0], jnp.where(slot == 2, others[1], others[2])))
+        slots.append(slot + 2 * (lax.div(group, 2) * (1 - 2 * (j // 2)) + j // 2))
     flows = []
     for f in range(2):
-        blocks = [unpack(g, f) for g in groups]
-        inner_above, inner_below = unpack(above_ref[...], f), unpack(below_ref[...], f)
+        others = [unpack(ref[...], f) for ref in (a_ref, c_ref, b_ref)]
+        blocks = [
+            tuple(jnp.where(slot == 1, x, jnp.where(slot == 2, y, z)) for x, y, z in zip(*others))
+            for slot in slots
+        ]
+        inner_above, inner_below = (tuple(ref[f, i] for i in range(6)) for ref in (above_ref, below_ref))
         upper, lower = (zero, zero, zero), (zero, zero)
         for j in (3, 2, 1):
             upper = above(upper, blocks[j], j > group)
@@ -497,7 +501,7 @@
         lower = below(lower, inner_below, place > 0)
         yf_above, z_above, a_above = upper
         yl_below, z_below = lower
-        yf, yl, z11, z12, z22, a = unpack(own, f)
+        yf, yl, z11, z12, z22, a = (own_ref[f, i] for i in range(6))
         p = 1.0 + a * (z_below + z11)
         q = 1.0 + a_above * (z_above + z22)
         s_below = a * (yl_below - yf)
@@ -597,8 +601,9 @@
 
     three, two, one = (swap(state, lambda i, k=k: i ^ k) for k in (3, 2, 1))
     pair, four = call(four_kernel, [state_shape] * 2, [VMEM] * 4)(state, one, two, three)
-    y, inner_above, inner_below = call(
-        local_kernel, [block, state_shape, state_shape], [VMEM] * 7, [pltpu.VMEM(block, F32)], flops=4_000_000
+    spread = (2, 6, ROWS, LANES)
+    y, inner_above, inner_below, own_spread = call(
+        local_kernel, [block, spread, spread, spread], [VMEM] * 7, [pltpu.VMEM(block, F32)], flops=4_000_000
     )(rhs, up, down, faces, state, one, pair)
     side_a = swap(four, lambda i: i ^ 4)
     side_b = swap(four, lambda i: (i + 4 if i & 4 else i - 4) % count)
@@ -609,7 +614,7 @@
         [VMEM] * 9,
         [pltpu.VMEM(block, F32), pltpu.SemaphoreType.DMA((2 * PARTS,))],
         [HBM] * 2,
-    )(y, up, down, state, inner_above, inner_below, side_a, side_b, side_c))
+    )(y, up, down, own_spread, inner_above, inner_below, side_a, side_b, side_c))
 
 
 def solution(mesh):

time: 30.6 us -> 30.6 us (level)
  no operation moved by 1% of the time
where the time goes in v8:
time: 30.6 us; the launch traced here: 30.1 us
  starting transfers between devices  14.7 us (48%)
  waiting for transfers between devices  8.54 us (28%)
  Pallas kernels  6.15 us (20%)
  between operations  0.69 us (2%)
    ppermute x6, starting transfers between devices, swap(): return lax.ppermute(x, 'gz', [(i, partner(i)) for i in range(count)])  10.6 us
    ppermute x6, waiting for transfers between devices, swap(): return lax.ppermute(x, 'gz', [(i, partner(i)) for i in range(count)])  7.84 us
    ppermute x1, starting transfers between devices, shards(): lax.ppermute(far, 'gx', [(i, (i + 1) % count if i % 2 else (i - 1) % coun...  4.1 us
    pallas_call x1, Pallas kernels, shards(): call(main_kernel, [block, state_shape, strip], [VMEM] * 13, [pltpu.VMEM(p...  2.09 us
    pallas_call x1, Pallas kernels, shards(): call(pack_kernel, [wide, wide, half, half, wide, wide, half, split, strip...  1.71 us
    pallas_call x1, Pallas kernels, shards(): call(final_kernel, [part, part], [VMEM] * 9, [pltpu.VMEM(block, F32), plt...  1.12 us
    ppermute x1, waiting for transfers between devices, shards(): lax.ppermute(far, 'gx', [(i, (i + 1) % count if i % 2 else (i - 1) % coun...  0.7 us
    pallas_call x1, Pallas kernels, shards(): call(local_kernel, [block, spread, spread, spread], [VMEM] * 7, [pltpu.VM...  0.7 us
  transfers between devices with their start and end apart: 8, of which 5 were waited for; matrix products, arithmetic and copies ran while one was open for 0% of the time, Pallas kernels for 9%

profile of v8, /device:TPU:2, one launch (start us, length us, event | category | flops | bytes accessed | tf_op | source)
XLA Modules:
  0.0 30.1 jit_solution(9890241106274698348)
XLA Ops:
  0.6 1.7 %shard_map.113 = (f32[40,16,128]{2,1,0:T(8,128)S(1)}, f32[40,16,128]{2,1,0:T(8,128)S(1)}, bf16[40,16,128]{2,1,0:T(8,128)(2,1)S(1)}, bf16[40,16,128]{2,1,0:T(8,12...) custom-call(f32[40,16,128]{2,1,0:T(8,128)} %ws_hbm.1, ...), custom_call_target="tpu_custom_call" | custom-call | tf_op jit(solution)/shard_map/pallas_call | solution.py:560
  2.4 4.1 %collective-permute-start = (f32[8,640]{1,0:T(8,128)S(1)}, f32[8,640]{1,0:T(8,128)S(1)}, u32[]{:S(2)}, u32[]{:S(2)}) collective-permute-start(f32[8,640]{1,0:T(8,128)S(1)} %get-tuple-element.43), channel_id=1, source_target_pairs={{0,240},{16,32},{32,16},{48,64},{64,48},{80,96},{96,80},{112,128},... | collective-permute-start | bytes 61448 | tf_op jit(solution)/shard_map/ppermute | solution.py:575
  6.5 0.0 collective-permute-start.1
  6.5 2.1 %shard_map.114 = (f32[2,40,16,128]{3,2,1,0:T(8,128)S(1)}, f32[72,128]{1,0:T(8,128)S(1)}, f32[8,640]{1,0:T(8,128)S(1)}) custom-call(f32[40,16,128]{2,1,0:T(8,128)S(1)} %get-tuple-element.29.wn_ref, f32[40,16,128]{2,1,0:T(8,128)S(1)} %get-tuple-element.30.tn_ref, bf16[40,16,128]{2,1,0:T(8,128)(2,1)S(1)} %get-tuple-element.31.north_ref, ...), custom_call_target="tpu_custom_call" | custom-call | flops 16000000 | bytes 2000000 | tf_op jit(solution)/shard_map/pallas_call | solution.py:579
  8.6 0.7 %collective-permute-done.far_ref = f32[8,640]{1,0:T(8,128)S(1)} collective-permute-done((f32[8,640]{1,0:T(8,128)S(1)}, f32[8,640]{1,0:T(8,128)S(1)}, u32[]{:S(2)}, u32[]{:S(2)}) %collective-permute-start) | collective-permute-done | bytes 20512 | tf_op jit(solution)/shard_map/ppermute | solution.py:575
  9.3 0.0 collective-permute-done.1.near_ref
  9.3 0.3 %shard_map.115 = (f32[72,128]{1,0:T(8,128)S(1)}, f32[16,640]{1,0:T(8,128)S(1)}) custom-call(f32[8,640]{1,0:T(8,128)S(1)} %collective-permute-done.far_ref, f32[8,640]{1,0:T(8,128)S(1)} %collective-permute-done.1.near_ref, f32[48,640]{1,0:T(8,128)S(1)} %get-tuple-element.45.own_ref, f32[72,128]{1,0:T(8,128)S(1)} %get-tuple-element.46.sums_ref, ...), custom_call_target="tpu_custom_call" | custom-call | tf_op jit(solution)/shard_map/pallas_call | solution.py:595
  9.6 2.2 %collective-permute-start.4 = (f32[72,128]{1,0:T(8,128)S(1)}, f32[72,128]{1,0:T(8,128)S(1)}, u32[]{:S(2)}, u32[]{:S(2)}) collective-permute-start(f32[72,128]{1,0:T(8,128)S(1)} %get-tuple-element.49.own_ref.state_ref), channel_id=1, source_target_pairs={{0,3},{1,2},{2,1},{3,0},{4,7},{5,6},{6,5},{7,4},{8,11},{9,10},{10,... | collective-permute-start | bytes 110600 | tf_op jit(solution)/shard_map/ppermute | solution.py:600
  11.8 1.6 %collective-permute-start.3 = (f32[72,128]{1,0:T(8,128)S(1)}, f32[72,128]{1,0:T(8,128)S(1)}, u32[]{:S(2)}, u32[]{:S(2)}) collective-permute-start(f32[72,128]{1,0:T(8,128)S(1)} %get-tuple-element.49.own_ref.state_ref), channel_id=1, source_target_pairs={{0,2},{1,3},{2,0},{3,1},{4,6},{5,7},{6,4},{7,5},{8,10},{9,11},{10,... | collective-permute-start | bytes 110600 | tf_op jit(solution)/shard_map/ppermute | solution.py:600
  13.4 0.0 collective-permute-start.2
  13.4 1.1 %collective-permute-done.4.three_ref = f32[72,128]{1,0:T(8,128)S(1)} collective-permute-done((f32[72,128]{1,0:T(8,128)S(1)}, f32[72,128]{1,0:T(8,128)S(1)}, u32[]{:S(2)}, u32[]{:S(2)}) %collective-permute-start.4) | collective-permute-done | bytes 36896 | tf_op jit(solution)/shard_map/ppermute | solution.py:600
  14.6 1.2 %collective-permute-done.3.two_ref = f32[72,128]{1,0:T(8,128)S(1)} collective-permute-done((f32[72,128]{1,0:T(8,128)S(1)}, f32[72,128]{1,0:T(8,128)S(1)}, u32[]{:S(2)}, u32[]{:S(2)}) %collective-permute-start.3) | collective-permute-done | bytes 36896 | tf_op jit(solution)/shard_map/ppermute | solution.py:600
  15.8 1.6 %collective-permute-done.2.one_ref = f32[72,128]{1,0:T(8,128)S(1)} collective-permute-done((f32[72,128]{1,0:T(8,128)S(1)}, f32[72,128]{1,0:T(8,128)S(1)}, u32[]{:S(2)}, u32[]{:S(2)}) %collective-permute-start.2) | collective-permute-done | bytes 36896 | tf_op jit(solution)/shard_map/ppermute | solution.py:600
  17.4 0.2 shard_map.116
  17.6 5.3 %collective-permute-start.7 = (f32[72,128]{1,0:T(8,128)S(1)}, f32[72,128]{1,0:T(8,128)S(1)}, u32[]{:S(2)}, u32[]{:S(2)}) collective-permute-start(f32[72,128]{1,0:T(8,128)S(1)} %get-tuple-element.55), channel_id=1, source_target_pairs={{0,10},{1,11},{2,8},{3,9},{4,14},{5,15},{6,12},{7,13},{8,2},{9,3},... | collective-permute-start | bytes 110600 | tf_op jit(solution)/shard_map/ppermute | solution.py:600
  22.9 0.6 %collective-permute-start.6 = (f32[72,128]{1,0:T(8,128)S(1)}, f32[72,128]{1,0:T(8,128)S(1)}, u32[]{:S(2)}, u32[]{:S(2)}) collective-permute-start(f32[72,128]{1,0:T(8,128)S(1)} %get-tuple-element.55), channel_id=1, source_target_pairs={{0,12},{1,13},{2,14},{3,15},{4,8},{5,9},{6,10},{7,11},{8,4},{9,5},... | collective-permute-start | bytes 110600 | tf_op jit(solution)/shard_map/ppermute | solution.py:600
  23.4 0.9 %collective-permute-start.5 = (f32[72,128]{1,0:T(8,128)S(1)}, f32[72,128]{1,0:T(8,128)S(1)}, u32[]{:S(2)}, u32[]{:S(2)}) collective-permute-start(f32[72,128]{1,0:T(8,128)S(1)} %get-tuple-element.55), channel_id=1, source_target_pairs={{0,4},{1,5},{2,6},{3,7},{4,0},{5,1},{6,2},{7,3},{8,12},{9,13},{10,... | collective-permute-start | bytes 110600 | tf_op jit(solution)/shard_map/ppermute | solution.py:600
  24.4 0.7 %shard_map.117 = (f32[2,40,16,128]{3,2,1,0:T(8,128)S(1)}, f32[2,6,16,128]{3,2,1,0:T(8,128)S(1)}, f32[2,6,16,128]{3,2,1,0:T(8,128)S(1)}, f32[2,6,16,128]{3,2,1,0:T(8,128)S(1)}) custom-call(f32[2,40,16,128]{3,2,1,0:T(8,128)S(1)} %get-tuple-element.42.rhs_ref, f32[2,40,16,128]{3,2,1,0:T(8,128)S(1)} %get-tuple-element.37.up_ref, ...), custom_call_target="tpu_custom_call" | custom-call | flops 4000000 | bytes 500000 | tf_op jit(solution)/shard_map/pallas_call | solution.py:605
  25.1 0.0 collective-permute-done.7.c_ref
  25.1 3.9 %collective-permute-done.6.b_ref = f32[72,128]{1,0:T(8,128)S(1)} collective-permute-done((f32[72,128]{1,0:T(8,128)S(1)}, f32[72,128]{1,0:T(8,128)S(1)}, u32[]{:S(2)}, u32[]{:S(2)}) %collective-permute-start.6) | collective-permute-done | bytes 36896 | tf_op jit(solution)/shard_map/ppermute | solution.py:600
  29.0 0.0 collective-permute-done.5.a_ref
  29.0 1.1 %shard_map.118 = (f32[40,16,128]{2,1,0:T(8,128)}, f32[40,16,128]{2,1,0:T(8,128)}) custom-call(f32[2,40,16,128]{3,2,1,0:T(8,128)S(1)} %get-tuple-element.51.y_ref, f32[2,40,16,128]{3,2,1,0:T(8,128)S(1)} %get-tuple-element.37.up_ref, f32[2,40,16,128]{3,2,1,0:T(8,128)S(1)} %get-tuple-element.38.down_ref, f32[2,6,16,128]{3,2,1,0:T(8,128)S(1)} %get-tuple-element.52.own_ref, ...), custom_call_target="tpu_custom_call" | custom-call | tf_op jit(solution)/shard_map/pallas_call | solution.py:611
Async XLA Ops:
  2.4 6.9 %collective-permute-start = (f32[8,640]{1,0:T(8,128)S(1)}, f32[8,640]{1,0:T(8,128)S(1)}, u32[]{:S(2)}, u32[]{:S(2)}) collective-permute-start(f32[8,640]{1,0:T(8,128)S(1)} %get-tuple-element.43), channel_id=1, source_target_pairs={{0,240},{16,32},{32,16},{48,64},{64,48},{80,96},{96,80},{112,128},... | collective-permute-start | bytes 61448 | tf_op jit(solution)/shard_map/ppermute | solution.py:575
  6.5 2.8 %collective-permute-start.1 = (f32[8,640]{1,0:T(8,128)S(1)}, f32[8,640]{1,0:T(8,128)S(1)}, u32[]{:S(2)}, u32[]{:S(2)}) collective-permute-start(f32[8,640]{1,0:T(8,128)S(1)} %get-tuple-element.44), channel_id=1, source_target_pairs={{0,16},{16,0},{32,48},{48,32},{64,80},{80,64},{96,112},{112,96},{1... | collective-permute-start | bytes 61448 | tf_op jit(solution)/shard_map/ppermute | solution.py:578
  9.6 4.9 %collective-permute-start.4 = (f32[72,128]{1,0:T(8,128)S(1)}, f32[72,128]{1,0:T(8,128)S(1)}, u32[]{:S(2)}, u32[]{:S(2)}) collective-permute-start(f32[72,128]{1,0:T(8,128)S(1)} %get-tuple-element.49.own_ref.state_ref), channel_id=1, source_target_pairs={{0,3},{1,2},{2,1},{3,0},{4,7},{5,6},{6,5},{7,4},{8,11},{9,10},{10,... | collective-permute-start | bytes 110600 | tf_op jit(solution)/shard_map/ppermute | solution.py:600
  11.8 4.0 %collective-permute-start.3 = (f32[72,128]{1,0:T(8,128)S(1)}, f32[72,128]{1,0:T(8,128)S(1)}, u32[]{:S(2)}, u32[]{:S(2)}) collective-permute-start(f32[72,128]{1,0:T(8,128)S(1)} %get-tuple-element.49.own_ref.state_ref), channel_id=1, source_target_pairs={{0,2},{1,3},{2,0},{3,1},{4,6},{5,7},{6,4},{7,5},{8,10},{9,11},{10,... | collective-permute-start | bytes 110600 | tf_op jit(solution)/shard_map/ppermute | solution.py:600
  13.4 4.0 %collective-permute-start.2 = (f32[72,128]{1,0:T(8,128)S(1)}, f32[72,128]{1,0:T(8,128)S(1)}, u32[]{:S(2)}, u32[]{:S(2)}) collective-permute-start(f32[72,128]{1,0:T(8,128)S(1)} %get-tuple-element.49.own_ref.state_ref), channel_id=1, source_target_pairs={{0,1},{1,0},{2,3},{3,2},{4,5},{5,4},{6,7},{7,6},{8,9},{9,8},{10,11... | collective-permute-start | bytes 110600 | tf_op jit(solution)/shard_map/ppermute | solution.py:600
  17.6 7.5 %collective-permute-start.7 = (f32[72,128]{1,0:T(8,128)S(1)}, f32[72,128]{1,0:T(8,128)S(1)}, u32[]{:S(2)}, u32[]{:S(2)}) collective-permute-start(f32[72,128]{1,0:T(8,128)S(1)} %get-tuple-element.55), channel_id=1, source_target_pairs={{0,10},{1,11},{2,8},{3,9},{4,14},{5,15},{6,12},{7,13},{8,2},{9,3},... | collective-permute-start | bytes 110600 | tf_op jit(solution)/shard_map/ppermute | solution.py:600
  22.9 6.1 %collective-permute-start.6 = (f32[72,128]{1,0:T(8,128)S(1)}, f32[72,128]{1,0:T(8,128)S(1)}, u32[]{:S(2)}, u32[]{:S(2)}) collective-permute-start(f32[72,128]{1,0:T(8,128)S(1)} %get-tuple-element.55), channel_id=1, source_target_pairs={{0,12},{1,13},{2,14},{3,15},{4,8},{5,9},{6,10},{7,11},{8,4},{9,5},... | collective-permute-start | bytes 110600 | tf_op jit(solution)/shard_map/ppermute | solution.py:600
  23.4 5.5 %collective-permute-start.5 = (f32[72,128]{1,0:T(8,128)S(1)}, f32[72,128]{1,0:T(8,128)S(1)}, u32[]{:S(2)}, u32[]{:S(2)}) collective-permute-start(f32[72,128]{1,0:T(8,128)S(1)} %get-tuple-element.55), channel_id=1, source_target_pairs={{0,4},{1,5},{2,6},{3,7},{4,0},{5,1},{6,2},{7,3},{8,12},{9,13},{10,... | collective-permute-start | bytes 110600 | tf_op jit(solution)/shard_map/ppermute | solution.py:600
